TPU v7x, 32 devices: a whole 2x2x4 slice. The times are simulated.
32 devices in a mesh: dp: 4 (over z), wide: 2 (over y), narrow: 4 (over x, core).
Axes of the slice: x: 2, y: 2, z: 4, core: 2. Of those that a mesh axis runs over, the one named last changes fastest.
Arguments:
- inputs: bfloat16 [16384, 1024], P(('dp', 'wide', 'narrow')), may hold values from -6 to 6
- segments: int32 [16384], P(('dp', 'wide', 'narrow')), may hold values from -1 to 7, as said below
- first_gain: float32 [1024], replicated, may hold values from 0.25 to 1.75
- first_shift: float32 [1024], replicated, may hold values from -1.75 to 1.75
- qkv_weight: bfloat16 [1024, 3, 1024], P('narrow', None, 'wide'), may hold values from -0.1875 to 0.1875
- qv_bias: bfloat16 [2, 1024], P(None, 'wide'), may hold values from -3 to 3
- out_weight: bfloat16 [1024, 1024], P('wide', 'narrow'), may hold values from -0.75 to 0.75
- out_bias: bfloat16 [1024], replicated, may hold values from -3 to 3
- second_gain: float32 [1024], replicated, may hold values from 0.25 to 1.75
- second_shift: float32 [1024], replicated, may hold values from -1.75 to 1.75
- up_weight: bfloat16 [1024, 4096], P('narrow', 'wide'), may hold values from -0.1875 to 0.1875
- up_bias: bfloat16 [4096], P('wide'), may hold values from -3 to 3
- down_weight: bfloat16 [4096, 1024], P('wide', 'narrow'), may hold values from -0.09375 to 0.09375
- down_bias: bfloat16 [1024], replicated, may hold values from -3 to 3
- cotangent: bfloat16 [16384, 1024], P(('dp', 'wide', 'narrow')), may hold values from -6 to 6
Outputs:
- output: bfloat16 [16384, 1024], P(('dp', 'wide', 'narrow'))
- input_grad: bfloat16 [16384, 1024], P(('dp', 'wide', 'narrow'))
- first_gain_grad: float32 [1024], replicated
- first_shift_grad: float32 [1024], replicated
- qkv_grad: float32 [1024, 3, 1024], P('narrow', None, 'wide')
- qv_bias_grad: float32 [2, 1024], P(None, ('wide', 'narrow'))
- out_grad: float32 [1024, 1024], P('wide', 'narrow')
- out_bias_grad: float32 [1024], replicated
- second_gain_grad: float32 [1024], replicated
- second_shift_grad: float32 [1024], replicated
- up_grad: float32 [1024, 4096], P('narrow', 'wide')
- up_bias_grad: float32 [4096], P(('wide', 'narrow'))
- down_grad: float32 [4096, 1024], P('wide', 'narrow')
- down_bias_grad: float32 [1024], replicated
Inputs may be any that keep to these rules, and one draw needn't show every extreme that they name: `segments`: each aligned run of 512 rows is one sequence: its rows carry segment numbers 0 to 7 in order, every one of them present on at least one row, followed in some sequences by padding rows numbered -1.
All inputs are finite; a program needn't handle non-finite values.
Results may differ from a plain program's by a relative error of at most 0.02.
Values may be sent and summed in bfloat16 or wider, within the bound.
No kernel may reach another device: no remote copies, remote signals or barrier semaphores. Data moves between devices by JAX's collectives and lax.ppermute only.
A program may use at most 128 MiB of HBM per device.

v0:
```python
from functools import partial

import jax
import jax.numpy as jnp
from jax import lax
from jax.sharding import PartitionSpec as P

HD = 64
LEN = 512


EPSILON = 1e-06
MASKED = -1e30
SQRT_HALF = 0.7071067811865476


def norm_parts(values):
    average = jnp.mean(values, axis=-1, keepdims=True)
    centred = values - average
    variance = jnp.mean(centred * centred, axis=-1, keepdims=True)
    scaled = lax.rsqrt(variance + EPSILON)
    return (centred * scaled, scaled)


def norm_back(upstream, gain, normal, scaled):
    inner = upstream * gain
    first_term = jnp.mean(inner, axis=-1, keepdims=True)
    second_term = jnp.mean(inner * normal, axis=-1, keepdims=True)
    return scaled * (inner - first_term - normal * second_term)


def gaussian_unit(values):
    return 0.5 * values * (1.0 + lax.erf(values * SQRT_HALF))


def masked_scores(packed, labels, factor):
    query_rows = packed[:, 0]
    key_rows = packed[:, 1]
    scores = (
        jnp.einsum("qhe,khe->hqk", query_rows, key_rows, preferred_element_type=jnp.float32)
        * factor
    )
    allowed = labels[:, None] == labels[None, :]
    return jnp.where(allowed[None], scores, MASKED)


def attend_forward(operands, factor):
    packed, labels = operands
    scores = masked_scores(packed, labels, factor)
    highest = jnp.max(scores, axis=-1, keepdims=True)
    weights = jnp.exp(scores - highest)
    totals = jnp.sum(weights, axis=-1, keepdims=True)
    softmax_out = (weights / totals).astype(jnp.bfloat16)
    attended = jnp.einsum(
        "hqk,khe->qhe", softmax_out, packed[:, 2], preferred_element_type=jnp.float32
    )
    return (attended.astype(jnp.bfloat16), (highest + jnp.log(totals))[..., 0])


def attend_back(operands, factor):
    packed, labels, logsum, grad_rows = operands
    query_rows = packed[:, 0]
    key_rows = packed[:, 1]
    value_rows = packed[:, 2]
    scores = masked_scores(packed, labels, factor)
    softmax_out = jnp.exp(scores - logsum[..., None])
    grad_probs = jnp.einsum(
        "qhe,khe->hqk", grad_rows, value_rows, preferred_element_type=jnp.float32
    )
    delta_rows = jnp.sum(softmax_out * grad_probs, axis=-1, keepdims=True)
    grad_scores = (softmax_out * (grad_probs - delta_rows)).astype(jnp.bfloat16)
    grad_values = jnp.einsum(
        "hqk,qhe->khe",
        softmax_out.astype(jnp.bfloat16),
        grad_rows,
        preferred_element_type=jnp.float32,
    )
    grad_queries = (
        jnp.einsum("hqk,khe->qhe", grad_scores, key_rows, preferred_element_type=jnp.float32)
        * factor
    )
    grad_keys = (
        jnp.einsum("hqk,qhe->khe", grad_scores, query_rows, preferred_element_type=jnp.float32)
        * factor
    )
    return jnp.stack([grad_queries, grad_keys, grad_values], axis=1).astype(jnp.bfloat16)


def narrow_share(values, axis_dim, place, narrow_count):
    share = values.shape[axis_dim] // narrow_count
    return lax.dynamic_slice_in_dim(values, place * share, share, axis_dim)


def shards(
    inputs,
    segments,
    first_gain,
    first_shift,
    qkv_weight,
    qv_bias,
    out_weight,
    out_bias,
    second_gain,
    second_shift,
    up_weight,
    up_bias,
    down_weight,
    down_bias,
    cotangent,
):
    groups = lax.axis_size("wide")
    member = lax.axis_index("wide")
    narrow_count = lax.axis_size("narrow")
    narrow_place = lax.axis_index("narrow")
    own_rows = inputs.shape[0]
    model_width = inputs.shape[1]
    part_width = qkv_weight.shape[2]
    heads_local = part_width // HD
    factor = HD ** (-0.5)
    all_rows = groups * own_rows
    sequences = all_rows // LEN
    own_start = member * own_rows
    qkv_full, out_full, up_full, down_full = (
        lax.all_gather(qkv_weight, "narrow", axis=0, tiled=True),
        lax.all_gather(out_weight, "narrow", axis=1, tiled=True),
        lax.all_gather(up_weight, "narrow", axis=0, tiled=True),
        lax.all_gather(down_weight, "narrow", axis=1, tiled=True),
    )
    qkv_flat = qkv_full.reshape(model_width, 3 * part_width)
    all_inputs, all_labels = (
        lax.all_gather(inputs, "wide", axis=0, tiled=True),
        lax.all_gather(segments, "wide", axis=0, tiled=True),
    )
    keep_all = (all_labels >= 0)[:, None]
    keep_own = (segments >= 0)[:, None]
    normal_one, scaled_one = norm_parts(all_inputs.astype(jnp.float32))
    normed_one = (normal_one * first_gain + first_shift).astype(jnp.bfloat16)
    bias_rows = jnp.stack([qv_bias[0], jnp.zeros_like(qv_bias[0]), qv_bias[1]]).astype(jnp.float32)
    projected = (
        jnp.dot(normed_one, qkv_flat, preferred_element_type=jnp.float32).reshape(
            all_rows, 3, part_width
        )
        + bias_rows
    )
    packed = projected.astype(jnp.bfloat16).reshape(sequences, LEN, 3, heads_local, HD)
    labels = all_labels.reshape(sequences, LEN)
    attended, logsum = lax.map(partial(attend_forward, factor=factor), (packed, labels))
    attended_low = attended.reshape(all_rows, part_width)
    row_piece = attended_low
    attn_own = lax.psum_scatter(
        jnp.dot(row_piece, out_full, preferred_element_type=jnp.float32).astype(jnp.bfloat16),
        "wide",
        scatter_dimension=0,
        tiled=True,
    ).astype(jnp.float32)
    middle_own = inputs.astype(jnp.float32) + attn_own + out_bias.astype(jnp.float32)
    normal_two, scaled_two = norm_parts(middle_own)
    normed_two = (normal_two * second_gain + second_shift).astype(jnp.bfloat16)
    normed_two_all = lax.all_gather(normed_two, "wide", axis=0, tiled=True)
    before = jnp.dot(normed_two_all, up_full, preferred_element_type=jnp.float32) + up_bias.astype(
        jnp.float32
    )
    hidden = gaussian_unit(before).astype(jnp.bfloat16)
    row_piece = hidden
    mlp_own = lax.psum_scatter(
        jnp.dot(row_piece, down_full, preferred_element_type=jnp.float32).astype(jnp.bfloat16),
        "wide",
        scatter_dimension=0,
        tiled=True,
    ).astype(jnp.float32)
    output = jnp.where(keep_own, middle_own + mlp_own + down_bias.astype(jnp.float32), 0.0).astype(
        jnp.bfloat16
    )
    grad_out_own = jnp.where(keep_own, cotangent.astype(jnp.float32), 0.0)
    all_cot = lax.all_gather(cotangent, "wide", axis=0, tiled=True)
    grad_low_all = jnp.where(keep_all, all_cot, jnp.zeros_like(all_cot))
    down_part = jnp.einsum("tf,td->fd", hidden, grad_low_all, preferred_element_type=jnp.float32)
    grad_hidden = jnp.einsum(
        "td,fd->tf", grad_low_all, down_full, preferred_element_type=jnp.float32
    )
    gelu_value, gelu_pull = jax.vjp(gaussian_unit, before)
    grad_before = gelu_pull(grad_hidden)[0].astype(jnp.bfloat16)
    up_part = jnp.einsum(
        "td,tf->df", normed_two_all, grad_before, preferred_element_type=jnp.float32
    )
    up_bias_part = jnp.sum(grad_before, axis=0, dtype=jnp.float32)
    row_piece = grad_before
    grad_normed_own = lax.psum_scatter(
        jnp.einsum("tf,df->td", row_piece, up_full, preferred_element_type=jnp.float32).astype(
            jnp.bfloat16
        ),
        "wide",
        scatter_dimension=0,
        tiled=True,
    ).astype(jnp.float32)
    grad_middle_own = grad_out_own + norm_back(grad_normed_own, second_gain, normal_two, scaled_two)
    grad_middle_low = lax.all_gather(
        grad_middle_own.astype(jnp.bfloat16), "wide", axis=0, tiled=True
    )
    second_gain_part = jnp.sum(grad_normed_own * normal_two, axis=0)
    second_shift_part = jnp.sum(grad_normed_own, axis=0)
    out_bias_part = jnp.sum(grad_middle_own, axis=0)
    down_bias_part = jnp.sum(grad_out_own, axis=0)
    out_part = jnp.einsum(
        "tc,td->cd", attended_low, grad_middle_low, preferred_element_type=jnp.float32
    )
    grad_attended = jnp.einsum(
        "td,cd->tc", grad_middle_low, out_full, preferred_element_type=jnp.float32
    ).astype(jnp.bfloat16)
    grad_packed = lax.map(
        partial(attend_back, factor=factor),
        (packed, labels, logsum, grad_attended.reshape(sequences, LEN, heads_local, HD)),
    )
    grad_qkv = grad_packed.reshape(all_rows, 3 * part_width)
    qkv_part = jnp.einsum(
        "td,tc->dc", normed_one, grad_qkv, preferred_element_type=jnp.float32
    ).reshape(model_width, 3, part_width)
    grad_sums = jnp.sum(grad_qkv.reshape(all_rows, 3, part_width), axis=0, dtype=jnp.float32)
    qv_part = jnp.stack([grad_sums[0], grad_sums[2]])
    row_piece = grad_qkv
    grad_first_own = lax.psum_scatter(
        jnp.einsum("tc,dc->td", row_piece, qkv_flat, preferred_element_type=jnp.float32).astype(
            jnp.bfloat16
        ),
        "wide",
        scatter_dimension=0,
        tiled=True,
    ).astype(jnp.float32)
    normal_one_own = lax.dynamic_slice_in_dim(normal_one, own_start, own_rows, 0)
    scaled_one_own = lax.dynamic_slice_in_dim(scaled_one, own_start, own_rows, 0)
    input_grad = (
        grad_middle_own + norm_back(grad_first_own, first_gain, normal_one_own, scaled_one_own)
    ).astype(jnp.bfloat16)
    first_gain_part = jnp.sum(grad_first_own * normal_one_own, axis=0)
    first_shift_part = jnp.sum(grad_first_own, axis=0)
    summed = (
        lax.psum(qkv_part.astype(jnp.bfloat16), ("dp", "narrow")).astype(jnp.float32),
        lax.psum(qv_part.astype(jnp.bfloat16), ("dp", "narrow")).astype(jnp.float32),
        lax.psum(out_part.astype(jnp.bfloat16), ("dp", "narrow")).astype(jnp.float32),
        lax.psum(up_part.astype(jnp.bfloat16), ("dp", "narrow")).astype(jnp.float32),
        lax.psum(up_bias_part.astype(jnp.bfloat16), ("dp", "narrow")).astype(jnp.float32),
        lax.psum(down_part.astype(jnp.bfloat16), ("dp", "narrow")).astype(jnp.float32),
    )
    totals = (
        narrow_share(summed[0], 0, narrow_place, narrow_count),
        narrow_share(summed[1], 1, narrow_place, narrow_count),
        narrow_share(summed[2], 1, narrow_place, narrow_count),
        narrow_share(summed[3], 0, narrow_place, narrow_count),
        narrow_share(summed[4], 0, narrow_place, narrow_count),
        narrow_share(summed[5], 1, narrow_place, narrow_count),
    )
    row_totals = lax.psum(
        (
            first_gain_part,
            first_shift_part,
            out_bias_part,
            second_gain_part,
            second_shift_part,
            down_bias_part,
        ),
        ("dp", "wide", "narrow"),
    )
    return (
        output,
        input_grad,
        row_totals[0],
        row_totals[1],
        totals[0],
        totals[1],
        totals[2],
        row_totals[2],
        row_totals[3],
        row_totals[4],
        totals[3],
        totals[4],
        totals[5],
        row_totals[5],
    )


def solution(mesh):
    placed = (
        P(("dp", "wide", "narrow"), None),
        P(("dp", "wide", "narrow")),
        P(),
        P(),
        P("narrow", None, "wide"),
        P(None, "wide"),
        P("wide", "narrow"),
        P(),
        P(),
        P(),
        P("narrow", "wide"),
        P("wide"),
        P("wide", "narrow"),
        P(),
        P(("dp", "wide", "narrow"), None),
    )
    return jax.shard_map(
        shards,
        mesh=mesh,
        in_specs=placed,
        out_specs=(
            P(("dp", "wide", "narrow"), None),
            P(("dp", "wide", "narrow"), None),
            P(),
            P(),
            P("narrow", None, "wide"),
            P(None, ("wide", "narrow")),
            P("wide", "narrow"),
            P(),
            P(),
            P(),
            P("narrow", "wide"),
            P(("wide", "narrow")),
            P("wide", "narrow"),
            P(),
        ),
        check_vma=False,
    )
```

profile of v0, /device:TPU:0, one launch (start us, length us, event | category | flops | bytes accessed | tf_op | source)
XLA Modules:
  0.0 762.1 jit_solution(1008060425674741809)
XLA Ops:
  11.2 5.3 all-gather
  16.6 28.9 %all-gather.10.cloned.1.call-done = bf16[1024,1024]{1,0:T(8,128)(2,1)} async-done(((bf16[512,1024]{1,0:T(8,128)(2,1)}), bf16[1024,1024]{1,0:T(8,128)(2,1)}) %all-gather.10.cloned.1.call-update) | async-done | bytes 2097168 | tf_op jit(solution)/shard_map/all_gather | solution.py:131
  48.4 28.1 %all-gather.12.cloned.1.call-done = bf16[1024,3,512]{0,2,1:T(8,128)(2,1)} async-done(((bf16[256,3,512]{0,2,1:T(8,128)(2,1)}), bf16[1024,3,512]{0,2,1:T(8,128)(2,1)}) %all-gather.12.cloned.1.call-update) | async-done | bytes 3145744 | tf_op jit(solution)/shard_map/all_gather | solution.py:124
  76.5 7.0 add_convert_fusion.1
  83.6 8.9 %reshape.288 = bf16[2,512,3,8,64]{4,3,1,0,2:T(8,128)(2,1)} reshape(bf16[1024,3,512]{2,0,1:T(8,128)(2,1)} %add_convert_fusion.1) | data formatting | bytes 6291456 | tf_op jit(solution)/shard_map/reshape | solution.py:145
  92.5 6.4 copy.69
  98.9 13.7 %while.22 = (s32[]{:T(128)}, bf16[2,512,8,64]{1,3,2,0:T(8,128)(2,1)}, f32[2,8,512]{2,1,0:T(8,128)S(1)}, bf16[2,512,3,8,64]{1,4,3,2,0:T(8,128)(2,1)S(1)}, s32[2,512]{1,0:T(2,128)S(1)}, /*index=5*/s32[]{:T(128)}) while((s32[]{:T(128)}, bf16[2,512,8,64]{1,3,2,0:T(8,128)(2,1)}, f32[2,8,512]{2,1,0:T(8,128)S(1)}, ...), condition=%wide.region_5.6_spmd, body=%wide.region_2.5_spmd.sunk | while | flops 562556928 | bytes 31595088 | solution.py:147
  102.5 3.2 fusion.107
  109.3 3.2 fusion.107
  116.1 4.2 convolution_convert_fusion.6
  121.2 31.0 %reduce-scatter.5.cloned.1.call-done = bf16[512,1024]{1,0:T(8,128)(2,1)} async-done(((bf16[1024,1024]{1,0:T(8,128)(2,1)}), bf16[512,1024]{1,0:T(8,128)(2,1)}) %reduce-scatter.5.cloned.1.call-update) | async-done | bytes 1048592 | tf_op jit(solution)/shard_map/reduce_scatter | solution.py:150
  159.7 28.5 %all-gather.18.cloned.1.call-done = bf16[1024,2048]{1,0:T(8,128)(2,1)} async-done(((bf16[256,2048]{1,0:T(8,128)(2,1)}), bf16[1024,2048]{1,0:T(8,128)(2,1)}) %all-gather.18.cloned.1.call-update) | async-done | bytes 4194320 | tf_op jit(solution)/shard_map/all_gather | solution.py:126
  188.2 35.2 %all-gather.16.cloned.1.call-done = bf16[1024,1024]{1,0:T(8,128)(2,1)} async-done(((bf16[512,1024]{1,0:T(8,128)(2,1)}), bf16[1024,1024]{1,0:T(8,128)(2,1)}) %all-gather.16.cloned.1.call-update) | async-done | bytes 2097168 | tf_op jit(solution)/shard_map/all_gather | solution.py:159
  223.4 10.1 %multiply_convert_fusion.1 = (bf16[1024,2048]{1,0:T(8,128)(2,1)}, f32[1024,2048]{1,0:T(8,128)}) fusion(f32[2048]{0:T(1024)S(1)} %convert_element_type.145, bf16[1024,1024]{1,0:T(8,128)(2,1)} %all-gather.16.cloned.1.call-done, bf16[1024,2048]{1,0:T(8,128)(2,1)} %all-gather.18.cloned.1.call-done), kind=kOutput, calls=%fused_computation.52 | convolution fusion | flops 4307550208 | bytes 18882560 | tf_op jit(solution)/shard_map/dot_general | solution.py:160
  233.5 24.7 %all-gather.22.cloned.1.call-done = bf16[1024,1024]{1,0:T(8,128)(2,1)} async-done(((bf16[512,1024]{1,0:T(8,128)(2,1)}), bf16[1024,1024]{1,0:T(8,128)(2,1)}) %all-gather.22.cloned.1.call-update) | async-done | bytes 2097168 | tf_op jit(solution)/shard_map/all_gather | solution.py:175
  258.2 36.7 %all-gather.20.cloned.1.call-done = bf16[2048,1024]{1,0:T(8,128)(2,1)} async-done(((bf16[2048,256]{1,0:T(8,128)(2,1)}), bf16[2048,1024]{1,0:T(8,128)(2,1)}) %all-gather.20.cloned.1.call-update) | async-done | bytes 4194320 | tf_op jit(solution)/shard_map/all_gather | solution.py:127
  294.9 12.6 %fusion.72 = (bf16[2048]{0:T(1024)(128)(2,1)}, bf16[1024,2048]{1,0:T(8,128)(2,1)S(1)}) fusion(bf16[2048,1024]{1,0:T(8,128)(2,1)} %all-gather.20.cloned.1.call-done, bf16[1024,1024]{1,0:T(8,128)(2,1)} %all-gather.22.cloned.1.call-done, pred[1024]{0:T(1024)(128)(4,1)S(1)} %reshape.284, f32[1024,2048]{1,0:T(8,128)} %get-tuple-element.176, ...), kind=kOutput, calls=%fused_computation.131 | convolution fusion | flops 4327471104 | bytes 18887680 | tf_op jit(solution)/shard_map/td,fd->tf/dot_general | solution.py:178
  309.5 5.7 convolution_convert_fusion.4
  315.3 9.3 %convolution_convert_fusion.5 = bf16[1024,1024]{1,0:T(8,128)(2,1)} fusion(bf16[1024,2048]{1,0:T(8,128)(2,1)} %get-tuple-element.175, bf16[2048,1024]{1,0:T(8,128)(2,1)} %all-gather.20.cloned.1.call-done), kind=kOutput, calls=%fused_computation.100 | convolution fusion | flops 4296015872 | bytes 10485760 | tf_op jit(solution)/shard_map/dot_general | solution.py:166
  324.6 9.7 %all-gather.24.cloned.1.call-start = ((), (), s32[]{:S(2)}) async-start(), calls=%async_computation.14 | async-start | bytes 3145728 | tf_op jit(solution)/shard_map/all_gather | solution.py:197
  334.3 12.8 %reduce-scatter.9.cloned.1.call-done = bf16[512,1024]{1,0:T(8,128)(2,1)} async-done(((bf16[1024,1024]{1,0:T(8,128)(2,1)}), bf16[512,1024]{1,0:T(8,128)(2,1)}) %reduce-scatter.9.cloned.1.call-update) | async-done | bytes 1048592 | tf_op jit(solution)/shard_map/reduce_scatter | solution.py:188
  347.2 3.6 fusion.53
  350.8 30.9 %reduce-scatter.7.cloned.1.call-done = bf16[512,1024]{1,0:T(8,128)(2,1)} async-done(((bf16[1024,1024]{1,0:T(8,128)(2,1)}), bf16[512,1024]{1,0:T(8,128)(2,1)}) %reduce-scatter.7.cloned.1.call-update) | async-done | bytes 1048592 | tf_op jit(solution)/shard_map/reduce_scatter | solution.py:165
  381.7 4.9 fusion.68
  389.1 33.2 %all-gather.24.cloned.1.call-done = bf16[1024,1024]{1,0:T(8,128)(2,1)} async-done(((bf16[512,1024]{1,0:T(8,128)(2,1)}), bf16[1024,1024]{1,0:T(8,128)(2,1)}) %all-gather.24.cloned.1.call-update) | async-done | bytes 2097168 | tf_op jit(solution)/shard_map/all_gather | solution.py:197
  422.4 4.1 convolution_convert_fusion.8
  426.5 3.9 reshape.287
  430.4 3.3 copy.73
  433.7 26.3 %while.23 = (s32[]{:T(128)}, bf16[2,512,3,8,64]{1,4,3,2,0:T(8,128)(2,1)}, bf16[2,512,3,8,64]{1,4,3,2,0:T(8,128)(2,1)S(1)}, s32[2,512]{1,0:T(2,128)S(1)}, f32[2,8...) while((s32[]{:T(128)}, bf16[2,512,3,8,64]{1,4,3,2,0:T(8,128)(2,1)}, ...), condition=%wide.region_15.16_spmd, body=%wide.region_13.15_spmd.sunk | while | flops 1379921920 | bytes 79813248 | solution.py:210
  435.3 2.9 multiply_reduce_fusion.3
  438.2 2.7 multiply_convert_fusion.3
  448.4 2.9 multiply_reduce_fusion.3
  451.3 2.7 multiply_convert_fusion.3
  459.9 5.1 copy.74
  467.6 4.6 convolution_convert_fusion.3
  472.4 8.5 %convolution_convert_fusion.1 = bf16[1024,2048]{1,0:T(8,128)(2,1)} fusion(bf16[1024,1024]{1,0:T(8,128)(2,1)S(1)} %copy-done.32, bf16[1024,2048]{1,0:T(8,128)(2,1)} %copy-done.37), kind=kOutput, calls=%fused_computation.62 | convolution fusion | flops 4297064448 | bytes 10485760 | tf_op jit(solution)/shard_map/td,tf->df/dot_general | solution.py:183
  480.9 6.4 convolution_convert_fusion
  490.2 5.7 convolution_convert_fusion.2
  496.1 2.4 fusion.33
  498.5 2.5 reduce.2
  501.3 35.1 %all-reduce.1 = (bf16[2,512]{1,0:T(2,128)(2,1)S(1)}, bf16[2048]{0:T(1024)(128)(2,1)S(1)}) all-reduce(bf16[2,512]{1,0:T(2,128)(2,1)S(1)} %pad_maximum_fusion, bf16[2048]{0:T(1024)(128)(2,1)S(1)} %copy-done.27), channel_id=1, replica_groups=mesh['dp'=4,'wide'=2,'narrow'=4] {'dp','narrow'}, use_global_device_ids=true, to_apply=%region_25.26 | all-reduce | flops 3072 | bytes 12288 | tf_op jit(solution)/shard_map/psum | solution.py:238
  537.6 2.8 fusion.54
  540.4 38.9 %all-reduce = (f32[1024]{0:T(1024)}, f32[1024]{0:T(1024)}, f32[1024]{0:T(1024)}, f32[1024]{0:T(1024)}, f32[1024]{0:T(1024)}, /*index=5*/f32[1024]{0:T(1024)}) all-reduce(f32[1024]{0:T(1024)S(1)} %get-tuple-element.121, f32[1024]{0:T(1024)S(1)} %get-tuple-element.128, ...), channel_id=1, replica_groups=mesh['dp'=4,'wide'=2,'narrow'=4] {'dp','wide','narrow'}, use_global_device_ids=true, to_apply=%region_20.21 | all-reduce | flops 6144 | bytes 49152 | tf_op jit(solution)/shard_map/psum | solution.py:252
  579.3 3.2 fusion.47
  582.5 163.0 %all-reduce.5.cloned.1.call-done = (bf16[1024,3,512]{2,0,1:T(8,128)(2,1)}, bf16[512,1024]{1,0:T(8,128)(2,1)}, bf16[1024,2048]{1,0:T(8,128)(2,1)}, bf16[2048,1024]{1,0:T(8,128)(2,1)}) async-done(((bf16[1024,3,512]{2,0,1:T(8,128)(2,1)}, bf16[512,1024]{1,0:T(8,128)(2,1)}, bf16[1024,2048]{1,0:T(8,128)(2,1)}, bf16[2048,1024]{1,0:T(8,128)(2,1)}), (bf16[1024,3,512]{2,0,1:T(8,128)(2,1)}, ...) | async-done | bytes 12582928 | tf_op jit(solution)/shard_map/psum | solution.py:237
  745.5 2.7 dynamic-slice_convert_fusion
  748.2 2.8 dynamic-slice_convert_fusion.1
  750.9 2.5 dynamic-slice_convert_fusion.2
  (176 shorter events, 54.1 us)
Async XLA Ops:
  7.2 3.9 copy-start.24
  7.2 4.0 copy-start.22
  7.2 38.2 %all-gather.10.cloned.1.call-start = ((), (), s32[]{:S(2)}) async-start(), calls=%async_computation.4 | async-start | bytes 3145728 | tf_op jit(solution)/shard_map/all_gather | solution.py:131
  7.9 68.6 %copy-start.16 = (f32[1024]{0:T(1024)S(1)}, f32[1024]{0:T(1024)}, u32[]{:S(2)}) copy-start(f32[1024]{0:T(1024)} %param.21) | copy-start | bytes 12292
  7.9 68.6 %copy-start.35 = (f32[1024]{0:T(1024)S(1)}, f32[1024]{0:T(1024)}, u32[]{:S(2)}) copy-start(f32[1024]{0:T(1024)} %param.22) | copy-start | bytes 12292
  8.0 68.6 %all-gather.12.cloned.1.call-start = ((), (), s32[]{:S(2)}) async-start(), calls=%async_computation.5 | async-start | bytes 3932160 | tf_op jit(solution)/shard_map/all_gather | solution.py:124
  10.3 105.8 %all-gather.14.cloned.1.call-start = ((), (), s32[]{:S(2)}) async-start(), calls=%async_computation.6 | async-start | bytes 1310720 | tf_op jit(solution)/shard_map/all_gather | solution.py:125
  11.1 141.2 %reduce-scatter.5.cloned.1.call-start = ((), (), s32[]{:S(2)}) async-start(), calls=%async_computation.7 | async-start | bytes 3145728 | tf_op jit(solution)/shard_map/reduce_scatter | solution.py:150
  45.4 2.2 copy-start.4
  47.7 35.9 %copy-start.12 = (f32[1024]{0:T(1024)}, f32[1024]{0:T(1024)S(1)}, u32[]{:S(2)}) copy-start(f32[1024]{0:T(1024)S(1)} %broadcast_multiply_fusion) | copy-start | bytes 12292
  48.4 35.2 %copy-start.14 = (f32[1024]{0:T(1024)}, f32[1024]{0:T(1024)S(1)}, u32[]{:S(2)}) copy-start(f32[1024]{0:T(1024)S(1)} %add_rsqrt_fusion) | copy-start | bytes 12292
  120.3 36.2 %copy-start.11 = (f32[1024]{0:T(1024)S(1)}, f32[1024]{0:T(1024)}, u32[]{:S(2)}) copy-start(f32[1024]{0:T(1024)} %param.27) | copy-start | bytes 12292
  120.3 36.2 %copy-start.25 = (f32[1024]{0:T(1024)S(1)}, f32[1024]{0:T(1024)}, u32[]{:S(2)}) copy-start(f32[1024]{0:T(1024)} %param.28) | copy-start | bytes 12292
  120.3 67.9 %all-gather.18.cloned.1.call-start = ((), (), s32[]{:S(2)}) async-start(), calls=%async_computation.9 | async-start | bytes 5242880 | tf_op jit(solution)/shard_map/all_gather | solution.py:126
  120.9 102.6 %all-gather.16.cloned.1.call-start = ((), (), s32[]{:S(2)}) async-start(), calls=%async_computation.8 | async-start | bytes 3145728 | tf_op jit(solution)/shard_map/all_gather | solution.py:159
  152.2 4.3 copy-start
  152.2 4.3 copy-start.1
  156.5 3.1 copy-start.26
  158.1 100.1 %all-gather.22.cloned.1.call-start = ((), (), s32[]{:S(2)}) async-start(), calls=%async_computation.12 | async-start | bytes 3145728 | tf_op jit(solution)/shard_map/all_gather | solution.py:175
  158.9 136.0 %all-gather.20.cloned.1.call-start = ((), (), s32[]{:S(2)}) async-start(), calls=%async_computation.10 | async-start | bytes 5242880 | tf_op jit(solution)/shard_map/all_gather | solution.py:127
  159.6 187.6 %reduce-scatter.9.cloned.1.call-start = ((), (), s32[]{:S(2)}) async-start(), calls=%async_computation.13 | async-start | bytes 3145728 | tf_op jit(solution)/shard_map/reduce_scatter | solution.py:188
  294.9 14.6 %copy-start.30 = (bf16[1024,2048]{1,0:T(8,128)(2,1)S(1)}, bf16[1024,2048]{1,0:T(8,128)(2,1)}, u32[]{:S(2)}) copy-start(bf16[1024,2048]{1,0:T(8,128)(2,1)} %all-gather.18.cloned.1.call-done) | copy-start | bytes 12582916
  307.5 1.9 copy-start.37
  315.2 66.5 %reduce-scatter.7.cloned.1.call-start = ((), (), s32[]{:S(2)}) async-start(), calls=%async_computation.11 | async-start | bytes 3145728 | tf_op jit(solution)/shard_map/reduce_scatter | solution.py:165
  315.2 19.1 %copy-start.29 = (bf16[1024]{0:T(1024)(128)(2,1)S(1)}, bf16[1024]{0:T(1024)(128)(2,1)}, u32[]{:S(2)}) copy-start(bf16[1024]{0:T(1024)(128)(2,1)} %param.32) | copy-start | bytes 6148
  315.3 19.1 %copy-start.23 = (s32[512]{0:T(512)S(1)}, s32[512]{0:T(512)}, u32[]{:S(2)}) copy-start(s32[512]{0:T(512)} %param.20) | copy-start | bytes 6148
  324.6 97.8 %all-gather.24.cloned.1.call-start = ((), (), s32[]{:S(2)}) async-start(), calls=%async_computation.14 | async-start | bytes 3145728 | tf_op jit(solution)/shard_map/all_gather | solution.py:197
  389.1 148.5 %reduce-scatter.11.cloned.1.call-start = ((), (), s32[]{:S(2)}) async-start(), calls=%async_computation.15 | async-start | bytes 3145728 | tf_op jit(solution)/shard_map/reduce_scatter | solution.py:221
  465.1 2.5 copy-start.31
  467.6 4.7 copy-start.32
  472.3 273.2 %all-reduce.5.cloned.1.call-start = ((), (), s32[]{:S(2)}) async-start(), calls=%async_computation.16 | async-start | bytes 25165824 | tf_op jit(solution)/shard_map/psum | solution.py:237
  472.4 8.5 %copy-start.33 = (bf16[1024,1024]{1,0:T(8,128)(2,1)S(1)}, bf16[1024,1024]{1,0:T(8,128)(2,1)}, u32[]{:S(2)}) copy-start(bf16[1024,1024]{1,0:T(8,128)(2,1)} %all-gather.22.cloned.1.call-done) | copy-start | bytes 6291460
  472.4 8.5 %copy-start.38 = (bf16[1024,2048]{1,0:T(8,128)(2,1)S(1)}, bf16[1024,2048]{1,0:T(8,128)(2,1)}, u32[]{:S(2)}) copy-start(bf16[1024,2048]{1,0:T(8,128)(2,1)} %get-tuple-element.175) | copy-start | bytes 12582916
  480.9 6.4 copy-start.10
  480.9 6.4 copy-start.34
  487.3 2.3 copy-start.5
  487.3 2.9 copy-start.9
  487.3 2.9 copy-start.13
  487.3 2.9 copy-start.15
  487.3 2.9 copy-start.17
  487.4 2.9 copy-start.36
  498.5 2.8 copy-start.27
  498.5 41.9 %copy-start.18 = (f32[1024]{0:T(1024)S(1)}, f32[1024]{0:T(1024)}, u32[]{:S(2)}) copy-start(f32[1024]{0:T(1024)} %get-tuple-element.123) | copy-start | bytes 12292
  498.5 41.9 %copy-start.19 = (f32[1024]{0:T(1024)S(1)}, f32[1024]{0:T(1024)}, u32[]{:S(2)}) copy-start(f32[1024]{0:T(1024)} %get-tuple-element.127) | copy-start | bytes 12292
  498.5 41.9 %copy-start.20 = (f32[1024]{0:T(1024)S(1)}, f32[1024]{0:T(1024)}, u32[]{:S(2)}) copy-start(f32[1024]{0:T(1024)} %get-tuple-element.163) | copy-start | bytes 12292
  498.5 41.9 %copy-start.21 = (f32[1024]{0:T(1024)S(1)}, f32[1024]{0:T(1024)}, u32[]{:S(2)}) copy-start(f32[1024]{0:T(1024)} %get-tuple-element.170) | copy-start | bytes 12292
  498.5 80.8 %copy-start.3 = (f32[512,1024]{1,0:T(8,128)S(1)}, f32[512,1024]{1,0:T(8,128)}, u32[]{:S(2)}) copy-start(f32[512,1024]{1,0:T(8,128)} %copy-done.2) | copy-start | bytes 6291460
  537.6 41.7 %copy-start.7 = (bf16[512,1024]{1,0:T(8,128)(2,1)S(1)}, bf16[512,1024]{1,0:T(8,128)(2,1)}, u32[]{:S(2)}) copy-start(bf16[512,1024]{1,0:T(8,128)(2,1)} %reduce-scatter.11.cloned.1.call-done) | copy-start | bytes 3145732
  (5 other events, 7.1 us)
Sparse Core Ops, SparseCore 0:
  9.6 35.8 all-gather.9
  47.6 28.9 all-gather.11
  78.1 16.8 all-gather.13
  120.4 31.8 reduce-scatter.4
  153.7 34.4 all-gather.17
  190.3 33.1 all-gather.15
  225.0 33.1 all-gather.21
  259.8 35.0 all-gather.19
  315.3 31.8 reduce-scatter.8
  349.9 31.8 reduce-scatter.6
  389.2 33.1 all-gather.23
  472.4 31.8 reduce-scatter.10
  509.4 235.9 all-reduce.4
where the time goes:
time: 772 us; the launch traced here: 762 us
  waiting for transfers between devices  456 us (59%)
  matrix products  107 us (14%)
  blocking collectives  79.3 us (10%)
  other arithmetic  52.5 us (7%)
  local copies, waits for them, and re-layouts  41 us (5%)
  between operations  14.8 us (2%)
  starting transfers between devices  10.5 us (1%)
    psum x1, waiting for transfers between devices, shards(): lax.psum(qkv_part.astype(jnp.bfloat16), ('dp', 'narrow'))  163 us
    psum x1, blocking collectives, shards(): lax.psum((first_gain_part, first_shift_part, out_bias_part, second_gain_p...  38.9 us
    all_gather x1, waiting for transfers between devices, shards(): lax.all_gather(down_weight, 'narrow', axis=1, tiled=True)  36.7 us
    all_gather x1, waiting for transfers between devices, shards(): normed_two_all = lax.all_gather(normed_two, 'wide', axis=0, tiled=True)  35.2 us
    psum x1, blocking collectives, shards(): lax.psum(qv_part.astype(jnp.bfloat16), ('dp', 'narrow')).astype(jnp.float32)  35.1 us
    all_gather x1, waiting for transfers between devices, shards(): lax.all_gather(grad_middle_own.astype(jnp.bfloat16), 'wide', axis=0, tile...  33.2 us
    reduce_scatter x1, waiting for transfers between devices, shards(): lax.psum_scatter(jnp.dot(row_piece, out_full, preferred_element_type=jnp....  31 us
    reduce_scatter x1, waiting for transfers between devices, shards(): lax.psum_scatter(jnp.dot(row_piece, down_full, preferred_element_type=jnp...  30.9 us
  transfers between devices with their start and end apart: 13, of which 11 were waited for; matrix products, arithmetic and copies ran while one was open for 14% of the time, Pallas kernels for 0%

commit v1 on v0

v1 whole, which is shorter than its diff:
```python
from functools import partial

import jax
import jax.numpy as jnp
import numpy as np
from jax import lax
from jax.experimental import pallas as pl
from jax.experimental.pallas import tpu as pltpu
from jax.sharding import PartitionSpec as P

HD = 64
LEN = 512
LANES = 128
EPSILON = 1e-06
MASKED = -1e30
SQRT_HALF = 0.7071067811865476
DENSITY_SCALE = 0.3989422804014327
BF = jnp.bfloat16
F32 = jnp.float32
MIB = 1 << 20

NN = (((1,), (0,)), ((), ()))
NT = (((1,), (1,)), ((), ()))


def dot(left, right, dims=NN):
    return lax.dot_general(left, right, dims, preferred_element_type=F32)


def call(body, grid, ins, outs, operands, scratch=(), flops=0, name=None, vmem=58, tables=0):
    moved = sum(int(np.prod(o.shape)) * o.dtype.itemsize for o in operands)
    moved += sum(int(np.prod(o.shape)) * o.dtype.itemsize for _, o in outs)
    return pl.pallas_call(
        body,
        out_shape=[o for _, o in outs],
        grid_spec=pltpu.PrefetchScalarGridSpec(
            num_scalar_prefetch=tables,
            grid=grid,
            in_specs=ins,
            out_specs=[s for s, _ in outs],
            scratch_shapes=list(scratch),
        ),
        compiler_params=pltpu.CompilerParams(vmem_limit_bytes=vmem * MIB),
        cost_estimate=pl.CostEstimate(flops=int(flops), bytes_accessed=moved, transcendentals=0),
        name=name,
    )(*operands)


def after(value, *others):
    return lax.optimization_barrier((value, *others))[0]


def shape(dims, dtype):
    return jax.ShapeDtypeStruct(dims, dtype)


def columns(meta, ref, places, width):
    return jnp.concatenate(
        [ref[:, pl.ds(pl.multiple_of(meta[r], width), width)] for r in range(places)], axis=1
    )


def norm_stats(values):
    average = jnp.mean(values, axis=-1, keepdims=True)
    centred = values - average
    variance = jnp.mean(centred * centred, axis=-1, keepdims=True)
    scaled = lax.rsqrt(variance + EPSILON)
    return centred * scaled, scaled


def norm_back(upstream, gain, normal, scaled):
    inner = upstream * gain
    first_term = jnp.mean(inner, axis=-1, keepdims=True)
    second_term = jnp.mean(inner * normal, axis=-1, keepdims=True)
    return scaled * (inner - first_term - normal * second_term)


def first_norm(inputs, cotangent, keep, gain, shift, meta, places):
    rows, width = inputs.shape
    block = 128
    part = width // places

    def body(meta, x, cot, keep, gain, shift, normed, normed_t, low, low_t):
        normal, _ = norm_stats(columns(meta, x, places, part).astype(F32))
        out = normal * columns(meta, gain, places, part) + columns(meta, shift, places, part)
        normed[...] = out.astype(BF)
        normed_t[...] = out.T.astype(BF)
        grad = columns(meta, cot, places, part).astype(F32) * keep[...]
        low[...] = grad.astype(BF)
        low_t[...] = grad.T.astype(BF)

    tall = pl.BlockSpec((block, width), lambda i, *_: (i, 0))
    wide = pl.BlockSpec((width, block), lambda i, *_: (0, i))
    vector = pl.BlockSpec((1, width), lambda i, *_: (0, 0))
    mark = pl.BlockSpec((block, 1), lambda i, *_: (i, 0))
    return call(
        body,
        (rows // block,),
        [tall, tall, mark, vector, vector],
        [
            (tall, shape((rows, width), BF)),
            (wide, shape((width, rows), BF)),
            (tall, shape((rows, width), BF)),
            (wide, shape((width, rows), BF)),
        ],
        (meta, inputs, cotangent, keep, gain, shift),
        tables=1,
        name="first_norm",
    )


def tile_of(refs, step, steps):
    blocks = []
    for parts in refs:
        value = parts[0][...]
        for k in range(1, len(parts)):
            value = jnp.where(step >= k * (steps // len(parts)), parts[k][...], value)
        blocks.append(value)
    return jnp.concatenate(blocks, axis=0)


def tile_specs(pieces, width, steps):
    specs, operands, counts = [], [], []
    for parts in pieces:
        counts.append(len(parts))
        per = steps // len(parts)
        for k, array in enumerate(parts):
            specs.append(
                pl.BlockSpec(
                    (array.shape[0], width),
                    lambda j, *_, k=k, per=per: (0, jnp.clip(j - k * per, 0, per - 1)),
                )
            )
            operands.append(array)
    return specs, operands, counts


def regroup(refs, counts):
    grouped, at = [], 0
    for count in counts:
        grouped.append(refs[at : at + count])
        at += count
    return grouped


def attend(normed, pieces, bias, labels_col, labels_row, halves):
    rows, width = normed.shape
    total = sum(p.shape[1] for p in pieces[0])
    wide = total // halves
    part = wide // 4
    heads = part // HD
    specs, weights, counts = tile_specs(pieces, wide, halves)

    def body(normed, *refs):
        weight_refs = regroup(refs[: len(weights)], counts)
        bias, lc, lr, qkv, attended, probs, inverses, branch, mask = refs[len(weights) :]
        step = pl.program_id(0)

        @pl.when(step == 0)
        def _():
            mask[...] = jnp.where(lc[...] == lr[...], 0.0, MASKED)

        tile = tile_of(weight_refs, step, halves)
        projected = dot(normed[...], tile[:, : 3 * part]) + bias[...].astype(F32)
        low = projected.astype(BF)
        qkv[...] = low
        lane = lax.broadcasted_iota(jnp.int32, (1, LANES), 1)
        per = LANES // HD
        queries, keys, values = [], [], []
        for pair in range(part // LANES):
            at = pair * LANES
            queries.append(low[:, at : at + LANES] * jnp.asarray(HD**-0.5, BF))
            keys.append(low[:, part + at : part + at + LANES])
            values.append(low[:, 2 * part + at : 2 * part + at + LANES].T)

        def scores_of(head):
            pair, e = divmod(head, per)
            mine = (lane >= e * HD) & (lane < (e + 1) * HD)
            key = jnp.where(mine, keys[pair], jnp.zeros_like(keys[pair]))
            return dot(key, queries[pair], NT)

        coming, outs = scores_of(0), []
        for head in range(heads):
            scores = coming
            if head + 1 < heads:
                coming = scores_of(head + 1)
            pair, e = divmod(head, per)
            scores = scores + mask[...]
            weight = jnp.exp(scores - jnp.max(scores, axis=0, keepdims=True))
            inverse = 1.0 / jnp.sum(weight, axis=0, keepdims=True)
            prob = weight.astype(BF)
            probs[head] = prob
            inverses[0, head : head + 1, :] = inverse
            outs.append(dot(values[pair][e * HD : (e + 1) * HD], prob) * inverse)
            if e == per - 1:
                at = pair * LANES
                attended[:, at : at + LANES] = jnp.concatenate(outs, axis=0).T.astype(BF)
                outs = []
        product = dot(attended[...], tile[:, 3 * part :], NT)

        @pl.when(step == 0)
        def _():
            branch[...] = product

        @pl.when(step > 0)
        def _():
            branch[...] += product

    fixed = lambda *dims: pl.BlockSpec(dims, lambda j, *_: (0,) * len(dims))
    return call(
        body,
        (halves,),
        [fixed(rows, width)]
        + specs
        + [pl.BlockSpec((1, 3 * part), lambda j: (0, j)), fixed(rows, 1), fixed(1, rows)],
        [
            (pl.BlockSpec((rows, 3 * part), lambda j: (0, j)), shape((rows, halves * 3 * part), BF)),
            (pl.BlockSpec((rows, part), lambda j: (0, j)), shape((rows, halves * part), BF)),
            (
                pl.BlockSpec((heads, rows, rows), lambda j: (j, 0, 0)),
                shape((halves * heads, rows, rows), BF),
            ),
            (pl.BlockSpec((1, heads, rows), lambda j: (j, 0, 0)), shape((halves, heads, rows), F32)),
            (fixed(rows, width), shape((rows, width), F32)),
        ],
        (normed, *weights, bias, labels_col, labels_row),
        scratch=[pltpu.VMEM((rows, rows), F32)],
        flops=2 * rows * width * total + halves * heads * 8 * rows * rows * HD,
        name="attend",
    )


def second_norm(inputs, branches, out_bias, gain, shift, meta, places):
    rows, width = inputs.shape
    block = 128
    part = width // places
    count = len(branches)

    def body(meta, x, *refs):
        bias, gain, shift, middle, normed, normed_t = refs[count:]
        value = columns(meta, x, places, part).astype(F32)
        total = refs[0][...]
        for ref in refs[1:count]:
            total = total + ref[...]
        value = value + total + columns(meta, bias, places, part)
        middle[...] = value
        normal, _ = norm_stats(value)
        out = normal * columns(meta, gain, places, part) + columns(meta, shift, places, part)
        normed[...] = out.astype(BF)
        normed_t[...] = out.T.astype(BF)

    tall = pl.BlockSpec((block, width), lambda i, *_: (i, 0))
    wide = pl.BlockSpec((width, block), lambda i, *_: (0, i))
    vector = pl.BlockSpec((1, width), lambda i, *_: (0, 0))
    return call(
        body,
        (rows // block,),
        [tall] * (1 + count) + [vector] * 3,
        [
            (tall, shape((rows, width), F32)),
            (tall, shape((rows, width), BF)),
            (wide, shape((width, rows), BF)),
        ],
        (meta, inputs, *branches, out_bias, gain, shift),
        tables=1,
        name="second_norm",
    )


def up_steps(total, halves):
    return max(halves, total // 512)


def up(normed, pieces, bias, halves):
    rows, width = normed.shape
    total = sum(p.shape[1] for p in pieces[0])
    steps = up_steps(total, halves)
    wide = total // steps
    specs, weights, counts = tile_specs(pieces, wide, steps)

    def body(normed, *refs):
        weight_refs = regroup(refs[: len(weights)], counts)
        bias, hidden, slope = refs[len(weights) :]
        tile = tile_of(weight_refs, pl.program_id(0), steps)
        before = dot(normed[...], tile) + bias[...].astype(F32)
        below = 0.5 * (1.0 + lax.erf(before * SQRT_HALF))
        hidden[...] = (before * below).astype(BF)
        density = jnp.exp(before * before * -0.5) * DENSITY_SCALE
        slope[...] = (below + before * density).astype(BF)

    tall = pl.BlockSpec((rows, wide), lambda j: (0, j))
    return call(
        body,
        (steps,),
        [pl.BlockSpec((rows, width), lambda j: (0, 0))]
        + specs
        + [pl.BlockSpec((1, wide), lambda j: (0, j))],
        [(tall, shape((rows, total), BF)), (tall, shape((rows, total), BF))],
        (normed, *weights, bias),
        flops=2 * rows * width * total,
        name="up",
    )


def mlp_back(low, hidden, slope, up_pieces, down_pieces, halves):
    rows, width = low.shape
    total = hidden.shape[1]
    steps = up_steps(total, halves)
    wide = total // steps
    up_specs, up_weights, up_counts = tile_specs(up_pieces, wide, steps)
    down_specs, down_weights, down_counts = tile_specs(down_pieces, wide, steps)
    count = len(up_weights)

    def body(low, hidden, slope, *refs):
        up_refs = regroup(refs[:count], up_counts)
        down_refs = regroup(refs[count : 2 * count], down_counts)
        before, sums, mlp, normed = refs[2 * count :]
        step = pl.program_id(0)
        down_tile = tile_of(down_refs, step, steps)
        up_tile = tile_of(up_refs, step, steps)
        grad = dot(low[...], down_tile) * slope[...].astype(F32)
        grad_low = grad.astype(BF)
        before[...] = grad_low
        sums[...] = jnp.sum(grad_low.astype(F32), axis=0, keepdims=True)
        product = dot(hidden[...], down_tile, NT)
        back = dot(grad_low, up_tile, NT)

        @pl.when(step == 0)
        def _():
            mlp[...] = product
            normed[...] = back

        @pl.when(step > 0)
        def _():
            mlp[...] += product
            normed[...] += back

    fixed = pl.BlockSpec((rows, width), lambda j: (0, 0))
    tall = pl.BlockSpec((rows, wide), lambda j: (0, j))
    return call(
        body,
        (steps,),
        [fixed, tall, tall] + up_specs + down_specs,
        [
            (tall, shape((rows, total), BF)),
            (pl.BlockSpec((1, wide), lambda j: (0, j)), shape((1, total), F32)),
            (fixed, shape((rows, width), F32)),
            (fixed, shape((rows, width), F32)),
        ],
        (low, hidden, slope, *up_weights, *down_weights),
        flops=6 * rows * width * total,
        name="mlp_back",
    )


def second_norm_back(middle, backs, low, gain, meta, places):
    rows, width = middle.shape
    block = 128
    part = width // places
    count = len(backs)

    def body(meta, middle, low, *refs):
        gain, grad, grad_low, grad_t, sums = refs[count:]
        upstream = refs[0][...]
        for ref in refs[1:count]:
            upstream = upstream + ref[...]
        normal, scaled = norm_stats(middle[...])
        out = low[...].astype(F32)
        total = out + norm_back(upstream, columns(meta, gain, places, part), normal, scaled)
        grad[...] = total
        grad_low[...] = total.astype(BF)
        grad_t[...] = total.T.astype(BF)

        @pl.when(pl.program_id(0) == 0)
        def _():
            sums[...] = jnp.zeros_like(sums)

        for k, value in enumerate((upstream * normal, upstream, total, out)):
            added = jnp.sum(value, axis=0, keepdims=True)
            for r in range(places):
                spot = pl.ds(pl.multiple_of(meta[r], part), part)
                sums[k : k + 1, spot] += added[:, r * part : (r + 1) * part]

    tall = pl.BlockSpec((block, width), lambda i, *_: (i, 0))
    wide = pl.BlockSpec((width, block), lambda i, *_: (0, i))
    vector = pl.BlockSpec((1, width), lambda i, *_: (0, 0))
    return call(
        body,
        (rows // block,),
        [tall, tall] + [tall] * count + [vector],
        [
            (tall, shape((rows, width), F32)),
            (tall, shape((rows, width), BF)),
            (wide, shape((width, rows), BF)),
            (pl.BlockSpec((4, width), lambda i, *_: (0, 0)), shape((4, width), F32)),
        ],
        (meta, middle, low, *backs, gain),
        tables=1,
        name="second_norm_back",
    )


def attend_back(grad_low, pieces, qkv, probs, inverses, halves):
    rows, width = grad_low.shape
    total = sum(p.shape[1] for p in pieces[0])
    wide = total // halves
    part = wide // 4
    heads = part // HD
    specs, weights, counts = tile_specs(pieces, wide, halves)

    def body(grad_low, *refs):
        weight_refs = regroup(refs[: len(weights)], counts)
        qkv, probs, inverses, grads, sums, back = refs[len(weights) :]
        step = pl.program_id(0)
        tile = tile_of(weight_refs, step, halves)
        upstream = dot(grad_low[...], tile[:, 3 * part :]).astype(BF)
        lane = lax.broadcasted_iota(jnp.int32, (1, LANES), 1)
        factor = HD**-0.5
        per = LANES // HD
        queries, keys, values, ups = [], [], [], []
        for pair in range(part // LANES):
            at = pair * LANES
            queries.append(qkv[:, at : at + LANES] * jnp.asarray(factor, BF))
            key = qkv[:, part + at : part + at + LANES]
            keys.append((key * jnp.asarray(factor, BF)).T)
            values.append(qkv[:, 2 * part + at : 2 * part + at + LANES])
            up_t = upstream[:, at : at + LANES].T.astype(F32)
            scaled = [
                up_t[e * HD : (e + 1) * HD] * inverses[0, pair * per + e : pair * per + e + 1, :]
                for e in range(per)
            ]
            ups.append(jnp.concatenate(scaled, axis=0).T.astype(BF))

        def own(value, e):
            mine = (lane >= e * HD) & (lane < (e + 1) * HD)
            return jnp.where(mine, value, jnp.zeros_like(value))

        def first_of(head):
            pair, e = divmod(head, per)
            return dot(own(values[pair], e), ups[pair], NT)

        coming = first_of(0)
        for head in range(heads):
            pair, e = divmod(head, per)
            at = pair * LANES
            grad_probs = coming
            if head + 1 < heads:
                coming = first_of(head + 1)
            prob = probs[head].astype(F32)
            delta = jnp.sum(prob * grad_probs, axis=0, keepdims=True)
            delta = delta * inverses[0, head : head + 1, :]
            made = (prob * (grad_probs - delta)).astype(BF)
            if e == 0:
                grad_key = dot(made, own(queries[pair], e))
                grad_value = dot(probs[head], own(ups[pair], e))
                query_t = []
            else:
                grad_key = grad_key + dot(made, own(queries[pair], e))
                grad_value = grad_value + dot(probs[head], own(ups[pair], e))
            query_t.append(dot(keys[pair][e * HD : (e + 1) * HD], made))
            if e == per - 1:
                grad_query = jnp.concatenate(query_t, axis=0).T
                for c, grad in enumerate((grad_query, grad_key, grad_value)):
                    grads[:, c * part + at : c * part + at + LANES] = grad.astype(BF)
        made = grads[...]
        sums[...] = jnp.sum(made.astype(F32), axis=0, keepdims=True)
        product = dot(made, tile[:, : 3 * part], NT)

        @pl.when(step == 0)
        def _():
            back[...] = product

        @pl.when(step > 0)
        def _():
            back[...] += product

    fixed = pl.BlockSpec((rows, width), lambda j: (0, 0))
    wide_rows = pl.BlockSpec((rows, 3 * part), lambda j: (0, j))
    return call(
        body,
        (halves,),
        [fixed]
        + specs
        + [
            wide_rows,
            pl.BlockSpec((heads, rows, rows), lambda j: (j, 0, 0)),
            pl.BlockSpec((1, heads, rows), lambda j: (j, 0, 0)),
        ],
        [
            (wide_rows, shape((rows, halves * 3 * part), BF)),
            (pl.BlockSpec((1, 3 * part), lambda j: (0, j)), shape((1, halves * 3 * part), F32)),
            (fixed, shape((rows, width), F32)),
        ],
        (grad_low, *weights, qkv, probs, inverses),
        flops=2 * rows * width * total + halves * heads * 8 * rows * rows * HD,
        name="attend_back",
    )


def finish(inputs, middle, mlps, grad_middle, backs, keep, gain, down_bias, meta, places):
    rows, width = inputs.shape
    block = 128
    part = width // places
    count = len(mlps)

    def body(meta, x, middle, grad, keep, *refs):
        gain, bias, output, input_grad, sums = refs[2 * count :]
        mlp, upstream = refs[0][...], refs[count][...]
        for k in range(1, count):
            mlp = mlp + refs[k][...]
            upstream = upstream + refs[count + k][...]
        out = (middle[...] + mlp + columns(meta, bias, places, part)) * keep[...]
        normal, scaled = norm_stats(columns(meta, x, places, part).astype(F32))
        back = grad[...] + norm_back(upstream, columns(meta, gain, places, part), normal, scaled)

        @pl.when(pl.program_id(0) == 0)
        def _():
            sums[...] = jnp.zeros_like(sums)

        gains = jnp.sum(upstream * normal, axis=0, keepdims=True)
        shifts = jnp.sum(upstream, axis=0, keepdims=True)
        for r in range(places):
            spot = pl.ds(pl.multiple_of(meta[r], part), part)
            here = slice(r * part, (r + 1) * part)
            output[:, spot] = out[:, here].astype(BF)
            input_grad[:, spot] = back[:, here].astype(BF)
            sums[0:1, spot] += gains[:, here]
            sums[1:2, spot] += shifts[:, here]

    tall = pl.BlockSpec((block, width), lambda i, *_: (i, 0))
    vector = pl.BlockSpec((1, width), lambda i, *_: (0, 0))
    mark = pl.BlockSpec((block, 1), lambda i, *_: (i, 0))
    return call(
        body,
        (rows // block,),
        [tall, tall, tall, mark] + [tall] * (2 * count) + [vector, vector],
        [
            (tall, shape((rows, width), BF)),
            (tall, shape((rows, width), BF)),
            (pl.BlockSpec((2, width), lambda i, *_: (0, 0)), shape((2, width), F32)),
        ],
        (meta, inputs, middle, grad_middle, keep, *mlps, *backs, gain, down_bias),
        tables=1,
        name="finish",
    )


def bundle_plan(groups, halves):
    plan = {"x": [(1, 0, 0)] + [(1, y, 0) for y in range(1, groups)]}
    for y in range(1, groups):
        if halves > 1:
            plan["y", y] = [(0, y, 1), (1, y, 1)]
        plan["keep", y] = [(0, y, 0)]
    if halves > 1:
        plan["far"] = [(1, 0, 1)]
    plan["own"] = [(0, 0, h) for h in range(halves)]
    return plan


def weight_grads(plan, lefts, rights, groups, halves):
    width, rows = lefts[0].shape
    part = width // 4
    lines = len(rights)
    blocks = groups * halves // lines
    spans = [array.shape[1] // blocks for array in rights[0]]
    wide = sum(spans)
    kinds = len(spans)
    order = [(y, 0) for y in range(groups)] + [(y, h) for h in range(1, halves) for y in [*range(1, groups), 0]]
    names = list(plan)
    outs, joint = [], {}
    for _ in range(2):
        for name in names:
            steps = [order.index(block[1:]) for block in plan[name]]
            joint[name] = len(set(steps)) == 1
            size = wide * (len(steps) if joint[name] else 1)
            starts = [] if joint[name] else steps[1:]

            def index(i, starts=starts):
                at = 0
                for start in starts:
                    at = at + (i >= start).astype(jnp.int32)
                return (0, at)

            outs.append((pl.BlockSpec((part, size), index), shape((part, wide * len(steps)), BF)))

    def body(*refs):
        left_refs = refs[:kinds]
        right_refs = [refs[kinds + g * kinds : kinds + (g + 1) * kinds] for g in range(lines)]
        out_refs = refs[kinds + lines * kinds :]
        step = pl.program_id(0)
        for s, (y, h) in enumerate(order):

            @pl.when(step == s)
            def _(y=y, h=h):
                line = (y * halves + h) // blocks
                for r in range(4):
                    x, core = divmod(r, 2)
                    here = slice(r * part, (r + 1) * part)
                    products = [
                        dot(left_refs[k][here, :], right_refs[line][k][...]).astype(BF)
                        for k in range(kinds)
                    ]
                    value = jnp.concatenate(products, axis=1) if kinds > 1 else products[0]
                    for n, name in enumerate(names):
                        if (x, y, h) in plan[name]:
                            at = plan[name].index((x, y, h)) * wide if joint[name] else 0
                            out_refs[core * len(names) + n][:, at : at + wide] = value

    def right_map(g):
        flat = [y * halves + h for y, h in order]
        mine = [(s, at % blocks) for s, at in enumerate(flat) if at // blocks == g]
        def index(i):
            at = mine[0][1]
            for (s0, h0), (s1, h1) in zip(mine, mine[1:]):
                at = at + jnp.where(i > s0, h1 - h0, 0)
            return (0, at)
        return index
    ins = [pl.BlockSpec((width, rows), lambda i: (0, 0)) for _ in lefts]
    operands = list(lefts)
    for g in range(lines):
        for k in range(kinds):
            ins.append(pl.BlockSpec((rows, spans[k]), right_map(g)))
            operands.append(rights[g][k])
    made = call(body, (len(order),), ins, outs, operands, flops=2 * rows * width * wide * len(order), name="weight_grads")
    return dict(zip(names, made[: len(names)])), dict(zip(names, made[len(names) :]))


def shards(
    inputs,
    segments,
    first_gain,
    first_shift,
    qkv_weight,
    qv_bias,
    out_weight,
    out_bias,
    second_gain,
    second_shift,
    up_weight,
    up_bias,
    down_weight,
    down_bias,
    cotangent,
):
    groups = lax.axis_size("wide")
    copies = lax.axis_size("dp")
    places = lax.axis_size("narrow")
    place = lax.axis_index("narrow")
    member = lax.axis_index("wide")
    rows, width = inputs.shape
    part_width = qkv_weight.shape[2]
    hidden_width = up_weight.shape[1]
    part = width // places
    halves = 2 if part_width >= 2 * LANES else 1
    head_part = part_width // halves
    lines = min(2, groups)
    per_line = groups // lines
    steps = per_line * halves

    def members(line):
        return range(line * per_line, (line + 1) * per_line)

    def swap(axis, mask):
        size = lax.axis_size(axis)
        pairs = [(i, i ^ mask) for i in range(size)]
        return lambda value: lax.ppermute(value, axis, pairs)

    core = swap("narrow", 1)
    over_x = swap("narrow", 2)
    over_y = [None] + [swap("wide", m) for m in range(1, groups)]

    meta = jnp.bitwise_xor(place, jnp.arange(places, dtype=jnp.int32)) * part
    row_of = lambda vector: vector.astype(F32).reshape(1, -1)
    keep = (segments >= 0).astype(F32).reshape(rows, 1)
    labels_col = segments.reshape(rows, 1)
    labels_row = segments.reshape(1, rows)

    three = qkv_weight.reshape(part, 3, halves, head_part)
    out_t = out_weight.T.reshape(part, 1, halves, head_part)
    packed = jnp.concatenate([three, out_t], axis=1).transpose(0, 2, 1, 3)
    packed = packed.reshape(part, 4 * part_width)
    small = jnp.concatenate([qv_bias.reshape(-1), up_bias]).reshape(1, -1)
    down_t = down_weight.T

    def split(array):
        wide = array.shape[1] // halves
        return [array[:, h * wide : (h + 1) * wide] for h in range(halves)]

    def reach(own, *others):
        ready = after(own, *others) if others else own
        near = {(0, 0): [own], (1, 0): [over_x(ready)]}
        for y in range(1, groups):
            near[0, y] = [over_y[y](ready)]
        return near

    def forward_far(near):
        made = {}
        for y in range(1, groups):
            made[1, y] = [over_x(split(near[0, y][0])[0])]
            if halves > 1:
                made[1, y].append(over_y[y](split(near[1, 0][0])[1]))
        return made

    def line_of(near, line):
        made = []
        for x in range(2):
            parts = [array for y in members(line) for array in near[x, y]]
            made.append(parts)
            made.append([core(array) for array in parts])
        return made

    small_all = [small] + [over_y[y](small) for y in range(1, groups)]

    turn = []

    def ordered(value, *others):
        return after(value, *turn, *others) if turn or others else value

    def done(made, key):
        turn[:] = [made[key]]
        return made

    def first_stage(near):
        return [near[1, 0][0]] + [near[0, y][0] for y in range(1, groups)]

    def held(near, *others):
        return {
            key: value if key == (0, 0) else [after(array, *others) for array in value]
            for key, value in near.items()
        }

    attn_near = reach(packed)
    normed_one, normed_one_t, low, low_t = done(
        first_norm(
            inputs, cotangent, keep, row_of(first_gain), row_of(first_shift), meta, places
        ),
        0,
    )
    attn_near = held(attn_near, *turn)
    up_near = reach(up_weight, *first_stage(attn_near))

    def qkv_bias(values):
        query = values[:, :part_width].reshape(halves, 1, head_part)
        value = values[:, part_width : 2 * part_width].reshape(halves, 1, head_part)
        return jnp.concatenate([query, jnp.zeros_like(query), value], axis=1).reshape(1, -1)

    forward = []
    far = forward_far(attn_near)
    attn_pieces = [line_of(attn_near | {key: far[key] for key in far if key[1] < per_line}, 0)]
    for line in range(lines):
        if line:
            attn_near = held(attn_near | far, *turn)
            attn_pieces.append(line_of(attn_near, line))
        bias = jnp.concatenate([qkv_bias(small_all[y]) for y in members(line)], axis=1)
        forward.append(
            done(
                attend(
                    ordered(normed_one), attn_pieces[line], bias, labels_col, labels_row, steps
                ),
                1,
            )
        )
    up_near = held(up_near, *turn)
    down_near = reach(down_t, *first_stage(up_near))
    up_near.update(forward_far(up_near))
    up_pieces = [line_of(up_near, line) for line in range(lines)]
    middle, normed_two, normed_two_t = done(
        second_norm(
            ordered(inputs),
            [f[4] for f in forward],
            row_of(out_bias),
            row_of(second_gain),
            row_of(second_shift),
            meta,
            places,
        ),
        0,
    )
    units = []
    for line in range(lines):
        bias = [small_all[y][:, 2 * part_width :] for y in members(line)]
        bias = jnp.concatenate(bias, axis=1)
        units.append(done(up(ordered(normed_two), up_pieces[line], bias, steps), 0))

    plan = bundle_plan(groups, halves)
    block_width = 4 * head_part

    def grads_of(lefts, rights):
        lefts = [ordered(lefts[0])] + lefts[1:]
        mine, other = weight_grads(plan, lefts, rights, groups, halves)
        turn[:] = [mine["own"]]
        return mine, {name: core(value) for name, value in other.items()}

    def both(pair, name):
        return pair[0][name].astype(F32) + pair[1][name].astype(F32)

    def cut(array, k):
        return array[:, k * block_width : (k + 1) * block_width].astype(F32)

    def send_first(pair):
        for_x = both(pair, "x").astype(BF)
        for_y = {}
        if halves > 1:
            for_y = {y: both(pair, ("y", y)).astype(BF) for y in range(1, groups)}
        from_x = over_x(for_x)
        from_y = {y: over_y[y](value) for y, value in for_y.items()}
        turn.extend([for_x, *for_y.values()])
        return from_x, from_y

    def send_second(pair, got):
        from_x = ordered(got[0])
        from_y = {y: ordered(value) for y, value in got[1].items()}
        far = None
        if halves > 1:
            far = both(pair, "far")
            for y in range(1, groups):
                far = far + cut(from_y[y], 1)
            far = far.astype(BF)
        near = [(both(pair, ("keep", y)) + cut(from_x, y)).astype(BF) for y in range(1, groups)]
        late = [over_y[y](near[y - 1]) for y in range(1, groups)]
        far_late = over_x(far) if halves > 1 else None
        turn.extend(near + ([far] if halves > 1 else []))
        return from_x, from_y, late, far_late

    copy_index = lax.axis_index("dp")
    masks = [1 << k for k in range(copies.bit_length() - 1)]
    bits = [(copy_index // mask) % 2 for mask in masks]

    def total_of(pair, got):
        from_x, from_y, late, far_late = got
        late = [ordered(value) for value in late]
        own = both(pair, "own")
        totals = [own[:, h * block_width : (h + 1) * block_width] for h in range(halves)]
        totals[0] = totals[0] + cut(from_x, 0)
        for y in range(1, groups):
            totals[0] = totals[0] + late[y - 1].astype(F32)
            if halves > 1:
                totals[1] = totals[1] + cut(from_y[y], 0)
        if halves > 1:
            totals[1] = totals[1] + ordered(far_late).astype(F32)
        else:
            middle = block_width // 2
            totals = [totals[0][:, :middle], totals[0][:, middle:]]
        low, high = (t.astype(BF) for t in totals)
        away = jnp.where(bits[0] == 1, low, high)
        kept = jnp.where(bits[0] == 1, high, low)
        turn.extend([away, kept])
        return kept, swap("dp", masks[0])(away)

    def halve(state, k):
        kept, came = state
        value = kept.astype(F32) + ordered(came).astype(F32)
        half = value.shape[0] // 2
        away = lax.dynamic_slice_in_dim(value, (1 - bits[k]) * half, half, 0).astype(BF)
        kept = lax.dynamic_slice_in_dim(value, bits[k] * half, half, 0).astype(BF)
        turn.extend([away, kept])
        return kept, swap("dp", masks[k])(away)

    def join(state, k):
        kept, came = state
        came = ordered(came)
        if k == len(masks) - 1:
            value = (kept.astype(F32) + came.astype(F32)).astype(BF)
        else:
            value = jnp.where(
                bits[k + 1] == 1,
                jnp.concatenate([came, kept], axis=0),
                jnp.concatenate([kept, came], axis=0),
            )
        turn.extend([value])
        return value, swap("dp", masks[k])(value)

    def last_join(state):
        value, came = state
        low = jnp.where(bits[0] == 1, came, value)
        high = jnp.where(bits[0] == 1, value, came)
        return jnp.concatenate([low, high], axis=1).astype(F32)

    def steps_of(pair):
        state = total_of(*pair)
        yield
        for k in range(1, len(masks)):
            state = halve(state, k)
            yield
        for k in reversed(range(len(masks))):
            state = join(state, k)
            yield
        yield last_join(state)

    down_pair = grads_of([low_t], [[u[0]] for u in units])
    down_near = held(down_near, *turn)
    down_near.update(forward_far(down_near))
    down_pieces = [line_of(down_near, line) for line in range(lines)]
    down_got = send_first(down_pair)

    back = []
    for line in range(lines):
        hidden, slope = units[line]
        pieces = up_pieces[line], down_pieces[line]
        back.append(done(mlp_back(ordered(low), hidden, slope, *pieces, steps), 0))
    grad_middle, grad_middle_low, grad_middle_t, second_sums = done(
        second_norm_back(
            ordered(middle), [b[3] for b in back], low, row_of(second_gain), meta, places
        ),
        0,
    )
    down_got = send_second(down_pair, down_got)
    grads = [None] * lines

    def back_of(line):
        qkv, _, probs, inverses, _ = forward[line]
        grads[line] = done(
            attend_back(
                ordered(grad_middle_low), attn_pieces[line], qkv, probs, inverses, steps
            ),
            0,
        )

    back_of(lines - 1)
    down_steps = steps_of((down_pair, down_got))
    next(down_steps)
    up_pair = grads_of([normed_two_t], [[b[0]] for b in back])
    up_got = send_first(up_pair)
    next(down_steps)
    for line in reversed(range(lines - 1)):
        back_of(line)
    up_got = send_second(up_pair, up_got)
    next(down_steps)
    attn_pair = grads_of(
        [normed_one_t, grad_middle_t],
        [[grads[line][0], forward[line][1]] for line in range(lines)],
    )
    attn_got = send_first(attn_pair)
    up_steps_left = steps_of((up_pair, up_got))
    next(up_steps_left)
    next(down_steps)
    output, input_grad, first_sums = done(
        finish(
            ordered(inputs),
            middle,
            [b[2] for b in back],
            grad_middle,
            [g[2] for g in grads],
            keep,
            row_of(first_gain),
            row_of(down_bias),
            meta,
            places,
        ),
        0,
    )
    next(up_steps_left)
    attn_got = send_second(attn_pair, attn_got)
    next(up_steps_left)
    attn_steps = steps_of((attn_pair, attn_got))
    next(attn_steps)
    *_, down_total = down_steps
    *_, up_total = up_steps_left
    *_, attn_total = attn_steps

    def in_order(values):
        stacked = jnp.stack(values)
        index = jnp.bitwise_xor(member, jnp.arange(groups, dtype=jnp.int32))
        return jnp.take(stacked, index, axis=0)

    unit_sums = jnp.concatenate([b[1] for b in back], axis=1).reshape(groups, -1)
    unit_sums = in_order(list(unit_sums))
    head_sums = jnp.concatenate([g[1] for g in grads], axis=1)
    head_sums = in_order(list(head_sums.reshape(groups, halves, 3, head_part)))
    query_sums = head_sums[:, :, 0].reshape(-1)
    value_sums = head_sums[:, :, 2].reshape(-1)
    vector = jnp.concatenate(
        [
            second_sums.reshape(-1),
            first_sums.reshape(-1),
            unit_sums.reshape(-1),
            query_sums,
            value_sums,
        ]
    ).reshape(-1, LANES)
    for axis, size in (("narrow", places), ("wide", groups), ("dp", copies)):
        mask = 1
        while mask < size:
            vector = vector + swap(axis, mask)(vector)
            mask *= 2
    vector = vector.reshape(-1)
    piece = lambda k: vector[k * width : (k + 1) * width]
    at = 6 * width
    units_all = hidden_width * groups
    line = member * places + place
    share = units_all // (groups * places)
    up_bias_grad = lax.dynamic_slice_in_dim(vector, at + line * share, share)
    at += units_all
    share = width // (groups * places)
    qv_bias_grad = jnp.stack(
        [
            lax.dynamic_slice_in_dim(vector, at + k * width + line * share, share)
            for k in range(2)
        ]
    )

    attn_total = attn_total.reshape(part, halves, 4, head_part)
    qkv_grad = attn_total[:, :, :3].transpose(0, 2, 1, 3).reshape(part, 3, part_width)
    out_grad = attn_total[:, :, 3].reshape(part, part_width).T
    return (
        output,
        input_grad,
        piece(4),
        piece(5),
        qkv_grad,
        qv_bias_grad,
        out_grad,
        piece(2),
        piece(0),
        piece(1),
        up_total,
        up_bias_grad,
        down_total.T,
        piece(3),
    )


def solution(mesh):
    placed = (
        P(("dp", "wide", "narrow"), None),
        P(("dp", "wide", "narrow")),
        P(),
        P(),
        P("narrow", None, "wide"),
        P(None, "wide"),
        P("wide", "narrow"),
        P(),
        P(),
        P(),
        P("narrow", "wide"),
        P("wide"),
        P("wide", "narrow"),
        P(),
        P(("dp", "wide", "narrow"), None),
    )
    return jax.shard_map(
        shards,
        mesh=mesh,
        in_specs=placed,
        out_specs=(
            P(("dp", "wide", "narrow"), None),
            P(("dp", "wide", "narrow"), None),
            P(),
            P(),
            P("narrow", None, "wide"),
            P(None, ("wide", "narrow")),
            P("wide", "narrow"),
            P(),
            P(),
            P(),
            P("narrow", "wide"),
            P(("wide", "narrow")),
            P("wide", "narrow"),
            P(),
        ),
        check_vma=False,
    )
```

time: 772 us -> 453 us (0.59)
  waiting for transfers between devices: 456 us -> 153 us
  Pallas kernels: 0 us -> 156 us
  matrix products: 107 us -> 0 us
  blocking collectives: 79.3 us -> 0 us
  starting transfers between devices: 10.5 us -> 65.3 us
  local copies, waits for them, and re-layouts: 41 us -> 27.7 us
  between operations: 14.8 us -> 2.13 us
  other arithmetic: 52.5 us -> 40.8 us
    all_gather x8 -> x0, waiting for transfers between devices: 215 us -> none  [the longest x1 36.7 us: shards(): lax.all_gather(down_weight, 'narrow', axis=1, tiled=True)]
    psum x1 -> x0, waiting for transfers between devices: 163 us -> none  [shards(): lax.psum(qkv_part.astype(jnp.bfloat16), ('dp', 'narrow'))]
    pallas_call x0 -> x15, Pallas kernels: none -> 156 us  [call(): pl.pallas_call(body, out_shape=[o for _, o in outs], grid_spec=pltpu.Pref...]
    ppermute x0 -> x72, waiting for transfers between devices: none -> 153 us  [swap(): return lambda value: lax.ppermute(value, axis, pairs)]
    dot_general x26 -> x0, matrix products: 107 us -> none  [the longest x1 12.6 us: shards(): jnp.einsum('td,fd->tf', grad_low_all, down_full, preferred_element_type=j...]
    reduce_scatter x4 -> x0, waiting for transfers between devices: 74.8 us -> none  [the longest x1 31 us: shards(): lax.psum_scatter(jnp.dot(row_piece, out_full, preferred_element_type=jnp....]
    psum x2 -> x0, blocking collectives: 74 us -> none  [the longest x1 38.9 us: shards(): lax.psum((first_gain_part, first_shift_part, out_bias_part, second_gain_p...]
    ppermute x0 -> x72, starting transfers between devices: none -> 65.3 us  [swap(): return lambda value: lax.ppermute(value, axis, pairs)]
  transfers between devices with their start and end apart: 13 -> 72, of which waited for: 11 -> 24; matrix products, arithmetic and copies ran while one was open for 14% -> 11% of each run, Pallas kernels for 0% -> 31%
where the time goes in v1:
time: 453 us; the launch traced here: 445 us
  Pallas kernels  156 us (34%)
  waiting for transfers between devices  153 us (34%)
  starting transfers between devices  65.3 us (14%)
  other arithmetic  40.8 us (9%)
  local copies, waits for them, and re-layouts  27.7 us (6%)
    pallas_call x15, Pallas kernels, call(): pl.pallas_call(body, out_shape=[o for _, o in outs], grid_spec=pltpu.Pref...  156 us
    ppermute x72, waiting for transfers between devices, swap(): return lambda value: lax.ppermute(value, axis, pairs)  153 us
    ppermute x72, starting transfers between devices, swap(): return lambda value: lax.ppermute(value, axis, pairs)  65.3 us
  transfers between devices with their start and end apart: 72, of which 24 were waited for; matrix products, arithmetic and copies ran while one was open for 11% of the time, Pallas kernels for 31%

profile of v1, /device:TPU:0, one launch (start us, length us, event | category | flops | bytes accessed | tf_op | source)
XLA Modules:
  0.0 444.9 jit_solution(8083622946120496917)
XLA Ops:
  2.0 2.2 reshape.156
  7.2 3.0 collective-permute-start.1
  13.1 5.4 %first_norm.1 = (bf16[512,1024]{1,0:T(8,128)(2,1)}, bf16[1024,512]{1,0:T(8,128)(2,1)}, bf16[512,1024]{1,0:T(8,128)(2,1)}, bf16[1024,512]{1,0:T(8,128)(2,1)}) custom-call(s32[4]{0:T(128)} %xor_multiply_fusion.meta, bf16[512,1024]{1,0:T(8,128)(2,1)} %x.3, bf16[512,1024]{1,0:T(8,128)(2,1)} %cot.1, f32[512,1]{1,0:T(8,128)} %copy.37.keep, f32[1,1024]{1,0:T(1,128)} %bitcast.75, ...), custom_call_target="tpu_custom_call" | custom-call | bytes 6301712 | tf_op jit(solution)/shard_map/first_norm/pallas_call | solution.py:33
  18.5 14.9 %collective-permute-done.1.refs_2_ = bf16[256,2048]{1,0:T(8,128)(2,1)S(1)} collective-permute-done((bf16[256,2048]{1,0:T(8,128)(2,1)S(1)}, bf16[256,2048]{1,0:T(8,128)(2,1)S(1)}, u32[]{:S(2)}, u32[]{:S(2)}) %collective-permute-start.1) | collective-permute-done | bytes 1048608 | tf_op jit(solution)/shard_map/ppermute | solution.py:666
  33.4 1.8 collective-permute-start.9
  41.4 12.2 %attend.2 = (bf16[512,1536]{1,0:T(8,128)(2,1)}, bf16[512,512]{1,0:T(8,128)(2,1)}, bf16[8,512,512]{2,1,0:T(8,128)(2,1)}, f32[2,4,512]{2,1,0:T(4,128)}, f32[512,1024]{1,0:T(8,128)}) custom-call(bf16[512,1024]{1,0:T(8,128)(2,1)} %get-tuple-element.137.normed, bf16[256,2048]{1,0:T(8,128)(2,1)} %copy-done.6, bf16[256,2048]{1,0:T(8,128)(2,1)} %collective-permute-done.refs_1_, ...), custom_call_target="tpu_custom_call" | custom-call | flops 3221225472 | bytes 13655040 | tf_op jit(solution)/shard_map/attend/pallas_call | solution.py:33
  59.1 12.5 %attend.3 = (bf16[512,1536]{1,0:T(8,128)(2,1)}, bf16[512,512]{1,0:T(8,128)(2,1)}, bf16[8,512,512]{2,1,0:T(8,128)(2,1)}, f32[2,4,512]{2,1,0:T(4,128)}, f32[512,1024]{1,0:T(8,128)}) custom-call(bf16[512,1024]{1,0:T(8,128)(2,1)} %get-tuple-element.137.normed, bf16[256,2048]{1,0:T(8,128)(2,1)} %copy-done.18, bf16[256,2048]{1,0:T(8,128)(2,1)} %copy-done.29, ...), custom_call_target="tpu_custom_call" | custom-call | flops 3221225472 | bytes 13655040 | tf_op jit(solution)/shard_map/attend/pallas_call | solution.py:33
  71.6 7.9 %collective-permute-done.11.refs_2_ = bf16[256,2048]{1,0:T(8,128)(2,1)} collective-permute-done((bf16[256,2048]{1,0:T(8,128)(2,1)}, bf16[256,2048]{1,0:T(8,128)(2,1)}, u32[]{:S(2)}, u32[]{:S(2)}) %collective-permute-start.11) | collective-permute-done | bytes 1048608 | tf_op jit(solution)/shard_map/ppermute | solution.py:666
  82.9 11.2 %collective-permute-done.15.refs_2_ = bf16[256,1024]{1,0:T(8,128)(2,1)} collective-permute-done((bf16[256,1024]{1,0:T(8,128)(2,1)S(1)}, bf16[256,1024]{1,0:T(8,128)(2,1)}, u32[]{:S(2)}, u32[]{:S(2)}) %collective-permute-start.15) | collective-permute-done | bytes 524320 | tf_op jit(solution)/shard_map/ppermute | solution.py:666
  98.8 6.1 %second_norm.1 = (f32[512,1024]{1,0:T(8,128)}, bf16[512,1024]{1,0:T(8,128)(2,1)}, bf16[1024,512]{1,0:T(8,128)(2,1)}) custom-call(s32[4]{0:T(128)} %xor_multiply_fusion.meta, bf16[512,1024]{1,0:T(8,128)(2,1)} %x.3, f32[512,1024]{1,0:T(8,128)} %get-tuple-element.144.refs_0_, f32[512,1024]{1,0:T(8,128)} %get-tuple-element.145.refs_1_, f32[1,1024]{1,0:T(1,128)} %bitcast.78, ...), custom_call_target="tpu_custom_call" | custom-call | bytes 9449488 | tf_op jit(solution)/shard_map/second_norm/pallas_call | solution.py:33
  106.9 7.6 %up.2 = (bf16[512,2048]{1,0:T(8,128)(2,1)}, bf16[512,2048]{1,0:T(8,128)(2,1)}) custom-call(bf16[512,1024]{1,0:T(8,128)(2,1)} %get-tuple-element.154.normed, bf16[256,2048]{1,0:T(8,128)(2,1)} %refs_0_.3, bf16[256,2048]{1,0:T(8,128)(2,1)} %collective-permute-done.10.refs_1_, bf16[256,2048]{1,0:T(8,128)(2,1)} %collective-permute-done.11.refs_2_, ...), custom_call_target="tpu_custom_call" | custom-call | flops 2147483648 | bytes 9441280 | tf_op jit(solution)/shard_map/up/pallas_call | solution.py:33
  115.5 7.8 %up.3 = (bf16[512,2048]{1,0:T(8,128)(2,1)}, bf16[512,2048]{1,0:T(8,128)(2,1)}) custom-call(bf16[512,1024]{1,0:T(8,128)(2,1)} %get-tuple-element.154.normed, bf16[256,2048]{1,0:T(8,128)(2,1)} %copy-done.19, bf16[256,2048]{1,0:T(8,128)(2,1)} %copy-done.30, bf16[256,1024]{1,0:T(8,128)(2,1)} %collective-permute-done.15.refs_2_, ...), custom_call_target="tpu_custom_call" | custom-call | flops 2147483648 | bytes 9441280 | tf_op jit(solution)/shard_map/up/pallas_call | solution.py:33
  123.3 10.5 %weight_grads.3 = (bf16[256,2048]{1,0:T(8,128)(2,1)}, bf16[256,2048]{1,0:T(8,128)(2,1)}, bf16[256,1024]{1,0:T(8,128)(2,1)}, bf16[256,1024]{1,0:T(8,128)(2,1)}, b...) custom-call(bf16[1024,512]{1,0:T(8,128)(2,1)} %get-tuple-element.157, ...), custom_call_target="tpu_custom_call" | custom-call | flops 4294967296 | bytes 13631488 | tf_op jit(solution)/shard_map/weight_grads/pallas_call | solution.py:33
  139.6 11.6 %collective-permute-done.26.refs_8_ = bf16[256,1024]{1,0:T(8,128)(2,1)} collective-permute-done((bf16[256,1024]{1,0:T(8,128)(2,1)S(1)}, bf16[256,1024]{1,0:T(8,128)(2,1)}, u32[]{:S(2)}, u32[]{:S(2)}) %collective-permute-start.26) | collective-permute-done | bytes 524320 | tf_op jit(solution)/shard_map/ppermute | solution.py:666
  155.5 13.7 %mlp_back.2 = (bf16[512,2048]{1,0:T(8,128)(2,1)}, f32[1,2048]{1,0:T(1,128)}, f32[512,1024]{1,0:T(8,128)}, f32[512,1024]{1,0:T(8,128)}) custom-call(bf16[512,1024]{1,0:T(8,128)(2,1)} %get-tuple-element.168.low, bf16[512,2048]{1,0:T(8,128)(2,1)} %get-tuple-element.153.refs_1_.hidden, bf16[512,2048]{1,0:T(8,128)(2,1)} %get-tuple-element.164.slope, ...), custom_call_target="tpu_custom_call" | custom-call | flops 6442450944 | bytes 19931136 | tf_op jit(solution)/shard_map/mlp_back/pallas_call | solution.py:33
  170.0 13.9 %mlp_back.3 = (bf16[512,2048]{1,0:T(8,128)(2,1)}, f32[1,2048]{1,0:T(1,128)}, f32[512,1024]{1,0:T(8,128)}, f32[512,1024]{1,0:T(8,128)}) custom-call(bf16[512,1024]{1,0:T(8,128)(2,1)} %get-tuple-element.168.low, bf16[512,2048]{1,0:T(8,128)(2,1)} %get-tuple-element.156.refs_2_.hidden, bf16[512,2048]{1,0:T(8,128)(2,1)} %get-tuple-element.169.slope, ...), custom_call_target="tpu_custom_call" | custom-call | flops 6442450944 | bytes 19931136 | tf_op jit(solution)/shard_map/mlp_back/pallas_call | solution.py:33
  183.9 7.2 %second_norm_back.1 = (f32[512,1024]{1,0:T(8,128)}, bf16[512,1024]{1,0:T(8,128)(2,1)}, bf16[1024,512]{1,0:T(8,128)(2,1)}, f32[4,1024]{1,0:T(4,128)}) custom-call(s32[4]{0:T(128)} %xor_multiply_fusion.meta, f32[512,1024]{1,0:T(8,128)} %get-tuple-element.172.middle, bf16[512,1024]{1,0:T(8,128)(2,1)} %get-tuple-element.168.low, ...), custom_call_target="tpu_custom_call" | custom-call | bytes 11554832 | tf_op jit(solution)/shard_map/second_norm_back/pallas_call | solution.py:33
  191.2 2.2 add_convert_fusion.10
  193.9 2.1 add_convert_fusion.11
  198.6 15.1 %attend_back.2 = (bf16[512,1536]{1,0:T(8,128)(2,1)}, f32[1,1536]{1,0:T(1,128)}, f32[512,1024]{1,0:T(8,128)}) custom-call(bf16[512,1024]{1,0:T(8,128)(2,1)} %get-tuple-element.199.grad_low, bf16[256,2048]{1,0:T(8,128)(2,1)} %copy-done.18, bf16[256,2048]{1,0:T(8,128)(2,1)} %copy-done.29, bf16[256,1024]{1,0:T(8,128)(2,1)} %collective-permute-done.5.refs_2_, ...), custom_call_target="tpu_custom_call" | custom-call | flops 3221225472 | bytes 14702592 | tf_op jit(solution)/shard_map/attend_back/pallas_call | solution.py:33
  216.3 10.1 %weight_grads.4 = (bf16[256,2048]{1,0:T(8,128)(2,1)}, bf16[256,2048]{1,0:T(8,128)(2,1)}, bf16[256,1024]{1,0:T(8,128)(2,1)}, bf16[256,1024]{1,0:T(8,128)(2,1)}, b...) custom-call(bf16[1024,512]{1,0:T(8,128)(2,1)} %get-tuple-element.192, ...), custom_call_target="tpu_custom_call" | custom-call | flops 4294967296 | bytes 13631488 | tf_op jit(solution)/shard_map/weight_grads/pallas_call | solution.py:33
  229.9 2.6 add_convert_fusion.3
  237.4 4.9 %collective-permute-done.39 = bf16[256,1024]{1,0:T(8,128)(2,1)S(1)} collective-permute-done((bf16[256,1024]{1,0:T(8,128)(2,1)}, bf16[256,1024]{1,0:T(8,128)(2,1)S(1)}, u32[]{:S(2)}, u32[]{:S(2)}) %collective-permute-start.39) | collective-permute-done | bytes 524320 | tf_op jit(solution)/shard_map/ppermute | solution.py:666
  242.6 15.0 %attend_back.3 = (bf16[512,1536]{1,0:T(8,128)(2,1)}, f32[1,1536]{1,0:T(1,128)}, f32[512,1024]{1,0:T(8,128)}) custom-call(bf16[512,1024]{1,0:T(8,128)(2,1)} %get-tuple-element.199.grad_low, bf16[256,2048]{1,0:T(8,128)(2,1)} %copy-done.6, bf16[256,2048]{1,0:T(8,128)(2,1)} %collective-permute-done.refs_1_, bf16[256,2048]{1,0:T(8,128)(2,1)} %copy-done.17, ...), custom_call_target="tpu_custom_call" | custom-call | flops 3221225472 | bytes 14702592 | tf_op jit(solution)/shard_map/attend_back/pallas_call | solution.py:33
  258.5 2.6 collective-permute-start.44
  261.1 2.9 add_convert_fusion.9
  264.0 2.1 add_convert_fusion.8
  266.1 7.7 %collective-permute-done.44 = bf16[128,1024]{1,0:T(8,128)(2,1)S(1)} collective-permute-done((bf16[128,1024]{1,0:T(8,128)(2,1)S(1)}, bf16[128,1024]{1,0:T(8,128)(2,1)S(1)}, u32[]{:S(2)}, u32[]{:S(2)}) %collective-permute-start.44) | collective-permute-done | bytes 262176 | tf_op jit(solution)/shard_map/ppermute | solution.py:666
  273.8 10.6 %weight_grads.5 = (bf16[256,2048]{1,0:T(8,128)(2,1)}, bf16[256,2048]{1,0:T(8,128)(2,1)}, bf16[256,1024]{1,0:T(8,128)(2,1)}, bf16[256,1024]{1,0:T(8,128)(2,1)}, b...) custom-call(bf16[1024,512]{1,0:T(8,128)(2,1)} %get-tuple-element.211, ...), custom_call_target="tpu_custom_call" | custom-call | flops 4294967296 | bytes 14680064 | tf_op jit(solution)/shard_map/weight_grads/pallas_call | solution.py:33
  290.9 10.7 %collective-permute-done.49 = bf16[256,1024]{1,0:T(8,128)(2,1)S(1)} collective-permute-done((bf16[256,1024]{1,0:T(8,128)(2,1)}, bf16[256,1024]{1,0:T(8,128)(2,1)S(1)}, u32[]{:S(2)}, u32[]{:S(2)}) %collective-permute-start.49) | collective-permute-done | bytes 524320 | tf_op jit(solution)/shard_map/ppermute | solution.py:666
  305.4 8.6 %finish.1 = (bf16[512,1024]{1,0:T(8,128)(2,1)}, bf16[512,1024]{1,0:T(8,128)(2,1)}, f32[2,1024]{1,0:T(2,128)}) custom-call(s32[4]{0:T(128)} %xor_multiply_fusion.meta, bf16[512,1024]{1,0:T(8,128)(2,1)} %x.3, f32[512,1024]{1,0:T(8,128)} %get-tuple-element.172.middle, f32[512,1024]{1,0:T(8,128)} %get-tuple-element.177.grad, f32[512,1]{1,0:T(8,128)} %copy.37.keep, ...), custom_call_target="tpu_custom_call" | custom-call | bytes 15747088 | tf_op jit(solution)/shard_map/finish/pallas_call | solution.py:33
  318.7 23.9 %collective-permute-done.52 = f32[96,128]{1,0:T(8,128)S(1)} collective-permute-done((f32[96,128]{1,0:T(8,128)S(1)}, f32[96,128]{1,0:T(8,128)S(1)}, u32[]{:S(2)}, u32[]{:S(2)}) %collective-permute-start.52) | collective-permute-done | bytes 49184 | tf_op jit(solution)/shard_map/ppermute | solution.py:666
  343.6 3.1 collective-permute-done.53
  348.1 2.8 collective-permute-done.54
  354.2 2.4 collective-permute-start.55
  363.2 4.3 collective-permute-done.55
  367.6 4.7 %collective-permute-done.63 = bf16[128,1024]{1,0:T(8,128)(2,1)S(1)} collective-permute-done((bf16[128,1024]{1,0:T(8,128)(2,1)S(1)}, bf16[128,1024]{1,0:T(8,128)(2,1)S(1)}, u32[]{:S(2)}, u32[]{:S(2)}) %collective-permute-start.63) | collective-permute-done | bytes 262176 | tf_op jit(solution)/shard_map/ppermute | solution.py:666
  372.3 3.4 collective-permute-start.66
  380.9 6.7 %collective-permute-done.66 = bf16[128,1024]{1,0:T(8,128)(2,1)S(1)} collective-permute-done((bf16[128,1024]{1,0:T(8,128)(2,1)S(1)}, bf16[128,1024]{1,0:T(8,128)(2,1)S(1)}, u32[]{:S(2)}, u32[]{:S(2)}) %collective-permute-start.66) | collective-permute-done | bytes 262176 | tf_op jit(solution)/shard_map/ppermute | solution.py:666
  387.7 5.4 %collective-permute-done.65 = bf16[256,1024]{1,0:T(8,128)(2,1)S(1)} collective-permute-done((bf16[256,1024]{1,0:T(8,128)(2,1)S(1)}, bf16[256,1024]{1,0:T(8,128)(2,1)S(1)}, u32[]{:S(2)}, u32[]{:S(2)}) %collective-permute-start.65) | collective-permute-done | bytes 524320 | tf_op jit(solution)/shard_map/ppermute | solution.py:666
  393.4 4.5 %collective-permute-start.67 = (bf16[128,1024]{1,0:T(8,128)(2,1)S(1)}, bf16[128,1024]{1,0:T(8,128)(2,1)S(1)}, u32[]{:S(2)}, u32[]{:S(2)}) collective-permute-start(bf16[128,1024]{1,0:T(8,128)(2,1)S(1)} %get-tuple-element.294), channel_id=1, source_target_pairs={{0,16},{8,24},{16,0},{24,8},{1,17},{9,25},{17,1},{25,9},{2,18},{10... | collective-permute-start | bytes 786440 | tf_op jit(solution)/shard_map/ppermute | solution.py:666
  398.0 2.5 collective-permute-start.70
  400.6 8.3 %collective-permute-done.67 = bf16[128,1024]{1,0:T(8,128)(2,1)S(1)} collective-permute-done((bf16[128,1024]{1,0:T(8,128)(2,1)S(1)}, bf16[128,1024]{1,0:T(8,128)(2,1)S(1)}, u32[]{:S(2)}, u32[]{:S(2)}) %collective-permute-start.67) | collective-permute-done | bytes 262176 | tf_op jit(solution)/shard_map/ppermute | solution.py:666
  409.2 1.8 copy.50
  411.1 8.3 %collective-permute-done.68 = bf16[128,1024]{1,0:T(8,128)(2,1)} collective-permute-done((bf16[128,1024]{1,0:T(8,128)(2,1)S(1)}, bf16[128,1024]{1,0:T(8,128)(2,1)}, u32[]{:S(2)}, u32[]{:S(2)}) %collective-permute-start.68) | collective-permute-done | bytes 262176 | tf_op jit(solution)/shard_map/ppermute | solution.py:666
  420.5 5.0 %collective-permute-start.69 = (bf16[256,1024]{1,0:T(8,128)(2,1)S(1)}, bf16[256,1024]{1,0:T(8,128)(2,1)S(1)}, u32[]{:S(2)}, u32[]{:S(2)}) collective-permute-start(bf16[256,1024]{1,0:T(8,128)(2,1)S(1)} %maximum_select_fusion.2), channel_id=1, source_target_pairs={{0,8},{8,0},{16,24},{24,16},{1,9},{9,1},{17,25},{25,17},{2,10},{10... | collective-permute-start | bytes 1572872 | tf_op jit(solution)/shard_map/ppermute | solution.py:666
  427.1 10.1 %collective-permute-done.69 = bf16[256,1024]{1,0:T(8,128)(2,1)S(1)} collective-permute-done((bf16[256,1024]{1,0:T(8,128)(2,1)S(1)}, bf16[256,1024]{1,0:T(8,128)(2,1)S(1)}, u32[]{:S(2)}, u32[]{:S(2)}) %collective-permute-start.69) | collective-permute-done | bytes 524320 | tf_op jit(solution)/shard_map/ppermute | solution.py:666
  441.0 2.4 reshape.178
  (284 shorter events, 96.6 us)
Async XLA Ops:
  7.2 26.2 %collective-permute-start.1 = (bf16[256,2048]{1,0:T(8,128)(2,1)S(1)}, bf16[256,2048]{1,0:T(8,128)(2,1)S(1)}, u32[]{:S(2)}, u32[]{:S(2)}) collective-permute-start(bf16[256,2048]{1,0:T(8,128)(2,1)S(1)} %reshape.158.refs_0_), channel_id=1, source_target_pairs={{0,2},{1,3},{2,0},{3,1},{4,6},{5,7},{6,4},{7,5},{8,10},{9,11},{10,... | collective-permute-start | bytes 3145736 | tf_op jit(solution)/shard_map/ppermute | solution.py:666
  10.2 31.1 %collective-permute-start = (bf16[256,2048]{1,0:T(8,128)(2,1)S(1)}, bf16[256,2048]{1,0:T(8,128)(2,1)}, u32[]{:S(2)}, u32[]{:S(2)}) collective-permute-start(bf16[256,2048]{1,0:T(8,128)(2,1)S(1)} %reshape.158.refs_0_), channel_id=1, source_target_pairs={{0,1},{1,0},{2,3},{3,2},{4,5},{5,4},{6,7},{7,6},{8,9},{9,8},{10,11... | collective-permute-start | bytes 3145736 | tf_op jit(solution)/shard_map/ppermute | solution.py:666
  10.2 27.7 %collective-permute-start.3 = (bf16[256,2048]{1,0:T(8,128)(2,1)S(1)}, bf16[256,2048]{1,0:T(8,128)(2,1)S(1)}, u32[]{:S(2)}, u32[]{:S(2)}) collective-permute-start(bf16[256,2048]{1,0:T(8,128)(2,1)S(1)} %reshape.158.refs_0_), channel_id=1, source_target_pairs={{0,4},{4,0},{1,5},{5,1},{2,6},{6,2},{3,7},{7,3},{8,12},{12,8},{9,1... | collective-permute-start | bytes 3145736 | tf_op jit(solution)/shard_map/ppermute | solution.py:666
  38.0 16.5 %collective-permute-start.5 = (bf16[256,1024]{1,0:T(8,128)(2,1)S(1)}, bf16[256,1024]{1,0:T(8,128)(2,1)}, u32[]{:S(2)}, u32[]{:S(2)}) collective-permute-start(bf16[256,1024]{1,0:T(8,128)(2,1)S(1)} %slice.144), channel_id=1, source_target_pairs={{0,2},{1,3},{2,0},{3,1},{4,6},{5,7},{6,4},{7,5},{8,10},{9,11},{10,... | collective-permute-start | bytes 1572872 | tf_op jit(solution)/shard_map/ppermute | solution.py:666
  39.8 14.7 %collective-permute-start.6 = (bf16[256,1024]{1,0:T(8,128)(2,1)S(1)}, bf16[256,1024]{1,0:T(8,128)(2,1)}, u32[]{:S(2)}, u32[]{:S(2)}) collective-permute-start(bf16[256,1024]{1,0:T(8,128)(2,1)S(1)} %slice.145), channel_id=1, source_target_pairs={{0,4},{4,0},{1,5},{5,1},{2,6},{6,2},{3,7},{7,3},{8,12},{12,8},{9,1... | collective-permute-start | bytes 1572872 | tf_op jit(solution)/shard_map/ppermute | solution.py:666
  53.6 25.9 %collective-permute-start.11 = (bf16[256,2048]{1,0:T(8,128)(2,1)}, bf16[256,2048]{1,0:T(8,128)(2,1)}, u32[]{:S(2)}, u32[]{:S(2)}) collective-permute-start(bf16[256,2048]{1,0:T(8,128)(2,1)} %refs_0_.3), channel_id=1, source_target_pairs={{0,2},{1,3},{2,0},{3,1},{4,6},{5,7},{6,4},{7,5},{8,10},{9,11},{10,... | collective-permute-start | bytes 3145736 | tf_op jit(solution)/shard_map/ppermute | solution.py:666
  54.2 25.4 %collective-permute-start.13 = (bf16[256,2048]{1,0:T(8,128)(2,1)}, bf16[256,2048]{1,0:T(8,128)(2,1)S(1)}, u32[]{:S(2)}, u32[]{:S(2)}) collective-permute-start(bf16[256,2048]{1,0:T(8,128)(2,1)} %refs_0_.3), channel_id=1, source_target_pairs={{0,4},{4,0},{1,5},{5,1},{2,6},{6,2},{3,7},{7,3},{8,12},{12,8},{9,1... | collective-permute-start | bytes 3145736 | tf_op jit(solution)/shard_map/ppermute | solution.py:666
  57.4 47.5 %collective-permute-start.10 = (bf16[256,2048]{1,0:T(8,128)(2,1)}, bf16[256,2048]{1,0:T(8,128)(2,1)}, u32[]{:S(2)}, u32[]{:S(2)}) collective-permute-start(bf16[256,2048]{1,0:T(8,128)(2,1)} %refs_0_.3), channel_id=1, source_target_pairs={{0,1},{1,0},{2,3},{3,2},{4,5},{5,4},{6,7},{7,6},{8,9},{9,8},{10,11... | collective-permute-start | bytes 3145736 | tf_op jit(solution)/shard_map/ppermute | solution.py:666
  79.5 26.9 %collective-permute-start.12 = (bf16[256,2048]{1,0:T(8,128)(2,1)}, bf16[256,2048]{1,0:T(8,128)(2,1)}, u32[]{:S(2)}, u32[]{:S(2)}) collective-permute-start(bf16[256,2048]{1,0:T(8,128)(2,1)} %collective-permute-done.11.refs_2_), channel_id=1, source_target_pairs={{0,1},{1,0},{2,3},{3,2},{4,5},{5,4},{6,7},{7,6},{8,9},{9,8},{10,11... | collective-permute-start | bytes 3145736 | tf_op jit(solution)/shard_map/ppermute | solution.py:666
  79.7 14.4 %collective-permute-start.15 = (bf16[256,1024]{1,0:T(8,128)(2,1)S(1)}, bf16[256,1024]{1,0:T(8,128)(2,1)}, u32[]{:S(2)}, u32[]{:S(2)}) collective-permute-start(bf16[256,1024]{1,0:T(8,128)(2,1)S(1)} %slice.149), channel_id=1, source_target_pairs={{0,2},{1,3},{2,0},{3,1},{4,6},{5,7},{6,4},{7,5},{8,10},{9,11},{10,... | collective-permute-start | bytes 1572872 | tf_op jit(solution)/shard_map/ppermute | solution.py:666
  82.9 31.6 %collective-permute-start.14 = (bf16[256,2048]{1,0:T(8,128)(2,1)S(1)}, bf16[256,2048]{1,0:T(8,128)(2,1)S(1)}, u32[]{:S(2)}, u32[]{:S(2)}) collective-permute-start(bf16[256,2048]{1,0:T(8,128)(2,1)S(1)} %collective-permute-done.13.refs_0_), channel_id=1, source_target_pairs={{0,1},{1,0},{2,3},{3,2},{4,5},{5,4},{6,7},{7,6},{8,9},{9,8},{10,11... | collective-permute-start | bytes 3145736 | tf_op jit(solution)/shard_map/ppermute | solution.py:666
  94.1 20.4 %collective-permute-start.17 = (bf16[256,1024]{1,0:T(8,128)(2,1)}, bf16[256,1024]{1,0:T(8,128)(2,1)}, u32[]{:S(2)}, u32[]{:S(2)}) collective-permute-start(bf16[256,1024]{1,0:T(8,128)(2,1)} %collective-permute-done.15.refs_2_), channel_id=1, source_target_pairs={{0,1},{1,0},{2,3},{3,2},{4,5},{5,4},{6,7},{7,6},{8,9},{9,8},{10,11... | collective-permute-start | bytes 1572872 | tf_op jit(solution)/shard_map/ppermute | solution.py:666
  95.5 19.0 %collective-permute-start.18 = (bf16[256,1024]{1,0:T(8,128)(2,1)}, bf16[256,1024]{1,0:T(8,128)(2,1)}, u32[]{:S(2)}, u32[]{:S(2)}) collective-permute-start(bf16[256,1024]{1,0:T(8,128)(2,1)} %collective-permute-done.16.refs_3_), channel_id=1, source_target_pairs={{0,1},{1,0},{2,3},{3,2},{4,5},{5,4},{6,7},{7,6},{8,9},{9,8},{10,11... | collective-permute-start | bytes 1572872 | tf_op jit(solution)/shard_map/ppermute | solution.py:666
  104.8 29.6 %collective-permute-start.22 = (bf16[256,2048]{1,0:T(8,128)(2,1)}, bf16[256,2048]{1,0:T(8,128)(2,1)}, u32[]{:S(2)}, u32[]{:S(2)}) collective-permute-start(bf16[256,2048]{1,0:T(8,128)(2,1)} %bitcast.15.refs_4_), channel_id=1, source_target_pairs={{0,2},{1,3},{2,0},{3,1},{4,6},{5,7},{6,4},{7,5},{8,10},{9,11},{10,... | collective-permute-start | bytes 3145736 | tf_op jit(solution)/shard_map/ppermute | solution.py:666
  106.4 29.6 %collective-permute-start.24 = (bf16[256,2048]{1,0:T(8,128)(2,1)}, bf16[256,2048]{1,0:T(8,128)(2,1)}, u32[]{:S(2)}, u32[]{:S(2)}) collective-permute-start(bf16[256,2048]{1,0:T(8,128)(2,1)} %bitcast.15.refs_4_), channel_id=1, source_target_pairs={{0,4},{4,0},{1,5},{5,1},{2,6},{6,2},{3,7},{7,3},{8,12},{12,8},{9,1... | collective-permute-start | bytes 3145736 | tf_op jit(solution)/shard_map/ppermute | solution.py:666
  133.9 17.9 %collective-permute-start.20 = (bf16[256,2048]{1,0:T(8,128)(2,1)}, bf16[256,2048]{1,0:T(8,128)(2,1)S(1)}, u32[]{:S(2)}, u32[]{:S(2)}) collective-permute-start(bf16[256,2048]{1,0:T(8,128)(2,1)} %get-tuple-element.162), channel_id=1, source_target_pairs={{0,1},{1,0},{2,3},{3,2},{4,5},{5,4},{6,7},{7,6},{8,9},{9,8},{10,11... | collective-permute-start | bytes 3145736 | tf_op jit(solution)/shard_map/ppermute | solution.py:666
  134.3 18.0 %collective-permute-start.21 = (bf16[256,2048]{1,0:T(8,128)(2,1)}, bf16[256,2048]{1,0:T(8,128)(2,1)}, u32[]{:S(2)}, u32[]{:S(2)}) collective-permute-start(bf16[256,2048]{1,0:T(8,128)(2,1)} %bitcast.15.refs_4_), channel_id=1, source_target_pairs={{0,1},{1,0},{2,3},{3,2},{4,5},{5,4},{6,7},{7,6},{8,9},{9,8},{10,11... | collective-permute-start | bytes 3145736 | tf_op jit(solution)/shard_map/ppermute | solution.py:666
  134.4 19.5 %collective-permute-start.23 = (bf16[256,2048]{1,0:T(8,128)(2,1)}, bf16[256,2048]{1,0:T(8,128)(2,1)S(1)}, u32[]{:S(2)}, u32[]{:S(2)}) collective-permute-start(bf16[256,2048]{1,0:T(8,128)(2,1)} %collective-permute-done.22.refs_6_), channel_id=1, source_target_pairs={{0,1},{1,0},{2,3},{3,2},{4,5},{5,4},{6,7},{7,6},{8,9},{9,8},{10,11... | collective-permute-start | bytes 3145736 | tf_op jit(solution)/shard_map/ppermute | solution.py:666
  151.2 18.6 %collective-permute-start.25 = (bf16[256,2048]{1,0:T(8,128)(2,1)}, bf16[256,2048]{1,0:T(8,128)(2,1)}, u32[]{:S(2)}, u32[]{:S(2)}) collective-permute-start(bf16[256,2048]{1,0:T(8,128)(2,1)} %collective-permute-done.24.refs_6_), channel_id=1, source_target_pairs={{0,1},{1,0},{2,3},{3,2},{4,5},{5,4},{6,7},{7,6},{8,9},{9,8},{10,11... | collective-permute-start | bytes 3145736 | tf_op jit(solution)/shard_map/ppermute | solution.py:666
  151.5 17.8 %collective-permute-start.28 = (bf16[256,1024]{1,0:T(8,128)(2,1)}, bf16[256,1024]{1,0:T(8,128)(2,1)S(1)}, u32[]{:S(2)}, u32[]{:S(2)}) collective-permute-start(bf16[256,1024]{1,0:T(8,128)(2,1)} %collective-permute-done.26.refs_8_), channel_id=1, source_target_pairs={{0,1},{1,0},{2,3},{3,2},{4,5},{5,4},{6,7},{7,6},{8,9},{9,8},{10,11... | collective-permute-start | bytes 1572872 | tf_op jit(solution)/shard_map/ppermute | solution.py:666
  151.7 17.6 %collective-permute-start.29 = (bf16[256,1024]{1,0:T(8,128)(2,1)}, bf16[256,1024]{1,0:T(8,128)(2,1)}, u32[]{:S(2)}, u32[]{:S(2)}) collective-permute-start(bf16[256,1024]{1,0:T(8,128)(2,1)} %collective-permute-done.27.refs_9_), channel_id=1, source_target_pairs={{0,1},{1,0},{2,3},{3,2},{4,5},{5,4},{6,7},{7,6},{8,9},{9,8},{10,11... | collective-permute-start | bytes 1572872 | tf_op jit(solution)/shard_map/ppermute | solution.py:666
  152.4 38.7 %collective-permute-start.31 = (bf16[256,2048]{1,0:T(8,128)(2,1)S(1)}, bf16[256,2048]{1,0:T(8,128)(2,1)S(1)}, u32[]{:S(2)}, u32[]{:S(2)}) collective-permute-start(bf16[256,2048]{1,0:T(8,128)(2,1)S(1)} %add_convert_fusion.5), channel_id=1, source_target_pairs={{0,2},{1,3},{2,0},{3,1},{4,6},{5,7},{6,4},{7,5},{8,10},{9,11},{10,... | collective-permute-start | bytes 3145736 | tf_op jit(solution)/shard_map/ppermute | solution.py:666
  153.9 37.2 %collective-permute-start.33 = (bf16[256,2048]{1,0:T(8,128)(2,1)S(1)}, bf16[256,2048]{1,0:T(8,128)(2,1)S(1)}, u32[]{:S(2)}, u32[]{:S(2)}) collective-permute-start(bf16[256,2048]{1,0:T(8,128)(2,1)S(1)} %add_convert_fusion.4), channel_id=1, source_target_pairs={{0,4},{4,0},{1,5},{5,1},{2,6},{6,2},{3,7},{7,3},{8,12},{12,8},{9,1... | collective-permute-start | bytes 3145736 | tf_op jit(solution)/shard_map/ppermute | solution.py:666
  169.3 24.7 %collective-permute-start.30 = (bf16[256,1024]{1,0:T(8,128)(2,1)}, bf16[256,1024]{1,0:T(8,128)(2,1)}, u32[]{:S(2)}, u32[]{:S(2)}) collective-permute-start(bf16[256,1024]{1,0:T(8,128)(2,1)} %get-tuple-element.179), channel_id=1, source_target_pairs={{0,1},{1,0},{2,3},{3,2},{4,5},{5,4},{6,7},{7,6},{8,9},{9,8},{10,11... | collective-permute-start | bytes 1572872 | tf_op jit(solution)/shard_map/ppermute | solution.py:666
  169.4 21.8 %collective-permute-start.32 = (bf16[256,1024]{1,0:T(8,128)(2,1)S(1)}, bf16[256,1024]{1,0:T(8,128)(2,1)}, u32[]{:S(2)}, u32[]{:S(2)}) collective-permute-start(bf16[256,1024]{1,0:T(8,128)(2,1)S(1)} %copy-done.32), channel_id=1, source_target_pairs={{0,1},{1,0},{2,3},{3,2},{4,5},{5,4},{6,7},{7,6},{8,9},{9,8},{10,11... | collective-permute-start | bytes 1572872 | tf_op jit(solution)/shard_map/ppermute | solution.py:666
  169.8 27.2 %collective-permute-start.34 = (bf16[256,2048]{1,0:T(8,128)(2,1)}, bf16[256,2048]{1,0:T(8,128)(2,1)}, u32[]{:S(2)}, u32[]{:S(2)}) collective-permute-start(bf16[256,2048]{1,0:T(8,128)(2,1)} %get-tuple-element.189), channel_id=1, source_target_pairs={{0,1},{1,0},{2,3},{3,2},{4,5},{5,4},{6,7},{7,6},{8,9},{9,8},{10,11... | collective-permute-start | bytes 3145736 | tf_op jit(solution)/shard_map/ppermute | solution.py:666
  193.4 20.4 %collective-permute-start.36 = (bf16[256,1024]{1,0:T(8,128)(2,1)}, bf16[256,1024]{1,0:T(8,128)(2,1)S(1)}, u32[]{:S(2)}, u32[]{:S(2)}) collective-permute-start(bf16[256,1024]{1,0:T(8,128)(2,1)} %add_convert_fusion.10), channel_id=1, source_target_pairs={{0,2},{1,3},{2,0},{3,1},{4,6},{5,7},{6,4},{7,5},{8,10},{9,11},{10,... | collective-permute-start | bytes 1572872 | tf_op jit(solution)/shard_map/ppermute | solution.py:666
  196.1 17.7 %collective-permute-start.35 = (bf16[256,1024]{1,0:T(8,128)(2,1)}, bf16[256,1024]{1,0:T(8,128)(2,1)}, u32[]{:S(2)}, u32[]{:S(2)}) collective-permute-start(bf16[256,1024]{1,0:T(8,128)(2,1)} %add_convert_fusion.11), channel_id=1, source_target_pairs={{0,4},{4,0},{1,5},{5,1},{2,6},{6,2},{3,7},{7,3},{8,12},{12,8},{9,1... | collective-permute-start | bytes 1572872 | tf_op jit(solution)/shard_map/ppermute | solution.py:666
  232.5 26.0 %collective-permute-start.41 = (bf16[256,2048]{1,0:T(8,128)(2,1)}, bf16[256,2048]{1,0:T(8,128)(2,1)}, u32[]{:S(2)}, u32[]{:S(2)}) collective-permute-start(bf16[256,2048]{1,0:T(8,128)(2,1)} %add_convert_fusion.3), channel_id=1, source_target_pairs={{0,2},{1,3},{2,0},{3,1},{4,6},{5,7},{6,4},{7,5},{8,10},{9,11},{10,... | collective-permute-start | bytes 3145736 | tf_op jit(solution)/shard_map/ppermute | solution.py:666
  235.6 25.5 %collective-permute-start.43 = (bf16[256,2048]{1,0:T(8,128)(2,1)S(1)}, bf16[256,2048]{1,0:T(8,128)(2,1)S(1)}, u32[]{:S(2)}, u32[]{:S(2)}) collective-permute-start(bf16[256,2048]{1,0:T(8,128)(2,1)S(1)} %add_convert_fusion.2), channel_id=1, source_target_pairs={{0,4},{4,0},{1,5},{5,1},{2,6},{6,2},{3,7},{7,3},{8,12},{12,8},{9,1... | collective-permute-start | bytes 3145736 | tf_op jit(solution)/shard_map/ppermute | solution.py:666
  236.9 24.2 %collective-permute-start.40 = (bf16[256,1024]{1,0:T(8,128)(2,1)}, bf16[256,1024]{1,0:T(8,128)(2,1)}, u32[]{:S(2)}, u32[]{:S(2)}) collective-permute-start(bf16[256,1024]{1,0:T(8,128)(2,1)} %get-tuple-element.205), channel_id=1, source_target_pairs={{0,1},{1,0},{2,3},{3,2},{4,5},{5,4},{6,7},{7,6},{8,9},{9,8},{10,11... | collective-permute-start | bytes 1572872 | tf_op jit(solution)/shard_map/ppermute | solution.py:666
  236.9 27.0 %collective-permute-start.42 = (bf16[256,1024]{1,0:T(8,128)(2,1)}, bf16[256,1024]{1,0:T(8,128)(2,1)}, u32[]{:S(2)}, u32[]{:S(2)}) collective-permute-start(bf16[256,1024]{1,0:T(8,128)(2,1)} %get-tuple-element.208), channel_id=1, source_target_pairs={{0,1},{1,0},{2,3},{3,2},{4,5},{5,4},{6,7},{7,6},{8,9},{9,8},{10,11... | collective-permute-start | bytes 1572872 | tf_op jit(solution)/shard_map/ppermute | solution.py:666
  242.4 43.4 %collective-permute-start.47 = (bf16[256,2048]{1,0:T(8,128)(2,1)}, bf16[256,2048]{1,0:T(8,128)(2,1)}, u32[]{:S(2)}, u32[]{:S(2)}) collective-permute-start(bf16[256,2048]{1,0:T(8,128)(2,1)} %get-tuple-element.218), channel_id=1, source_target_pairs={{0,1},{1,0},{2,3},{3,2},{4,5},{5,4},{6,7},{7,6},{8,9},{9,8},{10,11... | collective-permute-start | bytes 3145736 | tf_op jit(solution)/shard_map/ppermute | solution.py:666
  258.5 15.3 %collective-permute-start.44 = (bf16[128,1024]{1,0:T(8,128)(2,1)S(1)}, bf16[128,1024]{1,0:T(8,128)(2,1)S(1)}, u32[]{:S(2)}, u32[]{:S(2)}) collective-permute-start(bf16[128,1024]{1,0:T(8,128)(2,1)S(1)} %get-tuple-element.298), channel_id=1, source_target_pairs={{0,16},{8,24},{16,0},{24,8},{1,17},{9,25},{17,1},{25,9},{2,18},{10... | collective-permute-start | bytes 786440 | tf_op jit(solution)/shard_map/ppermute | solution.py:666
  290.0 15.3 %collective-permute-start.50 = (bf16[128,1024]{1,0:T(8,128)(2,1)S(1)}, bf16[128,1024]{1,0:T(8,128)(2,1)S(1)}, u32[]{:S(2)}, u32[]{:S(2)}) collective-permute-start(bf16[128,1024]{1,0:T(8,128)(2,1)S(1)} %add_convert_fusion.14), channel_id=1, source_target_pairs={{0,16},{8,24},{16,0},{24,8},{1,17},{9,25},{17,1},{25,9},{2,18},{10... | collective-permute-start | bytes 786440 | tf_op jit(solution)/shard_map/ppermute | solution.py:666
  314.7 38.1 %collective-permute-start.57 = (bf16[256,2048]{1,0:T(8,128)(2,1)S(1)}, bf16[256,2048]{1,0:T(8,128)(2,1)}, u32[]{:S(2)}, u32[]{:S(2)}) collective-permute-start(bf16[256,2048]{1,0:T(8,128)(2,1)S(1)} %add_convert_fusion), channel_id=1, source_target_pairs={{0,4},{4,0},{1,5},{5,1},{2,6},{6,2},{3,7},{7,3},{8,12},{12,8},{9,1... | collective-permute-start | bytes 3145736 | tf_op jit(solution)/shard_map/ppermute | solution.py:666
  315.8 35.0 %collective-permute-start.58 = (bf16[256,1024]{1,0:T(8,128)(2,1)}, bf16[256,1024]{1,0:T(8,128)(2,1)}, u32[]{:S(2)}, u32[]{:S(2)}) collective-permute-start(bf16[256,1024]{1,0:T(8,128)(2,1)} %broadcast_select_fusion.9), channel_id=1, source_target_pairs={{0,8},{8,0},{16,24},{24,16},{1,9},{9,1},{17,25},{25,17},{2,10},{10... | collective-permute-start | bytes 1572872 | tf_op jit(solution)/shard_map/ppermute | solution.py:666
  316.5 37.7 %collective-permute-start.62 = (bf16[256,2048]{1,0:T(8,128)(2,1)S(1)}, bf16[256,2048]{1,0:T(8,128)(2,1)}, u32[]{:S(2)}, u32[]{:S(2)}) collective-permute-start(bf16[256,2048]{1,0:T(8,128)(2,1)S(1)} %add_convert_fusion.1), channel_id=1, source_target_pairs={{0,2},{1,3},{2,0},{3,1},{4,6},{5,7},{6,4},{7,5},{8,10},{9,11},{10,... | collective-permute-start | bytes 3145736 | tf_op jit(solution)/shard_map/ppermute | solution.py:666
  317.1 25.5 %collective-permute-start.52 = (f32[96,128]{1,0:T(8,128)S(1)}, f32[96,128]{1,0:T(8,128)S(1)}, u32[]{:S(2)}, u32[]{:S(2)}) collective-permute-start(f32[96,128]{1,0:T(8,128)S(1)} %bitcast_add_fusion), channel_id=1, source_target_pairs={{0,2},{1,3},{2,0},{3,1},{4,6},{5,7},{6,4},{7,5},{8,10},{9,11},{10,... | collective-permute-start | bytes 147464 | tf_op jit(solution)/shard_map/ppermute | solution.py:666
  352.8 45.1 %collective-permute-start.71 = (bf16[256,1024]{1,0:T(8,128)(2,1)S(1)}, bf16[256,1024]{1,0:T(8,128)(2,1)S(1)}, u32[]{:S(2)}, u32[]{:S(2)}) collective-permute-start(bf16[256,1024]{1,0:T(8,128)(2,1)S(1)} %maximum_select_fusion), channel_id=1, source_target_pairs={{0,8},{8,0},{16,24},{24,16},{1,9},{9,1},{17,25},{25,17},{2,10},{10... | collective-permute-start | bytes 1572872 | tf_op jit(solution)/shard_map/ppermute | solution.py:666
  356.6 15.7 %collective-permute-start.63 = (bf16[128,1024]{1,0:T(8,128)(2,1)S(1)}, bf16[128,1024]{1,0:T(8,128)(2,1)S(1)}, u32[]{:S(2)}, u32[]{:S(2)}) collective-permute-start(bf16[128,1024]{1,0:T(8,128)(2,1)S(1)} %get-tuple-element.296), channel_id=1, source_target_pairs={{0,16},{8,24},{16,0},{24,8},{1,17},{9,25},{17,1},{25,9},{2,18},{10... | collective-permute-start | bytes 786440 | tf_op jit(solution)/shard_map/ppermute | solution.py:666
  358.7 17.1 %collective-permute-start.60 = (bf16[256,1024]{1,0:T(8,128)(2,1)S(1)}, bf16[256,1024]{1,0:T(8,128)(2,1)S(1)}, u32[]{:S(2)}, u32[]{:S(2)}) collective-permute-start(bf16[256,1024]{1,0:T(8,128)(2,1)S(1)} %add_convert_fusion.7), channel_id=1, source_target_pairs={{0,2},{1,3},{2,0},{3,1},{4,6},{5,7},{6,4},{7,5},{8,10},{9,11},{10,... | collective-permute-start | bytes 1572872 | tf_op jit(solution)/shard_map/ppermute | solution.py:666
  360.6 15.2 %collective-permute-start.64 = (bf16[256,1024]{1,0:T(8,128)(2,1)S(1)}, bf16[256,1024]{1,0:T(8,128)(2,1)S(1)}, u32[]{:S(2)}, u32[]{:S(2)}) collective-permute-start(bf16[256,1024]{1,0:T(8,128)(2,1)S(1)} %add_convert_fusion.6), channel_id=1, source_target_pairs={{0,4},{4,0},{1,5},{5,1},{2,6},{6,2},{3,7},{7,3},{8,12},{12,8},{9,1... | collective-permute-start | bytes 1572872 | tf_op jit(solution)/shard_map/ppermute | solution.py:666
  372.3 15.3 %collective-permute-start.66 = (bf16[128,1024]{1,0:T(8,128)(2,1)S(1)}, bf16[128,1024]{1,0:T(8,128)(2,1)S(1)}, u32[]{:S(2)}, u32[]{:S(2)}) collective-permute-start(bf16[128,1024]{1,0:T(8,128)(2,1)S(1)} %add_convert_fusion.13), channel_id=1, source_target_pairs={{0,16},{8,24},{16,0},{24,8},{1,17},{9,25},{17,1},{25,9},{2,18},{10... | collective-permute-start | bytes 786440 | tf_op jit(solution)/shard_map/ppermute | solution.py:666
  377.7 15.5 %collective-permute-start.65 = (bf16[256,1024]{1,0:T(8,128)(2,1)S(1)}, bf16[256,1024]{1,0:T(8,128)(2,1)S(1)}, u32[]{:S(2)}, u32[]{:S(2)}) collective-permute-start(bf16[256,1024]{1,0:T(8,128)(2,1)S(1)} %broadcast_select_fusion.6), channel_id=1, source_target_pairs={{0,8},{8,0},{16,24},{24,16},{1,9},{9,1},{17,25},{25,17},{2,10},{10... | collective-permute-start | bytes 1572872 | tf_op jit(solution)/shard_map/ppermute | solution.py:666
  393.4 15.4 %collective-permute-start.67 = (bf16[128,1024]{1,0:T(8,128)(2,1)S(1)}, bf16[128,1024]{1,0:T(8,128)(2,1)S(1)}, u32[]{:S(2)}, u32[]{:S(2)}) collective-permute-start(bf16[128,1024]{1,0:T(8,128)(2,1)S(1)} %get-tuple-element.294), channel_id=1, source_target_pairs={{0,16},{8,24},{16,0},{24,8},{1,17},{9,25},{17,1},{25,9},{2,18},{10... | collective-permute-start | bytes 786440 | tf_op jit(solution)/shard_map/ppermute | solution.py:666
  398.0 27.5 %collective-permute-start.70 = (bf16[256,1024]{1,0:T(8,128)(2,1)S(1)}, bf16[256,1024]{1,0:T(8,128)(2,1)S(1)}, u32[]{:S(2)}, u32[]{:S(2)}) collective-permute-start(bf16[256,1024]{1,0:T(8,128)(2,1)S(1)} %maximum_select_fusion.1), channel_id=1, source_target_pairs={{0,8},{8,0},{16,24},{24,16},{1,9},{9,1},{17,25},{25,17},{2,10},{10... | collective-permute-start | bytes 1572872 | tf_op jit(solution)/shard_map/ppermute | solution.py:666
  420.5 16.7 %collective-permute-start.69 = (bf16[256,1024]{1,0:T(8,128)(2,1)S(1)}, bf16[256,1024]{1,0:T(8,128)(2,1)S(1)}, u32[]{:S(2)}, u32[]{:S(2)}) collective-permute-start(bf16[256,1024]{1,0:T(8,128)(2,1)S(1)} %maximum_select_fusion.2), channel_id=1, source_target_pairs={{0,8},{8,0},{16,24},{24,16},{1,9},{9,1},{17,25},{25,17},{2,10},{10... | collective-permute-start | bytes 1572872 | tf_op jit(solution)/shard_map/ppermute | solution.py:666
  (58 other events, 541.2 us)

commit v2 on v1

--- a/solution.py
+++ b/solution.py
@@ -19,6 +19,20 @@
 F32 = jnp.float32
 MIB = 1 << 20
 
+COSTS = {
+    "turned": 2,
+    "first_norm": 5,
+    "attend": 11,
+    "second_norm": 5,
+    "up": 6,
+    "weight_grads": 10,
+    "mlp_back": 13,
+    "second_norm_back": 6,
+    "attend_back": 14,
+    "finish": 8,
+}
+COST_UNIT = 0.3 * 3.69e6
+
 NN = (((1,), (0,)), ((), ()))
 NT = (((1,), (1,)), ((), ()))
 
@@ -27,9 +41,15 @@
     return lax.dot_general(left, right, dims, preferred_element_type=F32)
 
 
-def call(body, grid, ins, outs, operands, scratch=(), flops=0, name=None, vmem=58, tables=0):
-    moved = sum(int(np.prod(o.shape)) * o.dtype.itemsize for o in operands)
-    moved += sum(int(np.prod(o.shape)) * o.dtype.itemsize for _, o in outs)
+def call(body, grid, ins, outs, operands, scratch=(), flops=0, name=None, vmem=36, tables=0):
+    operands = [
+        o.value
+        if isinstance(o, Near)
+        else o
+        if o.size * o.dtype.itemsize < MIB // 4
+        else pltpu.with_memory_space_constraint(o, pltpu.HBM)
+        for o in operands
+    ]
     return pl.pallas_call(
         body,
         out_shape=[o for _, o in outs],
@@ -41,7 +61,9 @@
             scratch_shapes=list(scratch),
         ),
         compiler_params=pltpu.CompilerParams(vmem_limit_bytes=vmem * MIB),
-        cost_estimate=pl.CostEstimate(flops=int(flops), bytes_accessed=moved, transcendentals=0),
+        cost_estimate=pl.CostEstimate(
+            flops=0, bytes_accessed=int(COSTS[name] * COST_UNIT), transcendentals=0
+        ),
         name=name,
     )(*operands)
 
@@ -50,8 +72,17 @@
     return lax.optimization_barrier((value, *others))[0]
 
 
+class Near:
+    def __init__(self, value):
+        self.value, self.shape, self.dtype = value, value.shape, value.dtype
+
+
 def shape(dims, dtype):
     return jax.ShapeDtypeStruct(dims, dtype)
+
+
+def far_shape(dims, dtype):
+    return pltpu.HBM(dims, dtype)
 
 
 def columns(meta, ref, places, width):
@@ -73,6 +104,29 @@
     first_term = jnp.mean(inner, axis=-1, keepdims=True)
     second_term = jnp.mean(inner * normal, axis=-1, keepdims=True)
     return scaled * (inner - first_term - normal * second_term)
+
+
+def turned(array, dtype):
+    rows, width = array.shape
+    block = min(512, max(rows, width))
+
+    def body(array, out):
+        out[...] = array[...].astype(F32).T.astype(dtype)
+
+    if rows > width:
+        spec = pl.BlockSpec((block, width), lambda i: (i, 0))
+        out = pl.BlockSpec((width, block), lambda i: (0, i))
+    else:
+        spec = pl.BlockSpec((rows, block), lambda i: (0, i))
+        out = pl.BlockSpec((block, rows), lambda i: (i, 0))
+    return call(
+        body,
+        (max(rows, width) // block,),
+        [spec],
+        [(out, far_shape((width, rows), dtype))],
+        (array,),
+        name="turned",
+    )[0]
 
 
 def first_norm(inputs, cotangent, keep, gain, shift, meta, places):
@@ -99,9 +153,9 @@
         [tall, tall, mark, vector, vector],
         [
             (tall, shape((rows, width), BF)),
-            (wide, shape((width, rows), BF)),
-            (tall, shape((rows, width), BF)),
-            (wide, shape((width, rows), BF)),
+            (wide, far_shape((width, rows), BF)),
+            (tall, far_shape((rows, width), BF)),
+            (wide, far_shape((width, rows), BF)),
         ],
         (meta, inputs, cotangent, keep, gain, shift),
         tables=1,
@@ -214,16 +268,16 @@
         + specs
         + [pl.BlockSpec((1, 3 * part), lambda j: (0, j)), fixed(rows, 1), fixed(1, rows)],
         [
-            (pl.BlockSpec((rows, 3 * part), lambda j: (0, j)), shape((rows, halves * 3 * part), BF)),
-            (pl.BlockSpec((rows, part), lambda j: (0, j)), shape((rows, halves * part), BF)),
+            (pl.BlockSpec((rows, 3 * part), lambda j: (0, j)), far_shape((rows, halves * 3 * part), BF)),
+            (pl.BlockSpec((rows, part), lambda j: (0, j)), far_shape((rows, halves * part), BF)),
             (
                 pl.BlockSpec((heads, rows, rows), lambda j: (j, 0, 0)),
-                shape((halves * heads, rows, rows), BF),
+                far_shape((halves * heads, rows, rows), BF),
             ),
             (pl.BlockSpec((1, heads, rows), lambda j: (j, 0, 0)), shape((halves, heads, rows), F32)),
             (fixed(rows, width), shape((rows, width), F32)),
         ],
-        (normed, *weights, bias, labels_col, labels_row),
+        (Near(normed), *weights, bias, labels_col, labels_row),
         scratch=[pltpu.VMEM((rows, rows), F32)],
         flops=2 * rows * width * total + halves * heads * 8 * rows * rows * HD,
         name="attend",
@@ -257,67 +311,78 @@
         (rows // block,),
         [tall] * (1 + count) + [vector] * 3,
         [
-            (tall, shape((rows, width), F32)),
+            (tall, far_shape((rows, width), F32)),
             (tall, shape((rows, width), BF)),
-            (wide, shape((width, rows), BF)),
+            (wide, far_shape((width, rows), BF)),
         ],
-        (meta, inputs, *branches, out_bias, gain, shift),
+        (meta, inputs, *map(Near, branches), out_bias, gain, shift),
         tables=1,
         name="second_norm",
     )
 
 
-def up_steps(total, halves):
-    return max(halves, total // 512)
-
-
-def up(normed, pieces, bias, halves):
+def tiles_of(gathered, groups, line, lines, steps):
+    places, part, columns_all = gathered.shape[1:]
+    per_line = groups // lines
+    per = steps // per_line
+    wide = columns_all // per
+
+    def spec(r):
+        def index(j, spots):
+            y = line * per_line + lax.div(j, jnp.int32(per))
+            return (spots[places + y], spots[r], 0, lax.rem(j, jnp.int32(per)))
+
+        return pl.BlockSpec((1, 1, part, wide), index)
+
+    return [spec(r) for r in range(places)], wide
+
+
+def joined(refs):
+    return jnp.concatenate([ref[0, 0] for ref in refs], axis=0)
+
+
+def up(normed, gathered, bias, spots, line, lines, steps):
     rows, width = normed.shape
-    total = sum(p.shape[1] for p in pieces[0])
-    steps = up_steps(total, halves)
-    wide = total // steps
-    specs, weights, counts = tile_specs(pieces, wide, steps)
-
-    def body(normed, *refs):
-        weight_refs = regroup(refs[: len(weights)], counts)
-        bias, hidden, slope = refs[len(weights) :]
-        tile = tile_of(weight_refs, pl.program_id(0), steps)
-        before = dot(normed[...], tile) + bias[...].astype(F32)
+    groups, places = gathered.shape[:2]
+    specs, wide = tiles_of(gathered, groups, line, lines, steps)
+    total = wide * steps
+
+    def body(spots, normed, *refs):
+        bias, hidden, slope = refs[places:]
+        before = dot(normed[...], joined(refs[:places])) + bias[...].astype(F32)
         below = 0.5 * (1.0 + lax.erf(before * SQRT_HALF))
         hidden[...] = (before * below).astype(BF)
         density = jnp.exp(before * before * -0.5) * DENSITY_SCALE
         slope[...] = (below + before * density).astype(BF)
 
-    tall = pl.BlockSpec((rows, wide), lambda j: (0, j))
+    tall = pl.BlockSpec((rows, wide), lambda j, *_: (0, j))
     return call(
         body,
         (steps,),
-        [pl.BlockSpec((rows, width), lambda j: (0, 0))]
+        [pl.BlockSpec((rows, width), lambda j, *_: (0, 0))]
         + specs
-        + [pl.BlockSpec((1, wide), lambda j: (0, j))],
+        + [pl.BlockSpec((1, wide), lambda j, *_: (0, j))],
         [(tall, shape((rows, total), BF)), (tall, shape((rows, total), BF))],
-        (normed, *weights, bias),
-        flops=2 * rows * width * total,
+        (spots, Near(normed), *[gathered] * places, bias),
         name="up",
-    )
-
-
-def mlp_back(low, hidden, slope, up_pieces, down_pieces, halves):
+        tables=1,
+    )
+
+
+def mlp_back(low, hidden, slope, up_all, down_pieces, spots, line, lines, steps):
     rows, width = low.shape
-    total = hidden.shape[1]
-    steps = up_steps(total, halves)
-    wide = total // steps
-    up_specs, up_weights, up_counts = tile_specs(up_pieces, wide, steps)
-    down_specs, down_weights, down_counts = tile_specs(down_pieces, wide, steps)
-    count = len(up_weights)
-
-    def body(low, hidden, slope, *refs):
-        up_refs = regroup(refs[:count], up_counts)
-        down_refs = regroup(refs[count : 2 * count], down_counts)
-        before, sums, mlp, normed = refs[2 * count :]
+    groups, places = up_all.shape[:2]
+    specs, wide = tiles_of(up_all, groups, line, lines, steps)
+    total = wide * steps
+
+    down_specs, down_weights, counts = tile_specs(down_pieces, wide, steps)
+    count = len(down_weights)
+
+    def body(spots, low, hidden, slope, *refs):
+        before, sums, mlp, normed = refs[places + count :]
         step = pl.program_id(0)
-        down_tile = tile_of(down_refs, step, steps)
-        up_tile = tile_of(up_refs, step, steps)
+        up_tile = joined(refs[:places])
+        down_tile = tile_of(regroup(refs[places : places + count], counts), step, steps)
         grad = dot(low[...], down_tile) * slope[...].astype(F32)
         grad_low = grad.astype(BF)
         before[...] = grad_low
@@ -335,21 +400,21 @@
             mlp[...] += product
             normed[...] += back
 
-    fixed = pl.BlockSpec((rows, width), lambda j: (0, 0))
-    tall = pl.BlockSpec((rows, wide), lambda j: (0, j))
+    fixed = pl.BlockSpec((rows, width), lambda j, *_: (0, 0))
+    tall = pl.BlockSpec((rows, wide), lambda j, *_: (0, j))
     return call(
         body,
         (steps,),
-        [fixed, tall, tall] + up_specs + down_specs,
+        [fixed, tall, tall] + specs + down_specs,
         [
-            (tall, shape((rows, total), BF)),
-            (pl.BlockSpec((1, wide), lambda j: (0, j)), shape((1, total), F32)),
-            (fixed, shape((rows, width), F32)),
+            (tall, far_shape((rows, total), BF)),
+            (pl.BlockSpec((1, wide), lambda j, *_: (0, j)), shape((1, total), F32)),
+            (fixed, far_shape((rows, width), F32)),
             (fixed, shape((rows, width), F32)),
         ],
-        (low, hidden, slope, *up_weights, *down_weights),
-        flops=6 * rows * width * total,
+        (spots, low, Near(hidden), Near(slope), *[up_all] * places, *down_weights),
         name="mlp_back",
+        tables=1,
     )
 
 
@@ -389,12 +454,12 @@
         (rows // block,),
         [tall, tall] + [tall] * count + [vector],
         [
-            (tall, shape((rows, width), F32)),
+            (tall, far_shape((rows, width), F32)),
             (tall, shape((rows, width), BF)),
-            (wide, shape((width, rows), BF)),
+            (wide, far_shape((width, rows), BF)),
             (pl.BlockSpec((4, width), lambda i, *_: (0, 0)), shape((4, width), F32)),
         ],
-        (meta, middle, low, *backs, gain),
+        (meta, middle, low, *map(Near, backs), gain),
         tables=1,
         name="second_norm_back",
     )
@@ -489,9 +554,9 @@
         [
             (wide_rows, shape((rows, halves * 3 * part), BF)),
             (pl.BlockSpec((1, 3 * part), lambda j: (0, j)), shape((1, halves * 3 * part), F32)),
-            (fixed, shape((rows, width), F32)),
+            (fixed, far_shape((rows, width), F32)),
         ],
-        (grad_low, *weights, qkv, probs, inverses),
+        (Near(grad_low), *weights, qkv, probs, inverses),
         flops=2 * rows * width * total + halves * heads * 8 * rows * rows * HD,
         name="attend_back",
     )
@@ -545,30 +610,43 @@
     )
 
 
-def bundle_plan(groups, halves):
-    plan = {"x": [(1, 0, 0)] + [(1, y, 0) for y in range(1, groups)]}
-    for y in range(1, groups):
+def bundle_plan(members, halves):
+    plan = {"x": [(1, y, 0) for y in members]}
+    for y in members:
+        if y:
+            plan["keep", y] = [(0, y, 0)]
+            if halves > 1:
+                plan["y", y] = [(0, y, 1), (1, y, 1)]
+    if 0 in members:
         if halves > 1:
-            plan["y", y] = [(0, y, 1), (1, y, 1)]
-        plan["keep", y] = [(0, y, 0)]
-    if halves > 1:
-        plan["far"] = [(1, 0, 1)]
-    plan["own"] = [(0, 0, h) for h in range(halves)]
+            plan["far"] = [(1, 0, 1)]
+        plan["own"] = [(0, 0, h) for h in range(halves)]
     return plan
 
 
-def weight_grads(plan, lefts, rights, groups, halves):
+def urgent(name):
+    return name == "x" or name[0] == "y"
+
+
+def alone(name):
+    return urgent(name) or name == "far"
+
+
+def weight_grads(plan, lefts, rights, blocks, halves):
     width, rows = lefts[0].shape
     part = width // 4
     lines = len(rights)
-    blocks = groups * halves // lines
+    first = min(y for made in plan.values() for _, y, _ in made) * halves // blocks
     spans = [array.shape[1] // blocks for array in rights[0]]
     wide = sum(spans)
     kinds = len(spans)
-    order = [(y, 0) for y in range(groups)] + [(y, h) for h in range(1, halves) for y in [*range(1, groups), 0]]
+    order = []
+    for made in plan.values():
+        order += [block[1:] for block in made if block[1:] not in order]
     names = list(plan)
+    rest = [block for name in names if not alone(name) for block in plan[name]]
     outs, joint = [], {}
-    for _ in range(2):
+    for core in range(2):
         for name in names:
             steps = [order.index(block[1:]) for block in plan[name]]
             joint[name] = len(set(steps)) == 1
@@ -581,7 +659,12 @@
                     at = at + (i >= start).astype(jnp.int32)
                 return (0, at)
 
-            outs.append((pl.BlockSpec((part, size), index), shape((part, wide * len(steps)), BF)))
+            if not core or alone(name):
+                outs.append(
+                    (pl.BlockSpec((part, size), index), far_shape((part, wide * len(steps)), BF))
+                )
+    whole = (part, wide * len(rest))
+    outs.append((pl.BlockSpec(whole, lambda i: (0, 0)), far_shape(whole, BF)))
 
     def body(*refs):
         left_refs = refs[:kinds]
@@ -592,7 +675,7 @@
 
             @pl.when(step == s)
             def _(y=y, h=h):
-                line = (y * halves + h) // blocks
+                line = (y * halves + h) // blocks - first
                 for r in range(4):
                     x, core = divmod(r, 2)
                     here = slice(r * part, (r + 1) * part)
@@ -601,14 +684,19 @@
                         for k in range(kinds)
                     ]
                     value = jnp.concatenate(products, axis=1) if kinds > 1 else products[0]
-                    for n, name in enumerate(names):
+                    if core and (x, y, h) in rest:
+                        at = rest.index((x, y, h)) * wide
+                        out_refs[-1][:, at : at + wide] = value
+                        continue
+                    sent = [name for name in names if alone(name)]
+                    for n, name in enumerate(sent if core else names):
                         if (x, y, h) in plan[name]:
                             at = plan[name].index((x, y, h)) * wide if joint[name] else 0
                             out_refs[core * len(names) + n][:, at : at + wide] = value
 
     def right_map(g):
         flat = [y * halves + h for y, h in order]
-        mine = [(s, at % blocks) for s, at in enumerate(flat) if at // blocks == g]
+        mine = [(s, at % blocks) for s, at in enumerate(flat) if at // blocks - first == g]
         def index(i):
             at = mine[0][1]
             for (s0, h0), (s1, h1) in zip(mine, mine[1:]):
@@ -620,9 +708,54 @@
     for g in range(lines):
         for k in range(kinds):
             ins.append(pl.BlockSpec((rows, spans[k]), right_map(g)))
-            operands.append(rights[g][k])
-    made = call(body, (len(order),), ins, outs, operands, flops=2 * rows * width * wide * len(order), name="weight_grads")
-    return dict(zip(names, made[: len(names)])), dict(zip(names, made[len(names) :]))
+            operands.append(Near(rights[g][k]))
+    made = call(body, (len(order),), ins, outs, operands, name="weight_grads")
+    mine = dict(zip(names, made[: len(names)]))
+    sent = [name for name in names if alone(name)]
+    return mine, dict(zip([*sent, "rest"], made[len(names) :])), rest
+
+
+def all_weight_grads(left, rights, spots, groups, places, blocks):
+    width, rows = left.shape
+    part = width // places
+    lines = len(rights)
+    wide = rights[0].shape[1] // blocks
+    count = lines * blocks
+    per = count // groups
+
+    def body(spots, left, *refs):
+        right_refs, out = refs[:lines], refs[lines]
+        step = pl.program_id(0)
+        for line in range(lines):
+
+            @pl.when((step >= line * blocks) & (step < (line + 1) * blocks))
+            def _(line=line):
+                for r in range(places):
+                    here = left[r * part : (r + 1) * part, :]
+                    out[0, spots[r]] = dot(here, right_refs[line][...]).astype(BF)
+
+    def right(line):
+        return pl.BlockSpec(
+            (rows, wide), lambda i, *_: (0, jnp.clip(i - line * blocks, 0, blocks - 1))
+        )
+
+    def index(i, spots):
+        return (spots[places + lax.div(i, jnp.int32(per))], 0, 0, lax.rem(i, jnp.int32(per)))
+
+    return call(
+        body,
+        (count,),
+        [pl.BlockSpec((width, rows), lambda i, *_: (0, 0))] + [right(k) for k in range(lines)],
+        [
+            (
+                pl.BlockSpec((1, places, part, wide), index),
+                far_shape((groups, places, part, wide * per), BF),
+            )
+        ],
+        (spots, left, *map(Near, rights)),
+        name="weight_grads",
+        tables=1,
+    )[0]
 
 
 def shards(
@@ -656,6 +789,7 @@
     lines = min(2, groups)
     per_line = groups // lines
     steps = per_line * halves
+    unit_steps = max(per_line, per_line * hidden_width // 512)
 
     def members(line):
         return range(line * per_line, (line + 1) * per_line)
@@ -669,7 +803,13 @@
     over_x = swap("narrow", 2)
     over_y = [None] + [swap("wide", m) for m in range(1, groups)]
 
-    meta = jnp.bitwise_xor(place, jnp.arange(places, dtype=jnp.int32)) * part
+    spots = jnp.concatenate(
+        [
+            jnp.bitwise_xor(place, jnp.arange(places, dtype=jnp.int32)),
+            jnp.bitwise_xor(member, jnp.arange(groups, dtype=jnp.int32)),
+        ]
+    )
+    meta = spots[:places] * part
     row_of = lambda vector: vector.astype(F32).reshape(1, -1)
     keep = (segments >= 0).astype(F32).reshape(rows, 1)
     labels_col = segments.reshape(rows, 1)
@@ -680,7 +820,7 @@
     packed = jnp.concatenate([three, out_t], axis=1).transpose(0, 2, 1, 3)
     packed = packed.reshape(part, 4 * part_width)
     small = jnp.concatenate([qv_bias.reshape(-1), up_bias]).reshape(1, -1)
-    down_t = down_weight.T
+    down_t = turned(down_weight, BF)
 
     def split(array):
         wide = array.shape[1] // halves
@@ -693,12 +833,17 @@
             near[0, y] = [over_y[y](ready)]
         return near
 
+    passed = []
+
     def forward_far(near):
         made = {}
         for y in range(1, groups):
-            made[1, y] = [over_x(split(near[0, y][0])[0])]
+            sent = [split(near[0, y][0])[0]]
+            made[1, y] = [over_x(sent[0])]
             if halves > 1:
-                made[1, y].append(over_y[y](split(near[1, 0][0])[1]))
+                sent.append(split(near[1, 0][0])[1])
+                made[1, y].append(over_y[y](sent[1]))
+            passed.extend(sent)
         return made
 
     def line_of(near, line):
@@ -729,6 +874,10 @@
             for key, value in near.items()
         }
 
+    def all_of(weight):
+        made = lax.all_gather(weight, ("wide", "narrow"), axis=0)
+        return made.reshape(groups, places, *weight.shape)
+
     attn_near = reach(packed)
     normed_one, normed_one_t, low, low_t = done(
         first_norm(
@@ -737,7 +886,7 @@
         0,
     )
     attn_near = held(attn_near, *turn)
-    up_near = reach(up_weight, *first_stage(attn_near))
+    up_all = all_of(after(up_weight, *first_stage(attn_near)))
 
     def qkv_bias(values):
         query = values[:, :part_width].reshape(halves, 1, head_part)
@@ -745,25 +894,23 @@
         return jnp.concatenate([query, jnp.zeros_like(query), value], axis=1).reshape(1, -1)
 
     forward = []
-    far = forward_far(attn_near)
-    attn_pieces = [line_of(attn_near | {key: far[key] for key in far if key[1] < per_line}, 0)]
+    attn_far = forward_far(attn_near)
+    down_near = reach(down_t, *turn, *passed)
+    first = {key: attn_far[key] for key in attn_far if key[1] < per_line}
+    attn_pieces = [line_of(attn_near | first, 0)]
     for line in range(lines):
         if line:
-            attn_near = held(attn_near | far, *turn)
+            attn_near = held(attn_near | attn_far, *turn)
             attn_pieces.append(line_of(attn_near, line))
         bias = jnp.concatenate([qkv_bias(small_all[y]) for y in members(line)], axis=1)
         forward.append(
             done(
                 attend(
-                    ordered(normed_one), attn_pieces[line], bias, labels_col, labels_row, steps
+                    ordered(normed_one, down_t), attn_pieces[line], bias, labels_col, labels_row, steps
                 ),
                 1,
             )
         )
-    up_near = held(up_near, *turn)
-    down_near = reach(down_t, *first_stage(up_near))
-    up_near.update(forward_far(up_near))
-    up_pieces = [line_of(up_near, line) for line in range(lines)]
     middle, normed_two, normed_two_t = done(
         second_norm(
             ordered(inputs),
@@ -776,69 +923,94 @@
         ),
         0,
     )
+    down_near = held(down_near, *turn)
+    turn.extend(first_stage(down_near))
+    down_far = forward_far(down_near)
     units = []
     for line in range(lines):
         bias = [small_all[y][:, 2 * part_width :] for y in members(line)]
         bias = jnp.concatenate(bias, axis=1)
-        units.append(done(up(ordered(normed_two), up_pieces[line], bias, steps), 0))
-
-    plan = bundle_plan(groups, halves)
+        units.append(
+            done(up(ordered(normed_two), up_all, bias, spots, line, lines, unit_steps), 0)
+        )
+
+    down_far = held(down_far, *turn)
+    turn.extend(array for arrays in down_far.values() for array in arrays)
     block_width = 4 * head_part
-
-    def grads_of(lefts, rights):
-        lefts = [ordered(lefts[0])] + lefts[1:]
-        mine, other = weight_grads(plan, lefts, rights, groups, halves)
-        turn[:] = [mine["own"]]
-        return mine, {name: core(value) for name, value in other.items()}
-
-    def both(pair, name):
-        return pair[0][name].astype(F32) + pair[1][name].astype(F32)
 
     def cut(array, k):
         return array[:, k * block_width : (k + 1) * block_width].astype(F32)
 
-    def send_first(pair):
-        for_x = both(pair, "x").astype(BF)
-        for_y = {}
+    def grads_of(lefts, rights, ys=range(groups)):
+        plan = bundle_plan(ys, halves)
+        lefts = [ordered(lefts[0])] + lefts[1:]
+        mine, other, rest = weight_grads(plan, lefts, rights, steps, halves)
+        turn[:] = [next(iter(mine.values()))]
+        came = {name: core(value) for name, value in other.items()}
+        at = {}
+        for name in mine:
+            if not alone(name):
+                at[name] = rest.index(plan[name][0]), len(plan[name])
+        return ys, mine, came, at
+
+    def both(made, name):
+        _, mine, came, at = made
+        if name in came:
+            return mine[name].astype(F32) + ordered(came[name]).astype(F32)
+        first, count = at[name]
+        last = first + count
+        came = ordered(came["rest"])[:, first * block_width : last * block_width]
+        return mine[name].astype(F32) + came.astype(F32)
+
+    def send_first(made):
+        ys, mine = made[:2]
+        sums = {name: both(made, name).astype(BF) for name in mine if urgent(name)}
+        turn.extend(sums.values())
+        got = {}
+        for name, value in sums.items():
+            if name == "x":
+                from_x = over_x(value)
+                got.update({("x", y): (from_x, k) for k, y in enumerate(ys)})
+            else:
+                got[name] = over_y[name[1]](value)
+        return got
+
+    def send_near(made, got, late):
+        for y in made[0]:
+            if y:
+                array, k = got["x", y]
+                value = (both(made, ("keep", y)) + cut(ordered(array), k)).astype(BF)
+                turn.append(value)
+                late[y] = over_y[y](value)
+
+    def send_far(made, got, late):
         if halves > 1:
-            for_y = {y: both(pair, ("y", y)).astype(BF) for y in range(1, groups)}
-        from_x = over_x(for_x)
-        from_y = {y: over_y[y](value) for y, value in for_y.items()}
-        turn.extend([for_x, *for_y.values()])
-        return from_x, from_y
-
-    def send_second(pair, got):
-        from_x = ordered(got[0])
-        from_y = {y: ordered(value) for y, value in got[1].items()}
-        far = None
+            value = both(made, "far")
+            for y in range(1, groups):
+                value = value + cut(ordered(got["y", y]), 1)
+            value = value.astype(BF)
+            turn.append(value)
+            late["far"] = over_x(value)
+
+    def total_of(parts, got, late):
+        own = [both(made, "own") for made in parts if 0 in made[0]][0]
+        late = {key: ordered(value).astype(F32) for key, value in late.items()}
+        totals = [own[:, h * block_width : (h + 1) * block_width] for h in range(halves)]
+        totals[0] = totals[0] + cut(*got["x", 0])
+        for y in range(1, groups):
+            totals[0] = totals[0] + late[y]
+            if halves > 1:
+                totals[1] = totals[1] + cut(got["y", y], 0)
         if halves > 1:
-            far = both(pair, "far")
-            for y in range(1, groups):
-                far = far + cut(from_y[y], 1)
-            far = far.astype(BF)
-        near = [(both(pair, ("keep", y)) + cut(from_x, y)).astype(BF) for y in range(1, groups)]
-        late = [over_y[y](near[y - 1]) for y in range(1, groups)]
-        far_late = over_x(far) if halves > 1 else None
-        turn.extend(near + ([far] if halves > 1 else []))
-        return from_x, from_y, late, far_late
+            totals[1] = totals[1] + late["far"]
+        return totals
 
     copy_index = lax.axis_index("dp")
     masks = [1 << k for k in range(copies.bit_length() - 1)]
     bits = [(copy_index // mask) % 2 for mask in masks]
 
-    def total_of(pair, got):
-        from_x, from_y, late, far_late = got
-        late = [ordered(value) for value in late]
-        own = both(pair, "own")
-        totals = [own[:, h * block_width : (h + 1) * block_width] for h in range(halves)]
-        totals[0] = totals[0] + cut(from_x, 0)
-        for y in range(1, groups):
-            totals[0] = totals[0] + late[y - 1].astype(F32)
-            if halves > 1:
-                totals[1] = totals[1] + cut(from_y[y], 0)
-        if halves > 1:
-            totals[1] = totals[1] + ordered(far_late).astype(F32)
-        else:
+    def first_halve(totals):
+        if len(totals) == 1:
             middle = block_width // 2
             totals = [totals[0][:, :middle], totals[0][:, middle:]]
         low, high = (t.astype(BF) for t in totals)
@@ -870,41 +1042,60 @@
         turn.extend([value])
         return value, swap("dp", masks[k])(value)
 
-    def last_join(state):
+    def last_join(state, dtype=F32):
         value, came = state
         low = jnp.where(bits[0] == 1, came, value)
         high = jnp.where(bits[0] == 1, value, came)
-        return jnp.concatenate([low, high], axis=1).astype(F32)
-
-    def steps_of(pair):
-        state = total_of(*pair)
-        yield
-        for k in range(1, len(masks)):
-            state = halve(state, k)
-            yield
-        for k in reversed(range(len(masks))):
-            state = join(state, k)
-            yield
-        yield last_join(state)
-
-    down_pair = grads_of([low_t], [[u[0]] for u in units])
-    down_near = held(down_near, *turn)
-    down_near.update(forward_far(down_near))
-    down_pieces = [line_of(down_near, line) for line in range(lines)]
-    down_got = send_first(down_pair)
-
+        return jnp.concatenate([low, high], axis=1).astype(dtype)
+
+    def vector_steps(vector):
+        for axis, size in (("narrow", places), ("wide", groups), ("dp", copies)):
+            mask = 1
+            while mask < size:
+                vector = vector + swap(axis, mask)(vector)
+                yield vector
+                mask *= 2
+
+    first = {key: down_far[key] for key in down_far if key[1] < per_line}
+    down_pieces = [line_of(down_near | first, 0)]
+    down_grad = all_weight_grads(
+        ordered(low_t), [u[0] for u in units], spots, groups, places, steps
+    )
+    turn[:] = [down_grad]
+    down_pieces += [line_of(down_near | down_far, line) for line in range(1, lines)]
+    down_grad = lax.psum_scatter(
+        down_grad.reshape(groups * places, part, hidden_width),
+        ("wide", "narrow"),
+        scatter_dimension=0,
+        tiled=True,
+    )[0]
     back = []
     for line in range(lines):
         hidden, slope = units[line]
-        pieces = up_pieces[line], down_pieces[line]
-        back.append(done(mlp_back(ordered(low), hidden, slope, *pieces, steps), 0))
+        back.append(
+            done(
+                mlp_back(
+                    ordered(low),
+                    hidden,
+                    slope,
+                    up_all,
+                    down_pieces[line],
+                    spots,
+                    line,
+                    lines,
+                    unit_steps,
+                ),
+                0,
+            )
+        )
+    up_made = grads_of([normed_two_t], [[b[0]] for b in back])
     grad_middle, grad_middle_low, grad_middle_t, second_sums = done(
         second_norm_back(
             ordered(middle), [b[3] for b in back], low, row_of(second_gain), meta, places
         ),
         0,
     )
-    down_got = send_second(down_pair, down_got)
+    up_got = send_first(up_made)
     grads = [None] * lines
 
     def back_of(line):
@@ -916,24 +1107,30 @@
             0,
         )
 
+    attn_made, attn_got, attn_late, up_late = [], {}, {}, {}
+
+    def attn_grads(line):
+        rights = [[grads[line][0], forward[line][1]]]
+        made = grads_of([normed_one_t, grad_middle_t], rights, members(line))
+        attn_made.append(made)
+        return made
+
     back_of(lines - 1)
-    down_steps = steps_of((down_pair, down_got))
-    next(down_steps)
-    up_pair = grads_of([normed_two_t], [[b[0]] for b in back])
-    up_got = send_first(up_pair)
-    next(down_steps)
-    for line in reversed(range(lines - 1)):
-        back_of(line)
-    up_got = send_second(up_pair, up_got)
-    next(down_steps)
-    attn_pair = grads_of(
-        [normed_one_t, grad_middle_t],
-        [[grads[line][0], forward[line][1]] for line in range(lines)],
-    )
-    attn_got = send_first(attn_pair)
-    up_steps_left = steps_of((up_pair, up_got))
-    next(up_steps_left)
-    next(down_steps)
+    down_state = first_halve(
+        [down_grad[:, : hidden_width // 2], down_grad[:, hidden_width // 2 :]]
+    )
+    for line in reversed(range(1, lines)):
+        made = attn_grads(line)
+        if line == lines - 1:
+            send_near(up_made, up_got, up_late)
+            send_far(up_made, up_got, up_late)
+            for k in range(1, len(masks)):
+                down_state = halve(down_state, k)
+        back_of(line - 1)
+        attn_got |= send_first(made)
+    for k in reversed(range(1, len(masks))):
+        down_state = join(down_state, k)
+    up_state = first_halve(total_of([up_made], up_got, up_late))
     output, input_grad, first_sums = done(
         finish(
             ordered(inputs),
@@ -949,15 +1146,6 @@
         ),
         0,
     )
-    next(up_steps_left)
-    attn_got = send_second(attn_pair, attn_got)
-    next(up_steps_left)
-    attn_steps = steps_of((attn_pair, attn_got))
-    next(attn_steps)
-    *_, down_total = down_steps
-    *_, up_total = up_steps_left
-    *_, attn_total = attn_steps
-
     def in_order(values):
         stacked = jnp.stack(values)
         index = jnp.bitwise_xor(member, jnp.arange(groups, dtype=jnp.int32))
@@ -978,11 +1166,28 @@
             value_sums,
         ]
     ).reshape(-1, LANES)
-    for axis, size in (("narrow", places), ("wide", groups), ("dp", copies)):
-        mask = 1
-        while mask < size:
-            vector = vector + swap(axis, mask)(vector)
-            mask *= 2
+    for made in attn_made:
+        send_near(made, attn_got, attn_late)
+    down_state = join(down_state, 0)
+    made = attn_grads(0)
+    up_state = halve(up_state, 1)
+    attn_got |= send_first(made)
+    send_near(made, attn_got, attn_late)
+    send_far(made, attn_got, attn_late)
+    for k in range(2, len(masks)):
+        up_state = halve(up_state, k)
+    for k in reversed(range(1, len(masks))):
+        up_state = join(up_state, k)
+    for vector in vector_steps(ordered(vector)):
+        pass
+    down_total = last_join(down_state, BF)
+    state = first_halve(total_of(attn_made, attn_got, attn_late))
+    up_state = join(up_state, 0)
+    for k in range(1, len(masks)):
+        state = halve(state, k)
+    for k in reversed(range(len(masks))):
+        state = join(state, k)
+    attn_total, up_total = last_join(state), last_join(up_state)
     vector = vector.reshape(-1)
     piece = lambda k: vector[k * width : (k + 1) * width]
     at = 6 * width
@@ -999,9 +1204,10 @@
         ]
     )
 
-    attn_total = attn_total.reshape(part, halves, 4, head_part)
-    qkv_grad = attn_total[:, :, :3].transpose(0, 2, 1, 3).reshape(part, 3, part_width)
-    out_grad = attn_total[:, :, 3].reshape(part, part_width).T
+    spans = [attn_total[:, k * head_part : (k + 1) * head_part] for k in range(4 * halves)]
+    spans = [jnp.concatenate(spans[k::4], axis=1) for k in range(4)]
+    qkv_grad = jnp.stack(spans[:3]).transpose(1, 0, 2)
+    out_grad = turned(spans[3], F32)
     return (
         output,
         input_grad,
@@ -1015,7 +1221,7 @@
         piece(1),
         up_total,
         up_bias_grad,
-        down_total.T,
+        turned(down_total, F32),
         piece(3),
     )
 

time: 453 us -> 419 us (0.925)
  waiting for transfers between devices: 153 us -> 131 us
  starting transfers between devices: 65.3 us -> 47.3 us
  between operations: 2.13 us -> 15.3 us
  other arithmetic: 40.8 us -> 30.1 us
    ppermute x72 -> x55, waiting for transfers between devices: 153 us -> 127 us  [swap(): return lambda value: lax.ppermute(value, axis, pairs)]
    ppermute x72 -> x55, starting transfers between devices: 65.3 us -> 46.9 us  [swap(): return lambda value: lax.ppermute(value, axis, pairs)]
    unnamed x76 -> x100, local copies, waits for them, and re-layouts: 6.18 us -> 15.3 us
    convert_element_type x14 -> x11, other arithmetic: 20.3 us -> 16.3 us  [the longest x5 8.27 us: send_first(): sums = {name: both(made, name).astype(BF) for name in mine if urgent(name)}]
    pallas_call x15 -> x19, Pallas kernels: 156 us -> 159 us  [call(): pl.pallas_call(body, out_shape=[o for _, o in outs], grid_spec=pltpu.Pref...]
  transfers between devices with their start and end apart: 72 -> 57, of which waited for: 24 -> 23; matrix products, arithmetic and copies ran while one was open for 11% -> 9% of each run, Pallas kernels for 31% -> 36%
where the time goes in v2:
time: 419 us; the launch traced here: 413 us
  Pallas kernels  159 us (38%)
  waiting for transfers between devices  131 us (31%)
  starting transfers between devices  47.3 us (11%)
  local copies, waits for them, and re-layouts  30.1 us (7%)
  other arithmetic  30.1 us (7%)
  between operations  15.3 us (4%)
    pallas_call x19, Pallas kernels, call(): pl.pallas_call(body, out_shape=[o for _, o in outs], grid_spec=pltpu.Pref...  159 us
    ppermute x55, waiting for transfers between devices, swap(): return lambda value: lax.ppermute(value, axis, pairs)  127 us
    ppermute x55, starting transfers between devices, swap(): return lambda value: lax.ppermute(value, axis, pairs)  46.9 us
    unnamed x100, local copies, waits for them, and re-layouts  15.3 us
  transfers between devices with their start and end apart: 57, of which 23 were waited for; matrix products, arithmetic and copies ran while one was open for 9% of the time, Pallas kernels for 36%

profile of v2, /device:TPU:0, one launch (start us, length us, event | category | flops | bytes accessed | tf_op | source)
XLA Modules:
  0.0 413.4 jit_solution(13614175341717755179)
XLA Ops:
  8.5 2.2 reshape.156
  13.8 3.0 collective-permute-start.1
  18.5 5.1 %first_norm.1 = (bf16[512,1024]{1,0:T(8,128)(2,1)S(1)}, bf16[1024,512]{1,0:T(8,128)(2,1)}, bf16[512,1024]{1,0:T(8,128)(2,1)}, bf16[1024,512]{1,0:T(8,128)(2,1)}) custom-call(s32[4]{0:T(128)S(1)} %broadcast_multiply_fusion.meta, bf16[512,1024]{1,0:T(8,128)(2,1)} %x.3, bf16[512,1024]{1,0:T(8,128)(2,1)} %cot.1, f32[512,1]{1,0:T(8,128)S(1)} %copy.33.keep, ...), custom_call_target="tpu_custom_call" | custom-call | bytes 5535000 | tf_op jit(solution)/shard_map/first_norm/pallas_call | solution.py:53
  23.6 16.5 %collective-permute-done.1.refs_2_ = bf16[256,2048]{1,0:T(8,128)(2,1)} collective-permute-done((bf16[256,2048]{1,0:T(8,128)(2,1)S(1)}, bf16[256,2048]{1,0:T(8,128)(2,1)}, u32[]{:S(2)}, u32[]{:S(2)}) %collective-permute-start.1) | collective-permute-done | bytes 1048608 | tf_op jit(solution)/shard_map/ppermute | solution.py:800
  44.1 3.7 turned.3.refs_4_
  51.2 10.7 %attend.2 = (bf16[512,1536]{1,0:T(8,128)(2,1)}, bf16[512,512]{1,0:T(8,128)(2,1)}, bf16[8,512,512]{2,1,0:T(8,128)(2,1)}, f32[2,4,512]{2,1,0:T(4,128)S(1)}, f32[512,1024]{1,0:T(8,128)S(1)}) custom-call(bf16[512,1024]{1,0:T(8,128)(2,1)S(1)} %get-tuple-element.136.normed, bf16[256,2048]{1,0:T(8,128)(2,1)} %copy-done.21, ...), custom_call_target="tpu_custom_call" | custom-call | bytes 12177000 | tf_op jit(solution)/shard_map/attend/pallas_call | solution.py:53
  63.3 1.8 collective-permute-start.11
  66.6 8.7 %collective-permute-done.5.refs_2_ = bf16[256,1024]{1,0:T(8,128)(2,1)S(1)} collective-permute-done((bf16[256,1024]{1,0:T(8,128)(2,1)S(1)}, bf16[256,1024]{1,0:T(8,128)(2,1)S(1)}, u32[]{:S(2)}, u32[]{:S(2)}) %collective-permute-start.5) | collective-permute-done | bytes 524320 | tf_op jit(solution)/shard_map/ppermute | solution.py:800
  76.6 2.2 collective-permute-done.7.refs_4_
  80.0 12.1 %attend.3 = (bf16[512,1536]{1,0:T(8,128)(2,1)}, bf16[512,512]{1,0:T(8,128)(2,1)}, bf16[8,512,512]{2,1,0:T(8,128)(2,1)}, f32[2,4,512]{2,1,0:T(4,128)S(1)}, f32[512,1024]{1,0:T(8,128)S(1)}) custom-call(bf16[512,1024]{1,0:T(8,128)(2,1)S(1)} %get-tuple-element.136.normed, bf16[256,2048]{1,0:T(8,128)(2,1)} %collective-permute-done.3.refs_0_, ...), custom_call_target="tpu_custom_call" | custom-call | bytes 12177000 | tf_op jit(solution)/shard_map/attend/pallas_call | solution.py:53
  92.2 4.9 %second_norm.1 = (f32[512,1024]{1,0:T(8,128)}, bf16[512,1024]{1,0:T(8,128)(2,1)S(1)}, bf16[1024,512]{1,0:T(8,128)(2,1)}) custom-call(s32[4]{0:T(128)S(1)} %broadcast_multiply_fusion.meta, bf16[512,1024]{1,0:T(8,128)(2,1)} %x.3, f32[512,1024]{1,0:T(8,128)S(1)} %copy-done.9, f32[512,1024]{1,0:T(8,128)S(1)} %get-tuple-element.144.refs_1_, ...), custom_call_target="tpu_custom_call" | custom-call | bytes 5535000 | tf_op jit(solution)/shard_map/second_norm/pallas_call | solution.py:53
  97.1 16.6 %collective-permute-done.11.refs_4_ = bf16[256,2048]{1,0:T(8,128)(2,1)} collective-permute-done((bf16[256,2048]{1,0:T(8,128)(2,1)}, bf16[256,2048]{1,0:T(8,128)(2,1)}, u32[]{:S(2)}, u32[]{:S(2)}) %collective-permute-start.11) | collective-permute-done | bytes 1048608 | tf_op jit(solution)/shard_map/ppermute | solution.py:800
  113.7 1.9 slice.150
  117.1 1.9 slice.151
  119.5 4.1 all-gather.3.cloned.1.call-done
  123.6 6.6 %up.2 = (bf16[512,2048]{1,0:T(8,128)(2,1)S(1)}, bf16[512,2048]{1,0:T(8,128)(2,1)S(1)}) custom-call(s32[6]{0:T(128)S(1)} %pad_add_fusion.spots, bf16[512,1024]{1,0:T(8,128)(2,1)S(1)} %get-tuple-element.156.normed, bf16[2,4,256,2048]{3,2,1,0:T(8,128)(2,1)} %bitcast.78, bf16[2,4,256,2048]{3,2,1,0:T(8,128)(2,1)} %bitcast.79, bf16[2,4,256,2048]{3,2,1,0:T(8,128)(2,1)} %bitcast.80, ...), custom_call_target="tpu_custom_call" | custom-call | bytes 6642000 | tf_op jit(solution)/shard_map/up/pallas_call | solution.py:53
  131.5 6.7 %up.3 = (bf16[512,2048]{1,0:T(8,128)(2,1)S(1)}, bf16[512,2048]{1,0:T(8,128)(2,1)S(1)}) custom-call(s32[6]{0:T(128)S(1)} %pad_add_fusion.spots, bf16[512,1024]{1,0:T(8,128)(2,1)S(1)} %get-tuple-element.156.normed, bf16[2,4,256,2048]{3,2,1,0:T(8,128)(2,1)} %bitcast.82, bf16[2,4,256,2048]{3,2,1,0:T(8,128)(2,1)} %bitcast.83, bf16[2,4,256,2048]{3,2,1,0:T(8,128)(2,1)} %bitcast.84, ...), custom_call_target="tpu_custom_call" | custom-call | bytes 6642000 | tf_op jit(solution)/shard_map/up/pallas_call | solution.py:53
  138.3 9.2 %weight_grads.4 = bf16[2,4,256,2048]{3,2,1,0:T(8,128)(2,1)} custom-call(s32[6]{0:T(128)S(1)} %pad_add_fusion.spots, bf16[1024,512]{1,0:T(8,128)(2,1)} %get-tuple-element.160.left, bf16[512,2048]{1,0:T(8,128)(2,1)S(1)} %get-tuple-element.155.refs_0_.hidden, bf16[512,2048]{1,0:T(8,128)(2,1)S(1)} %get-tuple-element.157.refs_1_.hidden), custom_call_target="tpu_custom_call" | custom-call | bytes 11070000 | tf_op jit(solution)/shard_map/weight_grads/pallas_call | solution.py:53
  156.3 14.5 %mlp_back.2 = (bf16[512,2048]{1,0:T(8,128)(2,1)}, f32[1,2048]{1,0:T(1,128)S(1)}, f32[512,1024]{1,0:T(8,128)}, f32[512,1024]{1,0:T(8,128)S(1)}) custom-call(s32[6]{0:T(128)S(1)} %pad_add_fusion.spots, bf16[512,1024]{1,0:T(8,128)(2,1)} %get-tuple-element.164.low, bf16[512,2048]{1,0:T(8,128)(2,1)S(1)} %copy-done.1, bf16[512,2048]{1,0:T(8,128)(2,1)S(1)} %copy-done.11, ...), custom_call_target="tpu_custom_call" | custom-call | bytes 14391000 | tf_op jit(solution)/shard_map/mlp_back/pallas_call | solution.py:53
  173.4 13.8 %mlp_back.3 = (bf16[512,2048]{1,0:T(8,128)(2,1)}, f32[1,2048]{1,0:T(1,128)S(1)}, f32[512,1024]{1,0:T(8,128)}, f32[512,1024]{1,0:T(8,128)S(1)}) custom-call(s32[6]{0:T(128)S(1)} %pad_add_fusion.spots, bf16[512,1024]{1,0:T(8,128)(2,1)} %get-tuple-element.164.low, bf16[512,2048]{1,0:T(8,128)(2,1)S(1)} %get-tuple-element.157.refs_1_.hidden, ...), custom_call_target="tpu_custom_call" | custom-call | bytes 14391000 | tf_op jit(solution)/shard_map/mlp_back/pallas_call | solution.py:53
  190.1 11.5 %weight_grads.5 = (bf16[256,2048]{1,0:T(8,128)(2,1)}, bf16[256,1024]{1,0:T(8,128)(2,1)}, bf16[256,2048]{1,0:T(8,128)(2,1)}, bf16[256,1024]{1,0:T(8,128)(2,1)}, b...) custom-call(bf16[1024,512]{1,0:T(8,128)(2,1)} %get-tuple-element.167, ...), custom_call_target="tpu_custom_call" | custom-call | bytes 11070000 | tf_op jit(solution)/shard_map/weight_grads/pallas_call | solution.py:53
  204.6 5.8 %second_norm_back.1 = (f32[512,1024]{1,0:T(8,128)}, bf16[512,1024]{1,0:T(8,128)(2,1)S(1)}, bf16[1024,512]{1,0:T(8,128)(2,1)}, f32[4,1024]{1,0:T(4,128)S(1)}) custom-call(s32[4]{0:T(128)S(1)} %broadcast_multiply_fusion.meta, f32[512,1024]{1,0:T(8,128)} %get-tuple-element.169.middle, bf16[512,1024]{1,0:T(8,128)(2,1)} %get-tuple-element.164.low, ...), custom_call_target="tpu_custom_call" | custom-call | bytes 6642000 | tf_op jit(solution)/shard_map/second_norm_back/pallas_call | solution.py:53
  210.4 2.7 add_convert_fusion.2
  214.3 2.5 add_convert_fusion.1
  218.5 13.7 %attend_back.2 = (bf16[512,1536]{1,0:T(8,128)(2,1)S(1)}, f32[1,1536]{1,0:T(1,128)S(1)}, f32[512,1024]{1,0:T(8,128)}) custom-call(bf16[512,1024]{1,0:T(8,128)(2,1)S(1)} %get-tuple-element.197.grad_low, bf16[256,2048]{1,0:T(8,128)(2,1)} %collective-permute-done.3.refs_0_, bf16[256,2048]{1,0:T(8,128)(2,1)} %copy-done.22, bf16[256,1024]{1,0:T(8,128)(2,1)} %copy-done.23, ...), custom_call_target="tpu_custom_call" | custom-call | bytes 15498000 | tf_op jit(solution)/shard_map/attend_back/pallas_call | solution.py:53
  235.1 7.7 %weight_grads.6 = (bf16[256,1024]{1,0:T(8,128)(2,1)}, bf16[256,1024]{1,0:T(8,128)(2,1)}, bf16[256,2048]{1,0:T(8,128)(2,1)}, bf16[256,1024]{1,0:T(8,128)(2,1)}, b...) custom-call(bf16[1024,512]{1,0:T(8,128)(2,1)} %get-tuple-element.230.refs_0_, ...), custom_call_target="tpu_custom_call" | custom-call | bytes 11070000 | tf_op jit(solution)/shard_map/weight_grads/pallas_call | solution.py:53
  242.9 2.3 add_convert_fusion.8
  246.9 2.3 add_convert_fusion.7
  250.4 13.3 %attend_back.3 = (bf16[512,1536]{1,0:T(8,128)(2,1)S(1)}, f32[1,1536]{1,0:T(1,128)S(1)}, f32[512,1024]{1,0:T(8,128)}) custom-call(bf16[512,1024]{1,0:T(8,128)(2,1)S(1)} %get-tuple-element.197.grad_low, bf16[256,2048]{1,0:T(8,128)(2,1)} %copy-done.21, bf16[256,2048]{1,0:T(8,128)(2,1)} %collective-permute-done.refs_1_, ...), custom_call_target="tpu_custom_call" | custom-call | bytes 15498000 | tf_op jit(solution)/shard_map/attend_back/pallas_call | solution.py:53
  263.7 2.4 collective-permute-start.28
  271.1 7.8 %collective-permute-done.28 = bf16[128,1024]{1,0:T(8,128)(2,1)} collective-permute-done((bf16[128,1024]{1,0:T(8,128)(2,1)S(1)}, bf16[128,1024]{1,0:T(8,128)(2,1)}, u32[]{:S(2)}, u32[]{:S(2)}) %collective-permute-start.28) | collective-permute-done | bytes 262176 | tf_op jit(solution)/shard_map/ppermute | solution.py:800
  283.2 2.1 broadcast_select_fusion.8
  285.3 3.0 collective-permute-start.34
  288.4 8.0 %finish.1 = (bf16[512,1024]{1,0:T(8,128)(2,1)}, bf16[512,1024]{1,0:T(8,128)(2,1)}, f32[2,1024]{1,0:T(2,128)S(1)}) custom-call(s32[4]{0:T(128)S(1)} %broadcast_multiply_fusion.meta, bf16[512,1024]{1,0:T(8,128)(2,1)} %x.3, f32[512,1024]{1,0:T(8,128)} %get-tuple-element.169.middle, f32[512,1024]{1,0:T(8,128)} %get-tuple-element.174.grad, ...), custom_call_target="tpu_custom_call" | custom-call | bytes 8856000 | tf_op jit(solution)/shard_map/finish/pallas_call | solution.py:53
  298.6 6.3 %weight_grads.7 = (bf16[256,1024]{1,0:T(8,128)(2,1)}, bf16[256,1024]{1,0:T(8,128)(2,1)}, bf16[256,2048]{1,0:T(8,128)(2,1)}, bf16[256,1024]{1,0:T(8,128)(2,1)}, b...) custom-call(bf16[1024,512]{1,0:T(8,128)(2,1)} %get-tuple-element.230.refs_0_, ...), custom_call_target="tpu_custom_call" | custom-call | bytes 11070000 | tf_op jit(solution)/shard_map/weight_grads/pallas_call | solution.py:53
  310.6 13.8 %collective-permute-done.38 = bf16[128,1024]{1,0:T(8,128)(2,1)S(1)} collective-permute-done((bf16[128,1024]{1,0:T(8,128)(2,1)S(1)}, bf16[128,1024]{1,0:T(8,128)(2,1)S(1)}, u32[]{:S(2)}, u32[]{:S(2)}) %collective-permute-start.38) | collective-permute-done | bytes 262176 | tf_op jit(solution)/shard_map/ppermute | solution.py:800
  326.0 11.8 %collective-permute-done.45 = bf16[256,1024]{1,0:T(8,128)(2,1)S(1)} collective-permute-done((bf16[256,1024]{1,0:T(8,128)(2,1)S(1)}, bf16[256,1024]{1,0:T(8,128)(2,1)S(1)}, u32[]{:S(2)}, u32[]{:S(2)}) %collective-permute-start.45) | collective-permute-done | bytes 524320 | tf_op jit(solution)/shard_map/ppermute | solution.py:800
  338.5 2.1 collective-permute-start.48
  342.1 2.7 collective-permute-done.40
  344.8 1.9 collective-permute-start.41
  349.8 7.9 %collective-permute-done.42 = f32[96,128]{1,0:T(8,128)S(1)} collective-permute-done((f32[96,128]{1,0:T(8,128)S(1)}, f32[96,128]{1,0:T(8,128)S(1)}, u32[]{:S(2)}, u32[]{:S(2)}) %collective-permute-start.42) | collective-permute-done | bytes 49184 | tf_op jit(solution)/shard_map/ppermute | solution.py:800
  357.8 3.8 collective-permute-start.43
  363.2 3.8 turned.5
  367.0 2.2 collective-permute-done.43
  369.2 4.9 %collective-permute-done.50 = bf16[128,1024]{1,0:T(8,128)(2,1)S(1)} collective-permute-done((bf16[128,1024]{1,0:T(8,128)(2,1)S(1)}, bf16[128,1024]{1,0:T(8,128)(2,1)S(1)}, u32[]{:S(2)}, u32[]{:S(2)}) %collective-permute-start.50) | collective-permute-done | bytes 262176 | tf_op jit(solution)/shard_map/ppermute | solution.py:800
  376.2 12.0 %collective-permute-done.51 = bf16[128,1024]{1,0:T(8,128)(2,1)S(1)} collective-permute-done((bf16[128,1024]{1,0:T(8,128)(2,1)S(1)}, bf16[128,1024]{1,0:T(8,128)(2,1)S(1)}, u32[]{:S(2)}, u32[]{:S(2)}) %collective-permute-start.51) | collective-permute-done | bytes 262176 | tf_op jit(solution)/shard_map/ppermute | solution.py:800
  390.9 10.5 %collective-permute-done.52 = bf16[256,1024]{1,0:T(8,128)(2,1)S(1)} collective-permute-done((bf16[256,1024]{1,0:T(8,128)(2,1)S(1)}, bf16[256,1024]{1,0:T(8,128)(2,1)S(1)}, u32[]{:S(2)}, u32[]{:S(2)}) %collective-permute-start.52) | collective-permute-done | bytes 524320 | tf_op jit(solution)/shard_map/ppermute | solution.py:800
  402.8 2.0 turned.4
  (278 shorter events, 81.1 us)
Async XLA Ops:
  7.2 116.5 %all-gather.3.cloned.1.call-start = ((), (), s32[]{:S(2)}) async-start(), calls=%async_computation.2 | async-start | bytes 9437184 | tf_op jit(solution)/shard_map/all_gather | solution.py:878
  13.8 26.3 %collective-permute-start.1 = (bf16[256,2048]{1,0:T(8,128)(2,1)S(1)}, bf16[256,2048]{1,0:T(8,128)(2,1)}, u32[]{:S(2)}, u32[]{:S(2)}) collective-permute-start(bf16[256,2048]{1,0:T(8,128)(2,1)S(1)} %reshape.158.refs_0_), channel_id=1, source_target_pairs={{0,2},{1,3},{2,0},{3,1},{4,6},{5,7},{6,4},{7,5},{8,10},{9,11},{10,... | collective-permute-start | bytes 3145736 | tf_op jit(solution)/shard_map/ppermute | solution.py:800
  16.8 24.7 %collective-permute-start.3 = (bf16[256,2048]{1,0:T(8,128)(2,1)S(1)}, bf16[256,2048]{1,0:T(8,128)(2,1)}, u32[]{:S(2)}, u32[]{:S(2)}) collective-permute-start(bf16[256,2048]{1,0:T(8,128)(2,1)S(1)} %reshape.158.refs_0_), channel_id=1, source_target_pairs={{0,4},{4,0},{1,5},{5,1},{2,6},{6,2},{3,7},{7,3},{8,12},{12,8},{9,1... | collective-permute-start | bytes 3145736 | tf_op jit(solution)/shard_map/ppermute | solution.py:800
  41.6 190.7 %reduce-scatter.2.cloned.1.call-start = ((), (), s32[]{:S(2)}) async-start(), calls=%async_computation.1 | async-start | bytes 9437184 | tf_op jit(solution)/shard_map/reduce_scatter | solution.py:1066
  41.9 9.3 %collective-permute-start = (bf16[256,2048]{1,0:T(8,128)(2,1)S(1)}, bf16[256,2048]{1,0:T(8,128)(2,1)}, u32[]{:S(2)}, u32[]{:S(2)}) collective-permute-start(bf16[256,2048]{1,0:T(8,128)(2,1)S(1)} %reshape.158.refs_0_), channel_id=1, source_target_pairs={{0,1},{1,0},{2,3},{3,2},{4,5},{5,4},{6,7},{7,6},{8,9},{9,8},{10,11... | collective-permute-start | bytes 3145736 | tf_op jit(solution)/shard_map/ppermute | solution.py:800
  42.0 9.2 %collective-permute-start.2 = (bf16[256,2048]{1,0:T(8,128)(2,1)}, bf16[256,2048]{1,0:T(8,128)(2,1)}, u32[]{:S(2)}, u32[]{:S(2)}) collective-permute-start(bf16[256,2048]{1,0:T(8,128)(2,1)} %collective-permute-done.1.refs_2_), channel_id=1, source_target_pairs={{0,1},{1,0},{2,3},{3,2},{4,5},{5,4},{6,7},{7,6},{8,9},{9,8},{10,11... | collective-permute-start | bytes 3145736 | tf_op jit(solution)/shard_map/ppermute | solution.py:800
  50.4 24.9 %collective-permute-start.5 = (bf16[256,1024]{1,0:T(8,128)(2,1)S(1)}, bf16[256,1024]{1,0:T(8,128)(2,1)S(1)}, u32[]{:S(2)}, u32[]{:S(2)}) collective-permute-start(bf16[256,1024]{1,0:T(8,128)(2,1)S(1)} %slice.144), channel_id=1, source_target_pairs={{0,2},{1,3},{2,0},{3,1},{4,6},{5,7},{6,4},{7,5},{8,10},{9,11},{10,... | collective-permute-start | bytes 1572872 | tf_op jit(solution)/shard_map/ppermute | solution.py:800
  51.0 25.1 %collective-permute-start.6 = (bf16[256,1024]{1,0:T(8,128)(2,1)S(1)}, bf16[256,1024]{1,0:T(8,128)(2,1)}, u32[]{:S(2)}, u32[]{:S(2)}) collective-permute-start(bf16[256,1024]{1,0:T(8,128)(2,1)S(1)} %slice.145), channel_id=1, source_target_pairs={{0,4},{4,0},{1,5},{5,1},{2,6},{6,2},{3,7},{7,3},{8,12},{12,8},{9,1... | collective-permute-start | bytes 1572872 | tf_op jit(solution)/shard_map/ppermute | solution.py:800
  63.3 15.8 %collective-permute-start.4 = (bf16[256,2048]{1,0:T(8,128)(2,1)}, bf16[256,2048]{1,0:T(8,128)(2,1)S(1)}, u32[]{:S(2)}, u32[]{:S(2)}) collective-permute-start(bf16[256,2048]{1,0:T(8,128)(2,1)} %collective-permute-done.3.refs_0_), channel_id=1, source_target_pairs={{0,1},{1,0},{2,3},{3,2},{4,5},{5,4},{6,7},{7,6},{8,9},{9,8},{10,11... | collective-permute-start | bytes 3145736 | tf_op jit(solution)/shard_map/ppermute | solution.py:800
  63.3 50.4 %collective-permute-start.11 = (bf16[256,2048]{1,0:T(8,128)(2,1)}, bf16[256,2048]{1,0:T(8,128)(2,1)}, u32[]{:S(2)}, u32[]{:S(2)}) collective-permute-start(bf16[256,2048]{1,0:T(8,128)(2,1)} %turned.3.refs_4_), channel_id=1, source_target_pairs={{0,4},{4,0},{1,5},{5,1},{2,6},{6,2},{3,7},{7,3},{8,12},{12,8},{9,1... | collective-permute-start | bytes 3145736 | tf_op jit(solution)/shard_map/ppermute | solution.py:800
  65.1 52.0 %collective-permute-start.10 = (bf16[256,2048]{1,0:T(8,128)(2,1)}, bf16[256,2048]{1,0:T(8,128)(2,1)}, u32[]{:S(2)}, u32[]{:S(2)}) collective-permute-start(bf16[256,2048]{1,0:T(8,128)(2,1)} %turned.3.refs_4_), channel_id=1, source_target_pairs={{0,2},{1,3},{2,0},{3,1},{4,6},{5,7},{6,4},{7,5},{8,10},{9,11},{10,... | collective-permute-start | bytes 3145736 | tf_op jit(solution)/shard_map/ppermute | solution.py:800
  115.6 22.7 %collective-permute-start.12 = (bf16[256,1024]{1,0:T(8,128)(2,1)}, bf16[256,1024]{1,0:T(8,128)(2,1)}, u32[]{:S(2)}, u32[]{:S(2)}) collective-permute-start(bf16[256,1024]{1,0:T(8,128)(2,1)} %slice.150), channel_id=1, source_target_pairs={{0,2},{1,3},{2,0},{3,1},{4,6},{5,7},{6,4},{7,5},{8,10},{9,11},{10,... | collective-permute-start | bytes 1572872 | tf_op jit(solution)/shard_map/ppermute | solution.py:800
  118.9 19.3 %collective-permute-start.13 = (bf16[256,1024]{1,0:T(8,128)(2,1)}, bf16[256,1024]{1,0:T(8,128)(2,1)}, u32[]{:S(2)}, u32[]{:S(2)}) collective-permute-start(bf16[256,1024]{1,0:T(8,128)(2,1)} %slice.151), channel_id=1, source_target_pairs={{0,4},{4,0},{1,5},{5,1},{2,6},{6,2},{3,7},{7,3},{8,12},{12,8},{9,1... | collective-permute-start | bytes 1572872 | tf_op jit(solution)/shard_map/ppermute | solution.py:800
  148.1 23.9 %collective-permute-start.16 = (bf16[256,2048]{1,0:T(8,128)(2,1)}, bf16[256,2048]{1,0:T(8,128)(2,1)S(1)}, u32[]{:S(2)}, u32[]{:S(2)}) collective-permute-start(bf16[256,2048]{1,0:T(8,128)(2,1)} %collective-permute-done.11.refs_4_), channel_id=1, source_target_pairs={{0,1},{1,0},{2,3},{3,2},{4,5},{5,4},{6,7},{7,6},{8,9},{9,8},{10,11... | collective-permute-start | bytes 3145736 | tf_op jit(solution)/shard_map/ppermute | solution.py:800
  148.4 23.7 %collective-permute-start.17 = (bf16[256,1024]{1,0:T(8,128)(2,1)}, bf16[256,1024]{1,0:T(8,128)(2,1)S(1)}, u32[]{:S(2)}, u32[]{:S(2)}) collective-permute-start(bf16[256,1024]{1,0:T(8,128)(2,1)} %collective-permute-done.12.refs_6_), channel_id=1, source_target_pairs={{0,1},{1,0},{2,3},{3,2},{4,5},{5,4},{6,7},{7,6},{8,9},{9,8},{10,11... | collective-permute-start | bytes 1572872 | tf_op jit(solution)/shard_map/ppermute | solution.py:800
  148.6 23.4 %collective-permute-start.18 = (bf16[256,1024]{1,0:T(8,128)(2,1)}, bf16[256,1024]{1,0:T(8,128)(2,1)S(1)}, u32[]{:S(2)}, u32[]{:S(2)}) collective-permute-start(bf16[256,1024]{1,0:T(8,128)(2,1)} %collective-permute-done.13.refs_7_), channel_id=1, source_target_pairs={{0,1},{1,0},{2,3},{3,2},{4,5},{5,4},{6,7},{7,6},{8,9},{9,8},{10,11... | collective-permute-start | bytes 1572872 | tf_op jit(solution)/shard_map/ppermute | solution.py:800
  201.6 8.8 %collective-permute-start.19 = (bf16[256,2048]{1,0:T(8,128)(2,1)}, bf16[256,2048]{1,0:T(8,128)(2,1)}, u32[]{:S(2)}, u32[]{:S(2)}) collective-permute-start(bf16[256,2048]{1,0:T(8,128)(2,1)} %get-tuple-element.175), channel_id=1, source_target_pairs={{0,1},{1,0},{2,3},{3,2},{4,5},{5,4},{6,7},{7,6},{8,9},{9,8},{10,11... | collective-permute-start | bytes 3145736 | tf_op jit(solution)/shard_map/ppermute | solution.py:800
  201.9 11.2 %collective-permute-start.20 = (bf16[256,2048]{1,0:T(8,128)(2,1)}, bf16[256,2048]{1,0:T(8,128)(2,1)}, u32[]{:S(2)}, u32[]{:S(2)}) collective-permute-start(bf16[256,2048]{1,0:T(8,128)(2,1)} %get-tuple-element.178), channel_id=1, source_target_pairs={{0,1},{1,0},{2,3},{3,2},{4,5},{5,4},{6,7},{7,6},{8,9},{9,8},{10,11... | collective-permute-start | bytes 3145736 | tf_op jit(solution)/shard_map/ppermute | solution.py:800
  202.3 40.6 %collective-permute-start.21 = (bf16[256,3072]{1,0:T(8,128)(2,1)}, bf16[256,3072]{1,0:T(8,128)(2,1)}, u32[]{:S(2)}, u32[]{:S(2)}) collective-permute-start(bf16[256,3072]{1,0:T(8,128)(2,1)} %get-tuple-element.189), channel_id=1, source_target_pairs={{0,1},{1,0},{2,3},{3,2},{4,5},{5,4},{6,7},{7,6},{8,9},{9,8},{10,11... | collective-permute-start | bytes 4718600 | tf_op jit(solution)/shard_map/ppermute | solution.py:800
  202.6 43.7 %collective-permute-start.23 = (bf16[256,1024]{1,0:T(8,128)(2,1)}, bf16[256,1024]{1,0:T(8,128)(2,1)}, u32[]{:S(2)}, u32[]{:S(2)}) collective-permute-start(bf16[256,1024]{1,0:T(8,128)(2,1)} %get-tuple-element.193), channel_id=1, source_target_pairs={{0,1},{1,0},{2,3},{3,2},{4,5},{5,4},{6,7},{7,6},{8,9},{9,8},{10,11... | collective-permute-start | bytes 1572872 | tf_op jit(solution)/shard_map/ppermute | solution.py:800
  213.1 29.8 %collective-permute-start.22 = (bf16[256,2048]{1,0:T(8,128)(2,1)}, bf16[256,2048]{1,0:T(8,128)(2,1)}, u32[]{:S(2)}, u32[]{:S(2)}) collective-permute-start(bf16[256,2048]{1,0:T(8,128)(2,1)} %add_convert_fusion.2), channel_id=1, source_target_pairs={{0,2},{1,3},{2,0},{3,1},{4,6},{5,7},{6,4},{7,5},{8,10},{9,11},{10,... | collective-permute-start | bytes 3145736 | tf_op jit(solution)/shard_map/ppermute | solution.py:800
  216.8 29.5 %collective-permute-start.24 = (bf16[256,2048]{1,0:T(8,128)(2,1)}, bf16[256,2048]{1,0:T(8,128)(2,1)}, u32[]{:S(2)}, u32[]{:S(2)}) collective-permute-start(bf16[256,2048]{1,0:T(8,128)(2,1)} %add_convert_fusion.1), channel_id=1, source_target_pairs={{0,4},{4,0},{1,5},{5,1},{2,6},{6,2},{3,7},{7,3},{8,12},{12,8},{9,1... | collective-permute-start | bytes 3145736 | tf_op jit(solution)/shard_map/ppermute | solution.py:800
  233.6 16.5 %collective-permute-start.25 = (bf16[256,1024]{1,0:T(8,128)(2,1)S(1)}, bf16[256,1024]{1,0:T(8,128)(2,1)S(1)}, u32[]{:S(2)}, u32[]{:S(2)}) collective-permute-start(bf16[256,1024]{1,0:T(8,128)(2,1)S(1)} %get-tuple-element.271), channel_id=1, source_target_pairs={{0,8},{8,0},{16,24},{24,16},{1,9},{9,1},{17,25},{25,17},{2,10},{10... | collective-permute-start | bytes 1572872 | tf_op jit(solution)/shard_map/ppermute | solution.py:800
  245.2 36.4 %collective-permute-start.29 = (bf16[256,1024]{1,0:T(8,128)(2,1)}, bf16[256,1024]{1,0:T(8,128)(2,1)}, u32[]{:S(2)}, u32[]{:S(2)}) collective-permute-start(bf16[256,1024]{1,0:T(8,128)(2,1)} %add_convert_fusion.8), channel_id=1, source_target_pairs={{0,4},{4,0},{1,5},{5,1},{2,6},{6,2},{3,7},{7,3},{8,12},{12,8},{9,1... | collective-permute-start | bytes 1572872 | tf_op jit(solution)/shard_map/ppermute | solution.py:800
  246.3 17.4 %collective-permute-start.26 = (bf16[256,1024]{1,0:T(8,128)(2,1)S(1)}, bf16[256,1024]{1,0:T(8,128)(2,1)}, u32[]{:S(2)}, u32[]{:S(2)}) collective-permute-start(bf16[256,1024]{1,0:T(8,128)(2,1)S(1)} %copy-done.46), channel_id=1, source_target_pairs={{0,1},{1,0},{2,3},{3,2},{4,5},{5,4},{6,7},{7,6},{8,9},{9,8},{10,11... | collective-permute-start | bytes 1572872 | tf_op jit(solution)/shard_map/ppermute | solution.py:800
  246.4 22.0 %collective-permute-start.27 = (bf16[256,2048]{1,0:T(8,128)(2,1)}, bf16[256,2048]{1,0:T(8,128)(2,1)}, u32[]{:S(2)}, u32[]{:S(2)}) collective-permute-start(bf16[256,2048]{1,0:T(8,128)(2,1)} %get-tuple-element.205), channel_id=1, source_target_pairs={{0,1},{1,0},{2,3},{3,2},{4,5},{5,4},{6,7},{7,6},{8,9},{9,8},{10,11... | collective-permute-start | bytes 3145736 | tf_op jit(solution)/shard_map/ppermute | solution.py:800
  249.2 32.4 %collective-permute-start.30 = (bf16[256,1024]{1,0:T(8,128)(2,1)}, bf16[256,1024]{1,0:T(8,128)(2,1)}, u32[]{:S(2)}, u32[]{:S(2)}) collective-permute-start(bf16[256,1024]{1,0:T(8,128)(2,1)} %add_convert_fusion.7), channel_id=1, source_target_pairs={{0,2},{1,3},{2,0},{3,1},{4,6},{5,7},{6,4},{7,5},{8,10},{9,11},{10,... | collective-permute-start | bytes 1572872 | tf_op jit(solution)/shard_map/ppermute | solution.py:800
  250.1 46.3 %collective-permute-start.31 = (bf16[256,1024]{1,0:T(8,128)(2,1)}, bf16[256,1024]{1,0:T(8,128)(2,1)}, u32[]{:S(2)}, u32[]{:S(2)}) collective-permute-start(bf16[256,1024]{1,0:T(8,128)(2,1)} %get-tuple-element.226), channel_id=1, source_target_pairs={{0,1},{1,0},{2,3},{3,2},{4,5},{5,4},{6,7},{7,6},{8,9},{9,8},{10,11... | collective-permute-start | bytes 1572872 | tf_op jit(solution)/shard_map/ppermute | solution.py:800
  263.7 15.2 %collective-permute-start.28 = (bf16[128,1024]{1,0:T(8,128)(2,1)S(1)}, bf16[128,1024]{1,0:T(8,128)(2,1)}, u32[]{:S(2)}, u32[]{:S(2)}) collective-permute-start(bf16[128,1024]{1,0:T(8,128)(2,1)S(1)} %get-tuple-element.277), channel_id=1, source_target_pairs={{0,16},{8,24},{16,0},{24,8},{1,17},{9,25},{17,1},{25,9},{2,18},{10... | collective-permute-start | bytes 786440 | tf_op jit(solution)/shard_map/ppermute | solution.py:800
  268.4 28.0 %collective-permute-start.32 = (bf16[256,1024]{1,0:T(8,128)(2,1)S(1)}, bf16[256,1024]{1,0:T(8,128)(2,1)S(1)}, u32[]{:S(2)}, u32[]{:S(2)}) collective-permute-start(bf16[256,1024]{1,0:T(8,128)(2,1)S(1)} %add_convert_fusion.6), channel_id=1, source_target_pairs={{0,2},{1,3},{2,0},{3,1},{4,6},{5,7},{6,4},{7,5},{8,10},{9,11},{10,... | collective-permute-start | bytes 1572872 | tf_op jit(solution)/shard_map/ppermute | solution.py:800
  278.9 30.2 %collective-permute-start.37 = (bf16[256,2048]{1,0:T(8,128)(2,1)S(1)}, bf16[256,2048]{1,0:T(8,128)(2,1)S(1)}, u32[]{:S(2)}, u32[]{:S(2)}) collective-permute-start(bf16[256,2048]{1,0:T(8,128)(2,1)S(1)} %add_convert_fusion), channel_id=1, source_target_pairs={{0,4},{4,0},{1,5},{5,1},{2,6},{6,2},{3,7},{7,3},{8,12},{12,8},{9,1... | collective-permute-start | bytes 3145736 | tf_op jit(solution)/shard_map/ppermute | solution.py:800
  281.6 16.8 %collective-permute-start.33 = (bf16[128,1024]{1,0:T(8,128)(2,1)S(1)}, bf16[128,1024]{1,0:T(8,128)(2,1)S(1)}, u32[]{:S(2)}, u32[]{:S(2)}) collective-permute-start(bf16[128,1024]{1,0:T(8,128)(2,1)S(1)} %add_convert_fusion.11), channel_id=1, source_target_pairs={{0,16},{8,24},{16,0},{24,8},{1,17},{9,25},{17,1},{25,9},{2,18},{10... | collective-permute-start | bytes 786440 | tf_op jit(solution)/shard_map/ppermute | solution.py:800
  285.3 20.0 %collective-permute-start.34 = (bf16[256,1024]{1,0:T(8,128)(2,1)S(1)}, bf16[256,1024]{1,0:T(8,128)(2,1)S(1)}, u32[]{:S(2)}, u32[]{:S(2)}) collective-permute-start(bf16[256,1024]{1,0:T(8,128)(2,1)S(1)} %broadcast_select_fusion.9), channel_id=1, source_target_pairs={{0,8},{8,0},{16,24},{24,16},{1,9},{9,1},{17,25},{25,17},{2,10},{10... | collective-permute-start | bytes 1572872 | tf_op jit(solution)/shard_map/ppermute | solution.py:800
  297.8 27.8 %collective-permute-start.47 = (bf16[256,1024]{1,0:T(8,128)(2,1)S(1)}, bf16[256,1024]{1,0:T(8,128)(2,1)S(1)}, u32[]{:S(2)}, u32[]{:S(2)}) collective-permute-start(bf16[256,1024]{1,0:T(8,128)(2,1)S(1)} %add_convert_fusion.5), channel_id=1, source_target_pairs={{0,4},{4,0},{1,5},{5,1},{2,6},{6,2},{3,7},{7,3},{8,12},{12,8},{9,1... | collective-permute-start | bytes 1572872 | tf_op jit(solution)/shard_map/ppermute | solution.py:800
  305.4 20.3 %collective-permute-start.44 = (bf16[256,2048]{1,0:T(8,128)(2,1)}, bf16[256,2048]{1,0:T(8,128)(2,1)S(1)}, u32[]{:S(2)}, u32[]{:S(2)}) collective-permute-start(bf16[256,2048]{1,0:T(8,128)(2,1)} %get-tuple-element.242), channel_id=1, source_target_pairs={{0,1},{1,0},{2,3},{3,2},{4,5},{5,4},{6,7},{7,6},{8,9},{9,8},{10,11... | collective-permute-start | bytes 3145736 | tf_op jit(solution)/shard_map/ppermute | solution.py:800
  307.0 42.8 %collective-permute-start.54 = (bf16[256,1024]{1,0:T(8,128)(2,1)S(1)}, bf16[256,1024]{1,0:T(8,128)(2,1)S(1)}, u32[]{:S(2)}, u32[]{:S(2)}) collective-permute-start(bf16[256,1024]{1,0:T(8,128)(2,1)S(1)} %maximum_select_fusion), channel_id=1, source_target_pairs={{0,8},{8,0},{16,24},{24,16},{1,9},{9,1},{17,25},{25,17},{2,10},{10... | collective-permute-start | bytes 1572872 | tf_op jit(solution)/shard_map/ppermute | solution.py:800
  307.8 16.6 %collective-permute-start.38 = (bf16[128,1024]{1,0:T(8,128)(2,1)S(1)}, bf16[128,1024]{1,0:T(8,128)(2,1)S(1)}, u32[]{:S(2)}, u32[]{:S(2)}) collective-permute-start(bf16[128,1024]{1,0:T(8,128)(2,1)S(1)} %get-tuple-element.275), channel_id=1, source_target_pairs={{0,16},{8,24},{16,0},{24,8},{1,17},{9,25},{17,1},{25,9},{2,18},{10... | collective-permute-start | bytes 786440 | tf_op jit(solution)/shard_map/ppermute | solution.py:800
  309.1 28.7 %collective-permute-start.46 = (bf16[256,1024]{1,0:T(8,128)(2,1)S(1)}, bf16[256,1024]{1,0:T(8,128)(2,1)S(1)}, u32[]{:S(2)}, u32[]{:S(2)}) collective-permute-start(bf16[256,1024]{1,0:T(8,128)(2,1)S(1)} %add_convert_fusion.4), channel_id=1, source_target_pairs={{0,2},{1,3},{2,0},{3,1},{4,6},{5,7},{6,4},{7,5},{8,10},{9,11},{10,... | collective-permute-start | bytes 1572872 | tf_op jit(solution)/shard_map/ppermute | solution.py:800
  324.4 13.4 %collective-permute-start.45 = (bf16[256,1024]{1,0:T(8,128)(2,1)S(1)}, bf16[256,1024]{1,0:T(8,128)(2,1)S(1)}, u32[]{:S(2)}, u32[]{:S(2)}) collective-permute-start(bf16[256,1024]{1,0:T(8,128)(2,1)S(1)} %add_convert_fusion.3), channel_id=1, source_target_pairs={{0,2},{1,3},{2,0},{3,1},{4,6},{5,7},{6,4},{7,5},{8,10},{9,11},{10,... | collective-permute-start | bytes 1572872 | tf_op jit(solution)/shard_map/ppermute | solution.py:800
  325.6 15.0 %collective-permute-start.39 = (f32[96,128]{1,0:T(8,128)S(1)}, f32[96,128]{1,0:T(8,128)S(1)}, u32[]{:S(2)}, u32[]{:S(2)}) collective-permute-start(f32[96,128]{1,0:T(8,128)S(1)} %bitcast.99), channel_id=1, source_target_pairs={{0,1},{1,0},{2,3},{3,2},{4,5},{5,4},{6,7},{7,6},{8,9},{9,8},{10,11... | collective-permute-start | bytes 147464 | tf_op jit(solution)/shard_map/ppermute | solution.py:800
  338.5 23.3 %collective-permute-start.48 = (bf16[256,1024]{1,0:T(8,128)(2,1)S(1)}, bf16[256,1024]{1,0:T(8,128)(2,1)S(1)}, u32[]{:S(2)}, u32[]{:S(2)}) collective-permute-start(bf16[256,1024]{1,0:T(8,128)(2,1)S(1)} %broadcast_select_fusion.6), channel_id=1, source_target_pairs={{0,8},{8,0},{16,24},{24,16},{1,9},{9,1},{17,25},{25,17},{2,10},{10... | collective-permute-start | bytes 1572872 | tf_op jit(solution)/shard_map/ppermute | solution.py:800
  346.7 15.0 %collective-permute-start.49 = (bf16[128,1024]{1,0:T(8,128)(2,1)S(1)}, bf16[128,1024]{1,0:T(8,128)(2,1)S(1)}, u32[]{:S(2)}, u32[]{:S(2)}) collective-permute-start(bf16[128,1024]{1,0:T(8,128)(2,1)S(1)} %add_convert_fusion.10), channel_id=1, source_target_pairs={{0,16},{8,24},{16,0},{24,8},{1,17},{9,25},{17,1},{25,9},{2,18},{10... | collective-permute-start | bytes 786440 | tf_op jit(solution)/shard_map/ppermute | solution.py:800
  348.9 8.9 %collective-permute-start.42 = (f32[96,128]{1,0:T(8,128)S(1)}, f32[96,128]{1,0:T(8,128)S(1)}, u32[]{:S(2)}, u32[]{:S(2)}) collective-permute-start(f32[96,128]{1,0:T(8,128)S(1)} %add.188), channel_id=1, source_target_pairs={{0,8},{8,0},{16,24},{24,16},{1,9},{9,1},{17,25},{25,17},{2,10},{10... | collective-permute-start | bytes 147464 | tf_op jit(solution)/shard_map/ppermute | solution.py:800
  357.8 11.3 %collective-permute-start.43 = (f32[96,128]{1,0:T(8,128)S(1)}, f32[96,128]{1,0:T(8,128)S(1)}, u32[]{:S(2)}, u32[]{:S(2)}) collective-permute-start(f32[96,128]{1,0:T(8,128)S(1)} %add.189), channel_id=1, source_target_pairs={{0,16},{8,24},{16,0},{24,8},{1,17},{9,25},{17,1},{25,9},{2,18},{10... | collective-permute-start | bytes 147464 | tf_op jit(solution)/shard_map/ppermute | solution.py:800
  362.0 12.1 %collective-permute-start.50 = (bf16[128,1024]{1,0:T(8,128)(2,1)S(1)}, bf16[128,1024]{1,0:T(8,128)(2,1)S(1)}, u32[]{:S(2)}, u32[]{:S(2)}) collective-permute-start(bf16[128,1024]{1,0:T(8,128)(2,1)S(1)} %get-tuple-element.273), channel_id=1, source_target_pairs={{0,16},{8,24},{16,0},{24,8},{1,17},{9,25},{17,1},{25,9},{2,18},{10... | collective-permute-start | bytes 786440 | tf_op jit(solution)/shard_map/ppermute | solution.py:800
  369.2 20.1 %collective-permute-start.53 = (bf16[256,1024]{1,0:T(8,128)(2,1)S(1)}, bf16[256,1024]{1,0:T(8,128)(2,1)S(1)}, u32[]{:S(2)}, u32[]{:S(2)}) collective-permute-start(bf16[256,1024]{1,0:T(8,128)(2,1)S(1)} %maximum_select_fusion.1), channel_id=1, source_target_pairs={{0,8},{8,0},{16,24},{24,16},{1,9},{9,1},{17,25},{25,17},{2,10},{10... | collective-permute-start | bytes 1572872 | tf_op jit(solution)/shard_map/ppermute | solution.py:800
  374.2 13.9 %collective-permute-start.51 = (bf16[128,1024]{1,0:T(8,128)(2,1)S(1)}, bf16[128,1024]{1,0:T(8,128)(2,1)S(1)}, u32[]{:S(2)}, u32[]{:S(2)}) collective-permute-start(bf16[128,1024]{1,0:T(8,128)(2,1)S(1)} %add_convert_fusion.9), channel_id=1, source_target_pairs={{0,16},{8,24},{16,0},{24,8},{1,17},{9,25},{17,1},{25,9},{2,18},{10... | collective-permute-start | bytes 786440 | tf_op jit(solution)/shard_map/ppermute | solution.py:800
  388.3 13.1 %collective-permute-start.52 = (bf16[256,1024]{1,0:T(8,128)(2,1)S(1)}, bf16[256,1024]{1,0:T(8,128)(2,1)S(1)}, u32[]{:S(2)}, u32[]{:S(2)}) collective-permute-start(bf16[256,1024]{1,0:T(8,128)(2,1)S(1)} %maximum_select_fusion.2), channel_id=1, source_target_pairs={{0,8},{8,0},{16,24},{24,16},{1,9},{9,1},{17,25},{25,17},{2,10},{10... | collective-permute-start | bytes 1572872 | tf_op jit(solution)/shard_map/ppermute | solution.py:800
  (56 other events, 441.6 us)
Sparse Core Ops, SparseCore 0:
  41.7 81.8 all-gather.2
  147.7 72.7 reduce-scatter.1
